TPU v7x, 32 devices: a whole 2x2x4 slice. The times are simulated.
32 devices in a mesh: seq: 4 (over y, x), row: 8 (over z, core).
Axes of the slice: x: 2, y: 2, z: 4, core: 2. Of those that a mesh axis runs over, the one named last changes fastest.
Arguments:
- tokens: bfloat16 [8, 1024, 2048], P('row', 'seq'), may hold values from -6 to 6
- segment_ids: int32 [8, 1024], P('row', 'seq'), may hold values from 0 to 2, as said below
- w_query: bfloat16 [2048, 2048], P(('seq', 'row')), may hold values from -0.125 to 0.125
- w_key: bfloat16 [2048, 2048], P(('seq', 'row')), may hold values from -0.125 to 0.125
- w_value: bfloat16 [2048, 2048], P(('seq', 'row')), may hold values from -0.125 to 0.125
- w_out: bfloat16 [2048, 2048], P(('seq', 'row')), may hold values from -0.125 to 0.125
- w_gate: bfloat16 [2048, 8192], P(('seq', 'row')), may hold values from -0.125 to 0.125
- w_up: bfloat16 [2048, 8192], P(('seq', 'row')), may hold values from -0.125 to 0.125
- w_down: bfloat16 [8192, 2048], P(('seq', 'row')), may hold values from -0.0625 to 0.0625
- query_gain: bfloat16 [2048], P(('seq', 'row')), may hold values from 0.099609375 to 1.8984375
- key_gain: bfloat16 [2048], P(('seq', 'row')), may hold values from 0.099609375 to 1.8984375
- attn_gain: bfloat16 [2048], P(('seq', 'row')), may hold values from 0.099609375 to 1.8984375
- ff_gain: bfloat16 [2048], P(('seq', 'row')), may hold values from 0.099609375 to 1.8984375
- cotangent: bfloat16 [8, 1024, 2048], P('row', 'seq'), may hold values from -6 to 6
Outputs:
- mixed: bfloat16 [8, 1024, 2048], P('row', 'seq')
- input_grad: float32 [8, 1024, 2048], P('row', 'seq')
- grad_query: float32 [2048, 2048], P(('seq', 'row'))
- grad_key: float32 [2048, 2048], P(('seq', 'row'))
- grad_value: float32 [2048, 2048], P(('seq', 'row'))
- grad_out: float32 [2048, 2048], P(('seq', 'row'))
- grad_gate: float32 [2048, 8192], P(('seq', 'row'))
- grad_up: float32 [2048, 8192], P(('seq', 'row'))
- grad_down: float32 [8192, 2048], P(('seq', 'row'))
- grad_query_gain: float32 [2048], P(('seq', 'row'))
- grad_key_gain: float32 [2048], P(('seq', 'row'))
- grad_attn_gain: float32 [2048], P(('seq', 'row'))
- grad_ff_gain: float32 [2048], P(('seq', 'row'))
Inputs may be any that keep to these rules, and one draw needn't show every extreme that they name: Along each sequence segment_ids never fall; segment 0 holds the first 1 to 128 tokens, segment 2 the last 1 to 128 tokens, and segment 1 all between.
All inputs are finite; a program needn't handle non-finite values.
Results may differ from a plain program's by a relative error of at most 0.03.
Values may be sent and summed in bfloat16 or wider, within the bound.
No kernel may reach another device: no remote copies, remote signals or barrier semaphores. Data moves between devices by JAX's collectives and lax.ppermute only.
A program may use at most 512 MiB of HBM per device.

v0:
```python
import jax
import jax.numpy as jnp
from jax import lax
from jax.sharding import PartitionSpec as P

HEADS = 16


rope_base = 500000.0
norm_eps = 1e-06
masked_score = -1e30


def shifted(x, axis, by):
    count = lax.axis_size(axis)
    pairs = [(i, i + by) for i in range(count) if 0 <= i + by < count]
    return lax.ppermute(x, axis, pairs)


def shifted_2(block, axis, distance):
    devices = range(lax.axis_size(axis))
    route = [((i - distance) % len(devices), i) for i in devices]
    return lax.ppermute(block, axis, route)


def rope_tables(positions, head_dim):
    half_dim = head_dim // 2
    frequency = rope_base ** (-(jnp.arange(half_dim, dtype=jnp.float32) * 2.0 / head_dim))
    angles = positions.astype(jnp.float32)[:, None] * frequency[None, :]
    return (jnp.cos(angles)[:, None, :], jnp.sin(angles)[:, None, :])


def rms_scale(values, gain_vec):
    return (
        values * lax.rsqrt(jnp.mean(values * values, axis=-1, keepdims=True) + norm_eps) * gain_vec
    )


def normed_rope(raw_proj, gain_vec, cosine_table, sine_table, head_count):
    normed = rms_scale(raw_proj, gain_vec)
    split_heads = normed.reshape(raw_proj.shape[0], head_count, -1)
    half_dim = split_heads.shape[-1] // 2
    first_half = split_heads[..., :half_dim]
    second = split_heads[..., half_dim:]
    return jnp.concatenate(
        [
            first_half * cosine_table - second * sine_table,
            second * cosine_table + first_half * sine_table,
        ],
        axis=-1,
    )


def rotate(key_blk, value_blk):
    return shifted((key_blk, value_blk), "seq", 1)


def block_mask(own_ids, row_ids, positions, owner_idx, tok_rows):
    key_ids = lax.dynamic_slice_in_dim(row_ids, owner_idx * tok_rows, tok_rows)
    key_pos = owner_idx * tok_rows + jnp.arange(tok_rows, dtype=jnp.int32)
    return (own_ids[:, None] == key_ids[None, :]) & (positions[:, None] >= key_pos[None, :])


def attend_block(running, query_low, key_blk, value_blk, allowed, score_scale):
    running_max, running_sum, running_out = running
    scores = (
        jnp.einsum("qhd,khd->hqk", query_low, key_blk, preferred_element_type=jnp.float32)
        * score_scale
    )
    scores = jnp.where(allowed[None], scores, masked_score)
    newest_max = jnp.maximum(running_max, jnp.max(scores, axis=-1))
    rescale = jnp.exp(running_max - newest_max)
    probability = jnp.exp(scores - newest_max[..., None])
    running_sum = running_sum * rescale + jnp.sum(probability, axis=-1)
    running_out = running_out * rescale[..., None] + jnp.einsum(
        "hqk,khd->hqd",
        probability.astype(jnp.bfloat16),
        value_blk,
        preferred_element_type=jnp.float32,
    )
    return (newest_max, running_sum, running_out)


def attend_back(
    running, query_low, grad_att_low, row_dot, log_total, key_blk, value_blk, allowed, score_scale
):
    grad_query, grad_keys, grad_values = running
    scores = (
        jnp.einsum("qhd,khd->hqk", query_low, key_blk, preferred_element_type=jnp.float32)
        * score_scale
    )
    scores = jnp.where(allowed[None], scores, masked_score)
    probability = jnp.exp(scores - log_total[..., None])
    grad_prob = jnp.einsum(
        "qhd,khd->hqk", grad_att_low, value_blk, preferred_element_type=jnp.float32
    )
    grad_score = (probability * (grad_prob - row_dot[..., None])).astype(jnp.bfloat16)
    grad_query = (
        grad_query
        + jnp.einsum("hqk,khd->qhd", grad_score, key_blk, preferred_element_type=jnp.float32)
        * score_scale
    )
    grad_keys = (
        grad_keys
        + jnp.einsum("hqk,qhd->khd", grad_score, query_low, preferred_element_type=jnp.float32)
        * score_scale
    )
    grad_values = grad_values + jnp.einsum(
        "hqk,qhd->khd",
        probability.astype(jnp.bfloat16),
        grad_att_low,
        preferred_element_type=jnp.float32,
    )
    return (grad_query, grad_keys, grad_values)


def spread_grad(left_side, right_side):
    return lax.psum_scatter(
        jnp.einsum("tc,tf->cf", left_side, right_side, preferred_element_type=jnp.float32),
        ("seq", "row"),
        scatter_dimension=0,
        tiled=True,
    )


def transposed(left_side, weight_all):
    return jnp.einsum("tf,cf->tc", left_side, weight_all, preferred_element_type=jnp.float32)


def per_device(
    tokens,
    segment_ids,
    w_query,
    w_key,
    w_value,
    w_out,
    w_gate,
    w_up,
    w_down,
    query_gain,
    key_gain,
    attn_gain,
    ff_gain,
    cotangent,
):
    head_count = HEADS
    inputs = tokens[0]
    tok_rows = inputs.shape[0]
    model_width = inputs.shape[1]
    head_dim = model_width // head_count
    score_scale = head_dim ** (-0.5)
    cycle_size = lax.axis_size("seq")
    seq_rank = lax.axis_index("seq")
    row_ids = lax.all_gather(segment_ids, "seq", axis=1, tiled=True)[0]
    own_ids = segment_ids[0]
    positions = seq_rank * tok_rows + jnp.arange(tok_rows, dtype=jnp.int32)
    cosine_table, sine_table = rope_tables(positions, head_dim)
    attn_set = (
        lax.all_gather(w_query, ("seq", "row"), axis=0, tiled=True),
        lax.all_gather(w_key, ("seq", "row"), axis=0, tiled=True),
        lax.all_gather(w_value, ("seq", "row"), axis=0, tiled=True),
        lax.all_gather(w_out, ("seq", "row"), axis=0, tiled=True),
        lax.all_gather(query_gain, ("seq", "row"), axis=0, tiled=True),
        lax.all_gather(key_gain, ("seq", "row"), axis=0, tiled=True),
        lax.all_gather(attn_gain, ("seq", "row"), axis=0, tiled=True),
        lax.all_gather(ff_gain, ("seq", "row"), axis=0, tiled=True),
    )
    query_all, key_weight, value_weight, out_weight = (
        attn_set[0],
        attn_set[1],
        attn_set[2],
        attn_set[3],
    )
    gain_query = attn_set[4].astype(jnp.float32)
    gain_key = attn_set[5].astype(jnp.float32)
    gain_attn = attn_set[6].astype(jnp.float32)
    gain_ff = attn_set[7].astype(jnp.float32)
    query_raw = jnp.dot(inputs, query_all, preferred_element_type=jnp.float32)
    key_raw = jnp.dot(inputs, key_weight, preferred_element_type=jnp.float32)
    value_raw = jnp.dot(inputs, value_weight, preferred_element_type=jnp.float32)
    query_rot, query_pull = jax.vjp(
        lambda raw_proj, gain_vec: normed_rope(
            raw_proj, gain_vec, cosine_table, sine_table, head_count
        ),
        query_raw,
        gain_query,
    )
    key_rot, key_pull = jax.vjp(
        lambda raw_proj, gain_vec: normed_rope(
            raw_proj, gain_vec, cosine_table, sine_table, head_count
        ),
        key_raw,
        gain_key,
    )
    query_low = query_rot.astype(jnp.bfloat16)
    key_low = key_rot.astype(jnp.bfloat16)
    value_low = value_raw.astype(jnp.bfloat16).reshape(tok_rows, head_count, head_dim)

    def forward_step(cycle_step, loop_carry):
        key_blk, value_blk, running = loop_carry
        owner_idx = (seq_rank - cycle_step) % cycle_size
        allowed = block_mask(own_ids, row_ids, positions, owner_idx, tok_rows)
        running = lax.cond(
            owner_idx <= seq_rank,
            lambda kept_state: attend_block(
                kept_state, query_low, key_blk, value_blk, allowed, score_scale
            ),
            lambda kept_state: kept_state,
            running,
        )
        return (key_blk, value_blk, running)

    def forward_move(cycle_step, loop_carry):
        key_blk, value_blk, running = forward_step(cycle_step, loop_carry)
        key_blk, value_blk = rotate(key_blk, value_blk)
        return (key_blk, value_blk, running)

    initial = (
        jnp.full((head_count, tok_rows), masked_score, jnp.float32),
        jnp.zeros((head_count, tok_rows), jnp.float32),
        jnp.zeros((head_count, tok_rows, head_dim), jnp.float32),
    )
    loop_carry = lax.fori_loop(0, cycle_size - 1, forward_move, (key_low, value_low, initial))
    running_max, running_sum, running_out = forward_step(cycle_size - 1, loop_carry)[2]
    log_total = running_max + jnp.log(running_sum)
    attended = jnp.transpose(running_out / running_sum[..., None], (1, 0, 2))
    attn_low = attended.reshape(tok_rows, model_width).astype(jnp.bfloat16)
    branch = jnp.dot(attn_low, out_weight, preferred_element_type=jnp.float32)
    attn_normed, attn_pull = jax.vjp(rms_scale, branch, gain_attn)
    hidden = inputs.astype(jnp.float32) + attn_normed
    hidden_low = hidden.astype(jnp.bfloat16)
    ff_set = (
        lax.all_gather(w_gate, ("seq", "row"), axis=0, tiled=True),
        lax.all_gather(w_up, ("seq", "row"), axis=0, tiled=True),
        lax.all_gather(w_down, ("seq", "row"), axis=0, tiled=True),
    )
    gate_act = jnp.dot(hidden_low, ff_set[0], preferred_element_type=jnp.float32)
    up_act = jnp.dot(hidden_low, ff_set[1], preferred_element_type=jnp.float32)
    middle_act, middle_pull = jax.vjp(
        lambda gate_in, up_in: jax.nn.silu(gate_in) * up_in, gate_act, up_act
    )
    middle = middle_act.astype(jnp.bfloat16)
    ff_raw = jnp.dot(middle, ff_set[2], preferred_element_type=jnp.float32)
    ff_normed, ff_pull = jax.vjp(rms_scale, ff_raw, gain_ff)
    mixed = (hidden + ff_normed).astype(jnp.bfloat16)
    grad_output = cotangent[0].astype(jnp.float32)
    grad_ff_raw, grad_ff_gain = ff_pull(grad_output)
    grad_ff_low = grad_ff_raw.astype(jnp.bfloat16)
    ff_back = (
        lax.all_gather(w_gate, ("seq", "row"), axis=0, tiled=True),
        lax.all_gather(w_up, ("seq", "row"), axis=0, tiled=True),
        lax.all_gather(w_down, ("seq", "row"), axis=0, tiled=True),
    )
    grad_down = spread_grad(middle, grad_ff_low)
    grad_middle = transposed(grad_ff_low, ff_back[2])
    grad_gate_act, grad_up_act = middle_pull(grad_middle)
    grad_gate_low = grad_gate_act.astype(jnp.bfloat16)
    grad_up_low = grad_up_act.astype(jnp.bfloat16)
    grad_gate = spread_grad(hidden_low, grad_gate_low)
    grad_up = spread_grad(hidden_low, grad_up_low)
    grad_hidden = (
        grad_output + transposed(grad_gate_low, ff_back[0]) + transposed(grad_up_low, ff_back[1])
    )
    grad_branch, grad_attn_gain = attn_pull(grad_hidden)
    grad_branch_low = grad_branch.astype(jnp.bfloat16)
    attn_back = (
        lax.all_gather(w_query, ("seq", "row"), axis=0, tiled=True),
        lax.all_gather(w_key, ("seq", "row"), axis=0, tiled=True),
        lax.all_gather(w_value, ("seq", "row"), axis=0, tiled=True),
        lax.all_gather(w_out, ("seq", "row"), axis=0, tiled=True),
    )
    grad_att_low = (
        transposed(grad_branch_low, attn_back[3])
        .astype(jnp.bfloat16)
        .reshape(tok_rows, head_count, head_dim)
    )
    row_dot = jnp.transpose(jnp.sum(grad_att_low.astype(jnp.float32) * attended, axis=-1))

    def backward_step(cycle_step, loop_carry):
        key_blk, value_blk, grad_keys, grad_values, grad_query = loop_carry
        owner_idx = (seq_rank - cycle_step) % cycle_size
        allowed = block_mask(own_ids, row_ids, positions, owner_idx, tok_rows)
        grad_query, grad_keys, grad_values = lax.cond(
            owner_idx <= seq_rank,
            lambda kept_state: attend_back(
                kept_state,
                query_low,
                grad_att_low,
                row_dot,
                log_total,
                key_blk,
                value_blk,
                allowed,
                score_scale,
            ),
            lambda kept_state: kept_state,
            (grad_query, grad_keys, grad_values),
        )
        key_blk, value_blk = rotate(key_blk, value_blk)
        grad_keys, grad_values = (
            shifted_2(grad_keys.astype(jnp.bfloat16), "seq", 1).astype(grad_keys.dtype),
            shifted_2(grad_values.astype(jnp.bfloat16), "seq", 1).astype(grad_values.dtype),
        )
        return (key_blk, value_blk, grad_keys, grad_values, grad_query)

    zero_heads = jnp.zeros((tok_rows, head_count, head_dim), jnp.float32)
    back_carry = lax.fori_loop(
        0, cycle_size, backward_step, (key_low, value_low, zero_heads, zero_heads, zero_heads)
    )
    grad_keys, grad_values, grad_query = (back_carry[2], back_carry[3], back_carry[4])
    grad_query_raw, grad_query_gain = query_pull(grad_query)
    grad_key_raw, grad_key_gain = key_pull(grad_keys)
    grad_query_low = grad_query_raw.astype(jnp.bfloat16)
    grad_key_low = grad_key_raw.astype(jnp.bfloat16)
    grad_value_low = grad_values.reshape(tok_rows, model_width).astype(jnp.bfloat16)
    query_term = jnp.einsum("tc,tf->cf", inputs, grad_query_low, preferred_element_type=jnp.float32)
    key_term = jnp.einsum("tc,tf->cf", inputs, grad_key_low, preferred_element_type=jnp.float32)
    value_term = jnp.einsum("tc,tf->cf", inputs, grad_value_low, preferred_element_type=jnp.float32)
    out_term = jnp.einsum(
        "tc,tf->cf", attn_low, grad_branch_low, preferred_element_type=jnp.float32
    )
    summed = (
        lax.psum_scatter(query_term, ("seq", "row"), scatter_dimension=0, tiled=True),
        lax.psum_scatter(key_term, ("seq", "row"), scatter_dimension=0, tiled=True),
        lax.psum_scatter(value_term, ("seq", "row"), scatter_dimension=0, tiled=True),
        lax.psum_scatter(out_term, ("seq", "row"), scatter_dimension=0, tiled=True),
        lax.psum_scatter(grad_query_gain, ("seq", "row"), scatter_dimension=0, tiled=True),
        lax.psum_scatter(grad_key_gain, ("seq", "row"), scatter_dimension=0, tiled=True),
        lax.psum_scatter(grad_attn_gain, ("seq", "row"), scatter_dimension=0, tiled=True),
        lax.psum_scatter(grad_ff_gain, ("seq", "row"), scatter_dimension=0, tiled=True),
    )
    input_grad = (
        grad_hidden
        + transposed(grad_query_low, attn_back[0])
        + transposed(grad_key_low, attn_back[1])
        + transposed(grad_value_low, attn_back[2])
    )
    return (
        mixed[None],
        input_grad[None],
        summed[0],
        summed[1],
        summed[2],
        summed[3],
        grad_gate,
        grad_up,
        grad_down,
        summed[4],
        summed[5],
        summed[6],
        summed[7],
    )


def solution(mesh):
    return jax.shard_map(
        per_device,
        mesh=mesh,
        in_specs=(
            P("row", "seq", None),
            P("row", "seq"),
            P(("seq", "row"), None),
            P(("seq", "row"), None),
            P(("seq", "row"), None),
            P(("seq", "row"), None),
            P(("seq", "row"), None),
            P(("seq", "row"), None),
            P(("seq", "row"), None),
            P(("seq", "row")),
            P(("seq", "row")),
            P(("seq", "row")),
            P(("seq", "row")),
            P("row", "seq", None),
        ),
        out_specs=(
            P("row", "seq", None),
            P("row", "seq", None),
            P(("seq", "row"), None),
            P(("seq", "row"), None),
            P(("seq", "row"), None),
            P(("seq", "row"), None),
            P(("seq", "row"), None),
            P(("seq", "row"), None),
            P(("seq", "row"), None),
            P(("seq", "row")),
            P(("seq", "row")),
            P(("seq", "row")),
            P(("seq", "row")),
        ),
        check_vma=False,
    )
```

profile of v0, /device:TPU:0, one launch (start us, length us, event | category | flops | bytes accessed | tf_op | source)
XLA Modules:
  0.0 4445.3 jit_solution(256098137372016780)
XLA Ops:
  13.1 42.7 all-reduce.13
  66.0 25.5 all-gather.8.cloned.1.call-done
  100.3 70.2 %all-gather.12.cloned.1.call-done = bf16[2048,2048]{1,0:T(8,128)(2,1)} async-done(((bf16[64,2048]{1,0:T(8,128)(2,1)}), bf16[2048,2048]{1,0:T(8,128)(2,1)}) %all-gather.12.cloned.1.call-update) | async-done | bytes 8388624 | tf_op jit(solution)/shard_map/all_gather | solution.py:159
  187.9 61.6 %all-gather.10.cloned.1.call-done = bf16[2048,2048]{1,0:T(8,128)(2,1)} async-done(((bf16[64,2048]{1,0:T(8,128)(2,1)}), bf16[2048,2048]{1,0:T(8,128)(2,1)}) %all-gather.10.cloned.1.call-update) | async-done | bytes 8388624 | tf_op jit(solution)/shard_map/all_gather | solution.py:161
  259.2 208.0 %while.48 = (s32[]{:T(128)}, bf16[256,16,128]{2,0,1:T(8,128)(2,1)}, bf16[256,16,128]{2,0,1:T(8,128)(2,1)}, f32[16,256]{1,0:T(8,128)S(1)}, f32[16,256]{1,0:T(8,12...) while((s32[]{:T(128)}, bf16[256,16,128]{2,0,1:T(8,128)(2,1)}, ...), condition=%wide.region_7.8_spmd.clone, body=%wide.region_2.7_spmd.clone.sunk | while | flops 549659136 | bytes 33042996 | solution.py:223
  278.4 17.8 collective-permute-done
  296.2 34.3 collective-permute-done.1
  344.5 18.7 collective-permute-done
  363.2 24.9 collective-permute-done.1
  403.0 38.0 collective-permute-done
  441.0 26.2 collective-permute-done.1
  479.3 98.4 %all-gather.16.cloned.1.call-done = bf16[2048,8192]{1,0:T(8,128)(2,1)} async-done(((bf16[64,8192]{1,0:T(8,128)(2,1)}), bf16[2048,8192]{1,0:T(8,128)(2,1)}) %all-gather.16.cloned.1.call-update) | async-done | bytes 33554448 | tf_op jit(solution)/shard_map/all_gather | solution.py:233
  577.7 17.8 fusion.78
  595.5 178.0 %all-gather.18.cloned.1.call-done = bf16[2048,8192]{1,0:T(8,128)(2,1)} async-done(((bf16[64,8192]{1,0:T(8,128)(2,1)}), bf16[2048,8192]{1,0:T(8,128)(2,1)}) %all-gather.18.cloned.1.call-update) | async-done | bytes 33554448 | tf_op jit(solution)/shard_map/all_gather | solution.py:234
  773.5 23.8 multiply_convert_fusion.2
  797.4 172.1 %all-gather.20.cloned.1.call-done = bf16[8192,2048]{1,0:T(8,128)(2,1)} async-done(((bf16[256,2048]{1,0:T(8,128)(2,1)}), bf16[8192,2048]{1,0:T(8,128)(2,1)}) %all-gather.20.cloned.1.call-update) | async-done | bytes 33554448 | tf_op jit(solution)/shard_map/all_gather | solution.py:235
  969.5 16.6 multiply_reduce_fusion.4
  988.9 23.3 multiply_convert_fusion.1
  1012.2 17.1 convert_add_fusion
  1029.3 17.6 multiply_reduce_fusion
  1063.1 446.4 %while.49 = (s32[]{:T(128)}, bf16[256,16,128]{2,0,1:T(8,128)(2,1)}, bf16[256,16,128]{2,0,1:T(8,128)(2,1)}, f32[256,16,128]{2,0,1:T(8,128)}, f32[256,16,128]{2,0,...) while((s32[]{:T(128)}, bf16[256,16,128]{2,0,1:T(8,128)(2,1)}, ...), condition=%wide.region_20.21_spmd.clone, body=%wide.region_17.20_spmd.clone.sunk | while | flops 1358627328 | bytes 114553744 | solution.py:307
  1114.4 20.4 collective-permute-done.5
  1137.5 18.3 collective-permute-done.2
  1155.8 21.9 collective-permute-done.3
  1186.2 18.7 collective-permute-start.4
  1230.5 20.5 collective-permute-done.5
  1253.8 19.6 collective-permute-done.2
  1273.4 21.0 collective-permute-done.3
  1308.1 19.4 collective-permute-start.5
  1347.8 19.1 collective-permute-done.5
  1373.8 20.1 collective-permute-done.3
  1402.4 19.5 collective-permute-start.4
  1428.0 18.4 collective-permute-start.2
  1464.4 18.1 collective-permute-done.5
  1490.4 19.1 collective-permute-done.3
  1528.1 17.6 copy.88
  1561.3 17.7 copy.86
  1601.1 17.7 copy.90
  1620.7 26.3 fusion.74
  1648.2 26.2 fusion.80
  1674.5 26.2 fusion.81
  1701.4 58.2 %all-reduce.12 = (f32[2048]{0:T(1024)S(1)}, f32[2048]{0:T(1024)S(1)}, f32[2048]{0:T(1024)S(1)}, f32[2048]{0:T(1024)S(1)}) all-reduce(f32[2048]{0:T(1024)S(1)} %copy-done.56, f32[2048]{0:T(1024)S(1)} %copy-done.55, f32[2048]{0:T(1024)S(1)} %copy-done.63, f32[2048]{0:T(1024)S(1)} %copy-done.54), channel_id=9, replica_groups=mesh['seq'=4,'row'=8] {'seq','row'}, use_global_device_ids=true, to_apply=%region_31.32.clone | all-reduce | flops 8192 | bytes 65536
  1777.7 158.8 %reduce-scatter.22.cloned.1.call-done = f32[64,2048]{1,0:T(8,128)} async-done(((f32[2048,2048]{1,0:T(8,128)}), f32[64,2048]{1,0:T(8,128)}) %reduce-scatter.22.cloned.1.call-update) | async-done | bytes 524304
  1936.6 187.1 %reduce-scatter.14.cloned.1.call-done = f32[64,2048]{1,0:T(8,128)} async-done(((f32[2048,2048]{1,0:T(8,128)}), f32[64,2048]{1,0:T(8,128)}) %reduce-scatter.14.cloned.1.call-update) | async-done | bytes 524304 | tf_op jit(solution)/shard_map/reduce_scatter | solution.py:326
  2123.7 187.3 %reduce-scatter.26.cloned.1.call-done = f32[64,2048]{1,0:T(8,128)} async-done(((f32[2048,2048]{1,0:T(8,128)}), f32[64,2048]{1,0:T(8,128)}) %reduce-scatter.26.cloned.1.call-update) | async-done | bytes 524304
  2311.0 709.9 %reduce-scatter.20.cloned.1.call-done = f32[256,2048]{1,0:T(8,128)} async-done(((f32[8192,2048]{1,0:T(8,128)}), f32[256,2048]{1,0:T(8,128)}) %reduce-scatter.20.cloned.1.call-update) | async-done | bytes 2097168 | tf_op jit(solution)/shard_map/reduce_scatter | solution.py:118
  3020.9 708.9 %reduce-scatter.16.cloned.1.call-done = f32[64,8192]{1,0:T(8,128)} async-done(((f32[2048,8192]{1,0:T(8,128)}), f32[64,8192]{1,0:T(8,128)}) %reduce-scatter.16.cloned.1.call-update) | async-done | bytes 2097168 | tf_op jit(solution)/shard_map/reduce_scatter | solution.py:118
  3729.8 708.7 %reduce-scatter.18.cloned.1.call-done = f32[64,8192]{1,0:T(8,128)} async-done(((f32[2048,8192]{1,0:T(8,128)}), f32[64,8192]{1,0:T(8,128)}) %reduce-scatter.18.cloned.1.call-update) | async-done | bytes 2097168 | tf_op jit(solution)/shard_map/reduce_scatter | solution.py:118
  (381 shorter events, 402.9 us)
Async XLA Ops:
  7.2 84.3 %all-gather.8.cloned.1.call-start = ((), (), s32[]{:S(2)}) async-start(), calls=%async_computation.7 | async-start | bytes 8650752 | tf_op jit(solution)/shard_map/all_gather | solution.py:160
  8.0 162.6 %all-gather.12.cloned.1.call-start = ((), (), s32[]{:S(2)}) async-start(), calls=%async_computation.9 | async-start | bytes 8650752 | tf_op jit(solution)/shard_map/all_gather | solution.py:159
  8.7 82.8 %copy-start.9 = (bf16[1,256,2048]{2,1,0:T(8,128)(2,1)S(1)}, bf16[1,256,2048]{2,1,0:T(8,128)(2,1)}, u32[]{:S(2)}) copy-start(bf16[1,256,2048]{2,1,0:T(8,128)(2,1)} %param.24) | copy-start | bytes 3145732
  8.7 240.7 %all-gather.10.cloned.1.call-start = ((), (), s32[]{:S(2)}) async-start(), calls=%async_computation.8 | async-start | bytes 8650752 | tf_op jit(solution)/shard_map/all_gather | solution.py:161
  9.5 461.8 %all-gather.14.cloned.1.call-start = ((), (), s32[]{:S(2)}) async-start(), calls=%async_computation.10 | async-start | bytes 8650752 | tf_op jit(solution)/shard_map/all_gather | solution.py:162
  10.0 567.6 %all-gather.16.cloned.1.call-start = ((), (), s32[]{:S(2)}) async-start(), calls=%async_computation.11 | async-start | bytes 34603008 | tf_op jit(solution)/shard_map/all_gather | solution.py:233
  10.6 762.9 %all-gather.18.cloned.1.call-start = ((), (), s32[]{:S(2)}) async-start(), calls=%async_computation.12 | async-start | bytes 34603008 | tf_op jit(solution)/shard_map/all_gather | solution.py:234
  11.2 958.3 %all-gather.20.cloned.1.call-start = ((), (), s32[]{:S(2)}) async-start(), calls=%async_computation.13 | async-start | bytes 34603008 | tf_op jit(solution)/shard_map/all_gather | solution.py:235
  12.0 1765.8 %reduce-scatter.24.cloned.1.call-start = ((), (), s32[]{:S(2)}) async-start(), calls=%async_computation.19 | async-start | bytes 17301504
  55.8 120.6 %copy-start.48 = (f32[2048]{0:T(1024)}, f32[2048]{0:T(1024)S(1)}, u32[]{:S(2)}) copy-start(f32[2048]{0:T(1024)S(1)} %convert_element_type.167) | copy-start | bytes 24580
  55.8 991.1 %copy-start.52 = (f32[2048]{0:T(1024)}, f32[2048]{0:T(1024)S(1)}, u32[]{:S(2)}) copy-start(f32[2048]{0:T(1024)S(1)} %convert_element_type.173) | copy-start | bytes 24580
  66.0 114.6 %copy-start.40 = (f32[256,64]{1,0:T(8,128)}, f32[256,64]{1,0:T(8,128)S(1)}, u32[]{:S(2)}) copy-start(f32[256,64]{1,0:T(8,128)S(1)} %get-tuple-element.1372) | copy-start | bytes 196612
  66.0 114.6 %copy-start.42 = (f32[256,64]{1,0:T(8,128)}, f32[256,64]{1,0:T(8,128)S(1)}, u32[]{:S(2)}) copy-start(f32[256,64]{1,0:T(8,128)S(1)} %get-tuple-element.1373) | copy-start | bytes 196612
  261.6 34.6 collective-permute-start
  268.2 62.2 %collective-permute-start.1 = (bf16[256,16,128]{2,0,1:T(8,128)(2,1)}, bf16[256,16,128]{2,0,1:T(8,128)(2,1)}, u32[]{:S(2)}, u32[]{:S(2)}) collective-permute-start(bf16[256,16,128]{2,0,1:T(8,128)(2,1)} %copy.144), channel_id=1, source_target_pairs={{0,8},{8,16},{16,24},{1,9},{9,17},{17,25},{2,10},{10,18},{18,26},{... | collective-permute-start | bytes 3145736 | tf_op jit(solution)/shard_map/while/body/eval_jaxpr/ppermute | solution.py:17
  332.7 30.5 collective-permute-start
  340.4 47.7 %collective-permute-start.1 = (bf16[256,16,128]{2,0,1:T(8,128)(2,1)}, bf16[256,16,128]{2,0,1:T(8,128)(2,1)}, u32[]{:S(2)}, u32[]{:S(2)}) collective-permute-start(bf16[256,16,128]{2,0,1:T(8,128)(2,1)} %copy.144), channel_id=1, source_target_pairs={{0,8},{8,16},{16,24},{1,9},{9,17},{17,25},{2,10},{10,18},{18,26},{... | collective-permute-start | bytes 3145736 | tf_op jit(solution)/shard_map/while/body/eval_jaxpr/ppermute | solution.py:17
  390.3 50.7 %collective-permute-start = (bf16[256,16,128]{2,0,1:T(8,128)(2,1)}, bf16[256,16,128]{2,0,1:T(8,128)(2,1)}, u32[]{:S(2)}, u32[]{:S(2)}) collective-permute-start(bf16[256,16,128]{2,0,1:T(8,128)(2,1)} %copy.143), channel_id=1, source_target_pairs={{0,8},{8,16},{16,24},{1,9},{9,17},{17,25},{2,10},{10,18},{18,26},{... | collective-permute-start | bytes 3145736 | tf_op jit(solution)/shard_map/while/body/eval_jaxpr/ppermute | solution.py:17
  398.0 69.2 %collective-permute-start.1 = (bf16[256,16,128]{2,0,1:T(8,128)(2,1)}, bf16[256,16,128]{2,0,1:T(8,128)(2,1)}, u32[]{:S(2)}, u32[]{:S(2)}) collective-permute-start(bf16[256,16,128]{2,0,1:T(8,128)(2,1)} %copy.144), channel_id=1, source_target_pairs={{0,8},{8,16},{16,24},{1,9},{9,17},{17,25},{2,10},{10,18},{18,26},{... | collective-permute-start | bytes 3145736 | tf_op jit(solution)/shard_map/while/body/eval_jaxpr/ppermute | solution.py:17
  479.3 294.2 %copy-start.27 = (bf16[256,2048]{1,0:T(8,128)(2,1)}, bf16[256,2048]{1,0:T(8,128)(2,1)S(1)}, u32[]{:S(2)}) copy-start(bf16[256,2048]{1,0:T(8,128)(2,1)S(1)} %fusion.58) | copy-start | bytes 3145732
  1063.1 446.4 %copy-start.41 = (f32[256,64]{1,0:T(8,128)S(1)}, f32[256,64]{1,0:T(8,128)}, u32[]{:S(2)}) copy-start(f32[256,64]{1,0:T(8,128)} %copy-done.40) | copy-start | bytes 196612
  1063.1 446.4 %copy-start.43 = (f32[256,64]{1,0:T(8,128)S(1)}, f32[256,64]{1,0:T(8,128)}, u32[]{:S(2)}) copy-start(f32[256,64]{1,0:T(8,128)} %copy-done.42) | copy-start | bytes 196612
  1085.9 26.9 collective-permute-start.4
  1090.2 44.6 %collective-permute-start.5 = (bf16[256,16,128]{2,0,1:T(8,128)(2,1)}, bf16[256,16,128]{2,0,1:T(8,128)(2,1)}, u32[]{:S(2)}, u32[]{:S(2)}) collective-permute-start(bf16[256,16,128]{2,0,1:T(8,128)(2,1)} %convert_element_type.245), channel_id=1, source_target_pairs={{24,0},{0,8},{8,16},{16,24},{25,1},{1,9},{9,17},{17,25},{26,2},{2,... | collective-permute-start | bytes 3145736 | tf_op jit(solution)/shard_map/while/body/eval_jaxpr/ppermute | solution.py:23
  1091.7 64.1 %collective-permute-start.2 = (bf16[256,16,128]{2,0,1:T(8,128)(2,1)S(1)}, bf16[256,16,128]{2,0,1:T(8,128)(2,1)}, u32[]{:S(2)}, u32[]{:S(2)}) collective-permute-start(bf16[256,16,128]{2,0,1:T(8,128)(2,1)S(1)} %copy-done.4), channel_id=1, source_target_pairs={{0,8},{8,16},{16,24},{1,9},{9,17},{17,25},{2,10},{10,18},{18,26},{... | collective-permute-start | bytes 3145736 | tf_op jit(solution)/shard_map/while/body/eval_jaxpr/ppermute | solution.py:17
  1095.1 82.6 %collective-permute-start.3 = (bf16[256,16,128]{2,0,1:T(8,128)(2,1)}, bf16[256,16,128]{2,0,1:T(8,128)(2,1)}, u32[]{:S(2)}, u32[]{:S(2)}) collective-permute-start(bf16[256,16,128]{2,0,1:T(8,128)(2,1)} %copy.168), channel_id=1, source_target_pairs={{0,8},{8,16},{16,24},{1,9},{9,17},{17,25},{2,10},{10,18},{18,26},{... | collective-permute-start | bytes 3145736 | tf_op jit(solution)/shard_map/while/body/eval_jaxpr/ppermute | solution.py:17
  1114.4 63.3 %copy-start.1 = (bf16[256,16,128]{2,0,1:T(8,128)(2,1)S(1)}, bf16[256,16,128]{2,0,1:T(8,128)(2,1)}, u32[]{:S(2)}) copy-start(bf16[256,16,128]{2,0,1:T(8,128)(2,1)} %copy-done) | copy-start | bytes 3145732 | tf_op jit(solution)/shard_map/while
  1186.2 42.7 collective-permute-start.4
  1207.6 43.4 collective-permute-start.5
  1210.0 63.4 %collective-permute-start.2 = (bf16[256,16,128]{2,0,1:T(8,128)(2,1)S(1)}, bf16[256,16,128]{2,0,1:T(8,128)(2,1)}, u32[]{:S(2)}, u32[]{:S(2)}) collective-permute-start(bf16[256,16,128]{2,0,1:T(8,128)(2,1)S(1)} %copy-done.4), channel_id=1, source_target_pairs={{0,8},{8,16},{16,24},{1,9},{9,17},{17,25},{2,10},{10,18},{18,26},{... | collective-permute-start | bytes 3145736 | tf_op jit(solution)/shard_map/while/body/eval_jaxpr/ppermute | solution.py:17
  1213.0 81.4 %collective-permute-start.3 = (bf16[256,16,128]{2,0,1:T(8,128)(2,1)}, bf16[256,16,128]{2,0,1:T(8,128)(2,1)}, u32[]{:S(2)}, u32[]{:S(2)}) collective-permute-start(bf16[256,16,128]{2,0,1:T(8,128)(2,1)} %copy.168), channel_id=1, source_target_pairs={{0,8},{8,16},{16,24},{1,9},{9,17},{17,25},{2,10},{10,18},{18,26},{... | collective-permute-start | bytes 3145736 | tf_op jit(solution)/shard_map/while/body/eval_jaxpr/ppermute | solution.py:17
  1230.5 63.9 %copy-start.1 = (bf16[256,16,128]{2,0,1:T(8,128)(2,1)S(1)}, bf16[256,16,128]{2,0,1:T(8,128)(2,1)}, u32[]{:S(2)}) copy-start(bf16[256,16,128]{2,0,1:T(8,128)(2,1)} %copy-done) | copy-start | bytes 3145732 | tf_op jit(solution)/shard_map/while
  1302.8 43.4 collective-permute-start.4
  1308.1 58.8 %collective-permute-start.5 = (bf16[256,16,128]{2,0,1:T(8,128)(2,1)}, bf16[256,16,128]{2,0,1:T(8,128)(2,1)}, u32[]{:S(2)}, u32[]{:S(2)}) collective-permute-start(bf16[256,16,128]{2,0,1:T(8,128)(2,1)} %convert_element_type.245), channel_id=1, source_target_pairs={{24,0},{0,8},{8,16},{16,24},{25,1},{1,9},{9,17},{17,25},{26,2},{2,... | collective-permute-start | bytes 3145736 | tf_op jit(solution)/shard_map/while/body/eval_jaxpr/ppermute | solution.py:23
  1327.6 46.3 %collective-permute-start.2 = (bf16[256,16,128]{2,0,1:T(8,128)(2,1)S(1)}, bf16[256,16,128]{2,0,1:T(8,128)(2,1)}, u32[]{:S(2)}, u32[]{:S(2)}) collective-permute-start(bf16[256,16,128]{2,0,1:T(8,128)(2,1)S(1)} %copy-done.4), channel_id=1, source_target_pairs={{0,8},{8,16},{16,24},{1,9},{9,17},{17,25},{2,10},{10,18},{18,26},{... | collective-permute-start | bytes 3145736 | tf_op jit(solution)/shard_map/while/body/eval_jaxpr/ppermute | solution.py:17
  1330.6 63.4 %collective-permute-start.3 = (bf16[256,16,128]{2,0,1:T(8,128)(2,1)}, bf16[256,16,128]{2,0,1:T(8,128)(2,1)}, u32[]{:S(2)}, u32[]{:S(2)}) collective-permute-start(bf16[256,16,128]{2,0,1:T(8,128)(2,1)} %copy.168), channel_id=1, source_target_pairs={{0,8},{8,16},{16,24},{1,9},{9,17},{17,25},{2,10},{10,18},{18,26},{... | collective-permute-start | bytes 3145736 | tf_op jit(solution)/shard_map/while/body/eval_jaxpr/ppermute | solution.py:17
  1402.4 60.4 %collective-permute-start.4 = (bf16[256,16,128]{2,0,1:T(8,128)(2,1)S(1)}, bf16[256,16,128]{2,0,1:T(8,128)(2,1)S(1)}, u32[]{:S(2)}, u32[]{:S(2)}) collective-permute-start(bf16[256,16,128]{2,0,1:T(8,128)(2,1)S(1)} %convert_element_type.243), channel_id=1, source_target_pairs={{24,0},{0,8},{8,16},{16,24},{25,1},{1,9},{9,17},{17,25},{26,2},{2,... | collective-permute-start | bytes 3145736 | tf_op jit(solution)/shard_map/while/body/eval_jaxpr/ppermute | solution.py:23
  1424.6 57.9 %collective-permute-start.5 = (bf16[256,16,128]{2,0,1:T(8,128)(2,1)}, bf16[256,16,128]{2,0,1:T(8,128)(2,1)}, u32[]{:S(2)}, u32[]{:S(2)}) collective-permute-start(bf16[256,16,128]{2,0,1:T(8,128)(2,1)} %convert_element_type.245), channel_id=1, source_target_pairs={{24,0},{0,8},{8,16},{16,24},{25,1},{1,9},{9,17},{17,25},{26,2},{2,... | collective-permute-start | bytes 3145736 | tf_op jit(solution)/shard_map/while/body/eval_jaxpr/ppermute | solution.py:23
  1428.0 62.4 %collective-permute-start.2 = (bf16[256,16,128]{2,0,1:T(8,128)(2,1)S(1)}, bf16[256,16,128]{2,0,1:T(8,128)(2,1)}, u32[]{:S(2)}, u32[]{:S(2)}) collective-permute-start(bf16[256,16,128]{2,0,1:T(8,128)(2,1)S(1)} %copy-done.4), channel_id=1, source_target_pairs={{0,8},{8,16},{16,24},{1,9},{9,17},{17,25},{2,10},{10,18},{18,26},{... | collective-permute-start | bytes 3145736 | tf_op jit(solution)/shard_map/while/body/eval_jaxpr/ppermute | solution.py:17
  1446.5 63.1 %collective-permute-start.3 = (bf16[256,16,128]{2,0,1:T(8,128)(2,1)}, bf16[256,16,128]{2,0,1:T(8,128)(2,1)}, u32[]{:S(2)}, u32[]{:S(2)}) collective-permute-start(bf16[256,16,128]{2,0,1:T(8,128)(2,1)} %copy.168), channel_id=1, source_target_pairs={{0,8},{8,16},{16,24},{1,9},{9,17},{17,25},{2,10},{10,18},{18,26},{... | collective-permute-start | bytes 3145736 | tf_op jit(solution)/shard_map/while/body/eval_jaxpr/ppermute | solution.py:17
  1545.7 390.9 %reduce-scatter.22.cloned.1.call-start = ((), (), s32[]{:S(2)}) async-start(), calls=%async_computation.18 | async-start | bytes 17301504
  1579.0 544.7 %reduce-scatter.14.cloned.1.call-start = ((), (), s32[]{:S(2)}) async-start(), calls=%async_computation.14 | async-start | bytes 17301504 | tf_op jit(solution)/shard_map/reduce_scatter | solution.py:326
  1588.7 722.3 %reduce-scatter.26.cloned.1.call-start = ((), (), s32[]{:S(2)}) async-start(), calls=%async_computation.20 | async-start | bytes 17301504
  1618.9 1402.0 %reduce-scatter.20.cloned.1.call-start = ((), (), s32[]{:S(2)}) async-start(), calls=%async_computation.17 | async-start | bytes 69206016 | tf_op jit(solution)/shard_map/reduce_scatter | solution.py:118
  1647.0 2082.8 %reduce-scatter.16.cloned.1.call-start = ((), (), s32[]{:S(2)}) async-start(), calls=%async_computation.15 | async-start | bytes 69206016 | tf_op jit(solution)/shard_map/reduce_scatter | solution.py:118
  1674.4 2764.1 %reduce-scatter.18.cloned.1.call-start = ((), (), s32[]{:S(2)}) async-start(), calls=%async_computation.16 | async-start | bytes 69206016 | tf_op jit(solution)/shard_map/reduce_scatter | solution.py:118
  1700.7 61.3 %copy-start.34 = (bf16[256,2048]{1,0:T(8,128)(2,1)S(1)}, bf16[256,2048]{1,0:T(8,128)(2,1)}, u32[]{:S(2)}) copy-start(bf16[256,2048]{1,0:T(8,128)(2,1)} %copy-done.33) | copy-start | bytes 3145732
  1700.7 61.3 %copy-start.39 = (f32[256,2048]{1,0:T(8,128)S(1)}, f32[256,2048]{1,0:T(8,128)}, u32[]{:S(2)}) copy-start(f32[256,2048]{1,0:T(8,128)} %copy-done.38) | copy-start | bytes 6291460
  (76 other events, 607.0 us)
Sparse Core Ops, SparseCore 0:
  11.0 80.4 all-gather.7
  94.5 76.0 all-gather.11
  173.5 75.8 all-gather.9
  252.3 95.4 all-gather.13
  350.6 227.0 all-gather.15
  580.5 192.9 all-gather.17
  776.5 192.9 all-gather.19
  1545.9 203.7 reduce-scatter.23
  1752.5 184.0 reduce-scatter.21
  1939.3 184.3 reduce-scatter.13
  2126.6 184.3 reduce-scatter.25
  2313.8 707.0 reduce-scatter.19
  3023.8 705.9 reduce-scatter.15
  3732.6 705.8 reduce-scatter.17
where the time goes:
time: 4450 us
  waiting for transfers between devices  3690 us (83%)
  matrix products  294 us (7%)
  starting transfers between devices  136 us (3%)
  local copies, waits for them, and re-layouts  124 us (3%)
  blocking collectives  111 us (2%)
  other arithmetic  70.8 us (2%)
    reduce_scatter x3, waiting for transfers between devices, spread_grad(): lax.psum_scatter(jnp.einsum('tc,tf->cf', left_side, right_side, preferred...  2130 us
    unnamed x17, waiting for transfers between devices  351 us
    ppermute x14, waiting for transfers between devices, shifted(): return lax.ppermute(x, axis, pairs)  289 us
    reduce_scatter x1, waiting for transfers between devices, per_device(): lax.psum_scatter(out_term, ('seq', 'row'), scatter_dimension=0, tiled=True)  187 us
    all_gather x1, waiting for transfers between devices, per_device(): lax.all_gather(w_up, ('seq', 'row'), axis=0, tiled=True)  178 us
    all_gather x1, waiting for transfers between devices, per_device(): lax.all_gather(w_down, ('seq', 'row'), axis=0, tiled=True)  172 us
    ppermute x8, waiting for transfers between devices, shifted_2(): return lax.ppermute(block, axis, route)  133 us
    unnamed x2, blocking collectives  101 us
  transfers between devices with their start and end apart: 36, of which 34 were waited for; matrix products, arithmetic and copies ran while one was open for 7% of the time, Pallas kernels for 0%

commit v1 on v0

v1 whole, which is shorter than its diff:
```python
import functools
import math

import jax
import jax.numpy as jnp
from jax import lax
from jax.experimental import pallas as pl
from jax.experimental.pallas import tpu as pltpu
from jax.sharding import Mesh
from jax.sharding import PartitionSpec as P

HEADS = 16

rope_base = 500000.0
norm_eps = 1e-06
masked_score = -1e30

bf16 = jnp.bfloat16
f32 = jnp.float32


def dims_of(axis):
    count = lax.axis_size(axis)
    return [(axis, 1 << bit) for bit in range(count.bit_length() - 1)]


def swap(block, dim):
    axis, mask = dim
    return lax.ppermute(block, axis, [(i, i ^ mask) for i in range(lax.axis_size(axis))])


def partner_index(dims, which):
    masks = {}
    for bit, (axis, mask) in enumerate(dims):
        if which >> bit & 1:
            masks[axis] = masks.get(axis, 0) | mask
    return masks


def column_cuts(width, count):
    tiles = width // 128
    return [round(tiles * i / count) * 128 for i in range(count + 1)]


def column_parts(block, count):
    cuts = column_cuts(block.shape[1], count)
    return [block[:, cuts[i] : cuts[i + 1]] for i in range(count)]


def route(which, count):
    bits = [i for i in range(count) if which >> i & 1]
    if len(bits) == 1:
        return bits[0]
    return bits[0] if bits[1] - bits[0] == 1 else bits[1]


def by_size(count):
    return sorted(range(1, 1 << count), key=lambda m: bin(m).count("1"))


def spread(block, dims):
    count = len(dims)
    full = (1 << count) - 1
    pieces = {0: block}
    for which in by_size(count):
        if which == full and count > 1:
            parts = [
                swap(column_parts(pieces[which ^ (1 << i)], count)[i], dims[i])
                for i in range(count)
            ]
            pieces[which] = jnp.concatenate(parts, axis=1)
        else:
            via = route(which, count)
            pieces[which] = swap(pieces[which ^ (1 << via)], dims[via])
    return [pieces[m] for m in range(1 << count)]


def collect(pieces, dims):
    count = len(dims)
    full = (1 << count) - 1
    pieces = list(pieces)
    got = {m: [] for m in range(1 << count)}
    for which in reversed(by_size(count)):
        total = pieces[which]
        if got[which]:
            total = total.astype(f32)
            for part, arrived in got[which]:
                if part is None:
                    total = total + arrived.astype(f32)
                else:
                    cuts = column_cuts(total.shape[1], count)
                    cols = column_parts(total, count)
                    cols[part] = cols[part] + arrived.astype(f32)
                    total = jnp.concatenate(cols, axis=1)
            total = total.astype(bf16)
        if which == full and count > 1:
            for i, cols in enumerate(column_parts(total, count)):
                got[which ^ (1 << i)].append((i, swap(cols, dims[i])))
        else:
            via = route(which, count)
            got[which ^ (1 << via)].append((None, swap(total, dims[via])))
    total = pieces[0].astype(f32)
    for _, arrived in got[0]:
        total = total + arrived.astype(f32)
    return total


def sum_all(table, dims):
    for bit, dim in enumerate(dims):
        there = swap(table, dim)
        order = [m ^ (1 << bit) for m in range(table.shape[0])]
        table = table + jnp.stack([there[m] for m in order])
    return table


def gather_blocks(block, dims, axes):
    pieces = {0: block}
    count = len(dims)
    for bit, dim in enumerate(dims):
        for m in range(1 << bit):
            pieces[m | (1 << bit)] = swap(pieces[m], dim)
    sizes = tuple(lax.axis_size(a) for a in axes)
    whole = jnp.zeros(sizes + block.shape, block.dtype)
    for m in range(1 << count):
        masks = partner_index(dims, m)
        at = tuple(lax.axis_index(a) ^ masks.get(a, 0) for a in axes)
        place = at + (0,) * block.ndim
        whole = lax.dynamic_update_slice(whole, pieces[m][(None,) * len(axes)], place)
    return whole


def scatter_blocks(whole, dims, axes):
    count = len(dims)
    shape = whole.shape[len(axes) :]

    def entry(m):
        masks = partner_index(dims, m)
        at = tuple(lax.axis_index(a) ^ masks.get(a, 0) for a in axes)
        piece = lax.dynamic_slice(whole, at + (0,) * len(shape), (1,) * len(axes) + shape)
        return piece.reshape(shape)

    pieces = [entry(m) for m in range(1 << count)]
    for bit in reversed(range(count)):
        half = 1 << bit
        kept = []
        for m in range(half):
            arrived = swap(pieces[m | half], dims[bit])
            total = pieces[m].astype(f32) + arrived.astype(f32)
            kept.append(total if bit == 0 else total.astype(bf16))
        pieces = kept
    return pieces[0]


def allowed_pairs(row_pos, row_ids, col_pos, col_ids):
    return (row_ids == col_ids) & (row_pos >= col_pos)


def forward_kernel(scale, rp, ri, cp, ci, q, k, v, out, log_total):
    scores = lax.dot_general(q[...], k[...], (((1,), (1,)), ((), ())), preferred_element_type=f32)
    allowed = allowed_pairs(rp[...], ri[...], cp[...], ci[...])
    scores = jnp.where(allowed, scores * scale, masked_score)
    top = jnp.max(scores, axis=-1, keepdims=True)
    expo = jnp.exp(scores - top)
    total = jnp.sum(expo, axis=-1, keepdims=True)
    probability = (expo * (1.0 / total)).astype(bf16)
    out[...] = jnp.dot(probability, v[...], preferred_element_type=f32)
    log_total[0] = top + jnp.log(total)


def backward_kernel(scale, rp, ri, cp, ci, q, k, v, d_out, out, log_total, d_q, d_k, d_v):
    @pl.when(pl.program_id(1) == 0)
    def _():
        d_k[...] = jnp.zeros_like(d_k)
        d_v[...] = jnp.zeros_like(d_v)

    q_blk, k_all, v_all, d_blk = q[...], k[...], v[...], d_out[...]
    scores = lax.dot_general(q_blk, k_all, (((1,), (1,)), ((), ())), preferred_element_type=f32)
    allowed = allowed_pairs(rp[...], ri[...], cp[...], ci[...])
    scores = jnp.where(allowed, scores * scale, masked_score)
    probability = jnp.exp(scores - log_total[0])
    row_dot = jnp.sum(d_blk.astype(f32) * out[...], axis=-1, keepdims=True)
    d_prob = lax.dot_general(d_blk, v_all, (((1,), (1,)), ((), ())), preferred_element_type=f32)
    d_scores = (probability * (d_prob - row_dot)).astype(bf16)
    d_q[...] = jnp.dot(d_scores, k_all, preferred_element_type=f32) * scale
    across = (((0,), (0,)), ((), ()))
    d_k[...] += lax.dot_general(d_scores, q_blk, across, preferred_element_type=f32) * scale
    d_v[...] += lax.dot_general(
        probability.astype(bf16), d_blk, across, preferred_element_type=f32
    )


def attention_specs(tokens, block, head_dim):
    rows = pl.BlockSpec((block, 1), lambda h, b: (b, 0))
    cols = pl.BlockSpec((1, tokens), lambda h, b: (0, 0))
    mine = pl.BlockSpec((block, head_dim), lambda h, b: (b, h))
    every = pl.BlockSpec((tokens, head_dim), lambda h, b: (0, h))
    logs = pl.BlockSpec((1, block, 1), lambda h, b: (h, b, 0))
    return rows, cols, mine, every, logs


def attend(places, q, k, v, heads, block):
    tokens, width = q.shape
    head_dim = width // heads
    rows, cols, mine, every, logs = attention_specs(tokens, block, head_dim)
    return pl.pallas_call(
        functools.partial(forward_kernel, head_dim**-0.5),
        grid=(heads, tokens // block),
        in_specs=[rows, rows, cols, cols, mine, every, every],
        out_specs=[mine, logs],
        out_shape=[
            jax.ShapeDtypeStruct((tokens, width), f32),
            jax.ShapeDtypeStruct((heads, tokens, 1), f32),
        ],
        compiler_params=pltpu.CompilerParams(vmem_limit_bytes=48 * 1024 * 1024),
        cost_estimate=pl.CostEstimate(
            flops=4 * tokens * tokens * width,
            bytes_accessed=14 * tokens * width,
            transcendentals=heads * tokens * tokens,
        ),
        name="attend",
    )(*places, q, k, v)


def attend_back(places, q, k, v, d_out, out, log_total, heads, block):
    tokens, width = q.shape
    head_dim = width // heads
    rows, cols, mine, every, logs = attention_specs(tokens, block, head_dim)
    return pl.pallas_call(
        functools.partial(backward_kernel, head_dim**-0.5),
        grid=(heads, tokens // block),
        in_specs=[rows, rows, cols, cols, mine, every, every, mine, mine, logs],
        out_specs=[mine, every, every],
        out_shape=[jax.ShapeDtypeStruct((tokens, width), f32)] * 3,
        compiler_params=pltpu.CompilerParams(vmem_limit_bytes=48 * 1024 * 1024),
        cost_estimate=pl.CostEstimate(
            flops=10 * tokens * tokens * width,
            bytes_accessed=24 * tokens * width,
            transcendentals=heads * tokens * tokens,
        ),
        name="attend_back",
    )(*places, q, k, v, d_out, out, log_total)


def dot(left, right):
    return jnp.dot(left, right, preferred_element_type=f32)


def dot_t(left, right):
    return lax.dot_general(left, right, (((1,), (1,)), ((), ())), preferred_element_type=f32)


def t_dot(left, right):
    return lax.dot_general(left, right, (((0,), (0,)), ((), ())), preferred_element_type=f32)


def held(block):
    return lax.optimization_barrier(block)


def rope_tables(positions, head_dim):
    half_dim = head_dim // 2
    frequency = rope_base ** (-(jnp.arange(half_dim, dtype=f32) * 2.0 / head_dim))
    angles = positions.astype(f32)[:, None] * frequency[None, :]
    cosine, sine = jnp.cos(angles), jnp.sin(angles)
    return jnp.concatenate([cosine, cosine], 1)[:, None, :], jnp.concatenate([-sine, sine], 1)[:, None, :]


def rotate(values, tables, heads, back=False):
    cosine, sine = tables
    split = values.reshape(values.shape[0], heads, -1)
    half = split.shape[-1] // 2
    other = jnp.concatenate([split[..., half:], split[..., :half]], axis=-1)
    turned = split * cosine - other * sine if back else split * cosine + other * sine
    return turned.reshape(values.shape)


def rms(values):
    inverse = lax.rsqrt(jnp.mean(values * values, axis=-1, keepdims=True) + norm_eps)
    return values * inverse, inverse


def rms_back(grad, normed, inverse, gain):
    scaled = grad * gain
    return (scaled - normed * jnp.mean(scaled * normed, axis=-1, keepdims=True)) * inverse


def per_device(
    tokens,
    segment_ids,
    w_query,
    w_key,
    w_value,
    w_out,
    w_gate,
    w_up,
    w_down,
    query_gain,
    key_gain,
    attn_gain,
    ff_gain,
    cotangent,
):
    inputs = tokens[0]
    tok, width = inputs.shape
    n_seq, n_hi, n_lo, n_core = (lax.axis_size(a) for a in ("seq", "zhi", "zlo", "core"))
    n_dev = n_seq * n_hi * n_lo * n_core
    seq = lax.axis_index("seq")
    heads = HEADS // n_seq
    head_dim = width // HEADS
    part = width // n_seq
    length = n_seq * tok
    d_rows = w_query.shape[0]
    ff_rows = w_down.shape[0]
    units = ff_rows * n_hi * n_core

    seq_dims = dims_of("seq")
    cube_dims = seq_dims + dims_of("zlo")
    z_dims = dims_of("zhi") + dims_of("zlo") + dims_of("core")
    pair_dims = dims_of("zhi") + dims_of("core")

    every = ("seq", "zhi", "zlo", "core")
    gains = jnp.stack([query_gain, key_gain, attn_gain, ff_gain])
    gains = lax.all_gather(gains, every, axis=0, tiled=False)
    gains = jnp.transpose(gains, (1, 0, 2)).reshape(4, width).astype(f32)
    my_cols = lambda row: lax.dynamic_slice(row, (seq * part,), (part,))
    gain_query, gain_key = my_cols(gains[0]), my_cols(gains[1])
    gain_attn, gain_ff = gains[2], gains[3]

    w_qkv = jnp.stack([w_query, w_key, w_value], 1).reshape(d_rows, 3, n_seq, part)
    w_qkv = jnp.transpose(w_qkv, (2, 0, 1, 3)).reshape(n_seq, d_rows, 3 * part)
    w_qkv = lax.all_to_all(w_qkv, "seq", 0, 0, tiled=True)
    w_qkv = gather_blocks(w_qkv, z_dims, ("zhi", "zlo", "core"))
    w_qkv = jnp.transpose(w_qkv, (3, 0, 1, 2, 4, 5)).reshape(width, 3 * part)
    out_weight = gather_blocks(w_out, z_dims, ("zhi", "zlo", "core")).reshape(part, width)

    x_all = jnp.concatenate(spread(inputs, seq_dims), axis=0)
    ids = jnp.concatenate(spread(segment_ids, seq_dims), axis=1) if n_seq == 1 else None
    id_pieces = {0: segment_ids}
    for m in by_size(len(seq_dims)):
        via = route(m, len(seq_dims))
        id_pieces[m] = swap(id_pieces[m ^ (1 << via)], seq_dims[via])
    ids = jnp.concatenate([id_pieces[m] for m in range(n_seq)], axis=1)
    positions = jnp.concatenate(
        [(seq ^ m) * tok + jnp.arange(tok, dtype=jnp.int32) for m in range(n_seq)]
    )
    places = (positions[:, None], ids.reshape(length, 1), positions[None, :], ids)
    tables = rope_tables(positions, head_dim)

    w_gu = jnp.stack([w_gate, w_up], 1).reshape(d_rows, 2, n_seq, n_hi, n_lo, n_core, ff_rows)
    w_gu = jnp.transpose(w_gu, (2, 4, 0, 1, 3, 5, 6)).reshape(n_seq * n_lo, d_rows, 2 * units)
    w_gu = lax.all_to_all(w_gu, ("seq", "zlo"), 0, 0, tiled=True)
    w_gu = w_gu.reshape(n_seq, n_lo, d_rows, 2 * units)
    w_gu = gather_blocks(w_gu, pair_dims, ("zhi", "core"))
    w_gu = jnp.transpose(w_gu, (2, 0, 3, 1, 4, 5)).reshape(width, 2 * units)
    down = gather_blocks(w_down, pair_dims, ("zhi", "core")).reshape(units, width)

    raw = dot(x_all, w_qkv)
    query_raw, key_raw = raw[:, :part], raw[:, part : 2 * part]
    value = raw[:, 2 * part :].astype(bf16)
    squares = jnp.stack(
        [jnp.sum(query_raw * query_raw, -1), jnp.sum(key_raw * key_raw, -1)]
    ).reshape(2, n_seq, tok)
    squares = sum_all(jnp.transpose(squares, (1, 0, 2)), seq_dims)
    inverse = lax.rsqrt(jnp.transpose(squares, (1, 0, 2)).reshape(2, length, 1) / width + norm_eps)
    query_norm, key_norm = query_raw * inverse[0], key_raw * inverse[1]
    query = rotate(query_norm * gain_query, tables, heads).astype(bf16)
    key = rotate(key_norm * gain_key, tables, heads).astype(bf16)

    attended, log_total = attend(places, query, key, value, heads, tok)
    attn_low = attended.astype(bf16)
    rows_of = lambda block, m: block[m * tok : (m + 1) * tok]
    branch = collect(
        [held(dot(rows_of(attn_low, m), out_weight).astype(bf16)) for m in range(n_seq)], seq_dims
    )
    branch_norm, branch_inv = rms(branch)
    hidden = inputs.astype(f32) + branch_norm * gain_attn
    hidden_low = hidden.astype(bf16)

    h_pieces = spread(hidden_low, cube_dims)
    gates, ups, middles, partials = [], [], [], []
    for piece in h_pieces:
        gate_act = dot(piece, w_gu[:, :units])
        up_act = dot(piece, w_gu[:, units:])
        middle = (jax.nn.silu(gate_act) * up_act).astype(bf16)
        gates.append(gate_act)
        ups.append(up_act)
        middles.append(middle)
        partials.append(held(dot(middle, down).astype(bf16)))
    ff_raw = collect(partials, cube_dims)
    ff_norm, ff_inv = rms(ff_raw)
    mixed = (hidden + ff_norm * gain_ff).astype(bf16)

    grad_output = cotangent[0].astype(f32)
    grad_ff_gain = jnp.sum(grad_output * ff_norm, axis=0)
    d_ff = rms_back(grad_output, ff_norm, ff_inv, gain_ff).astype(bf16)
    d_ff_pieces = spread(d_ff, cube_dims)
    d_gus, partials = [], []
    for piece, gate_act, up_act in zip(d_ff_pieces, gates, ups, strict=True):
        d_middle = dot_t(piece, down)
        sig = jax.nn.sigmoid(gate_act)
        d_gate = d_middle * up_act * (sig * (1.0 + gate_act * (1.0 - sig)))
        d_up = d_middle * (gate_act * sig)
        d_gu = jnp.concatenate([d_gate.astype(bf16), d_up.astype(bf16)], axis=1)
        d_gus.append(d_gu)
        partials.append(held(dot_t(d_gu, w_gu).astype(bf16)))
    d_hidden = grad_output + collect(partials, cube_dims)

    d_ff_all = jnp.concatenate(d_ff_pieces, axis=0)
    grad_down = t_dot(jnp.concatenate(middles, axis=0), d_ff_all).astype(bf16)
    grad_down = scatter_blocks(
        grad_down.reshape(n_hi, n_core, ff_rows, width), pair_dims, ("zhi", "core")
    )
    grad_gu = t_dot(jnp.concatenate(h_pieces, axis=0), jnp.concatenate(d_gus, axis=0)).astype(bf16)
    grad_gu = grad_gu.reshape(n_seq, n_hi, n_lo, n_core, d_rows, 2 * units)
    grad_gu = jnp.transpose(grad_gu, (1, 3, 0, 2, 4, 5))
    grad_gu = scatter_blocks(grad_gu, pair_dims, ("zhi", "core")).astype(bf16)
    grad_gu = grad_gu.reshape(n_seq * n_lo, d_rows, 2 * units)
    grad_gu = lax.all_to_all(grad_gu, ("seq", "zlo"), 0, 0, tiled=True)
    grad_gu = grad_gu.reshape(n_seq, n_lo, d_rows, 2, n_hi, n_core, ff_rows)
    grad_gu = jnp.transpose(grad_gu, (3, 2, 0, 4, 1, 5, 6)).reshape(2, d_rows, -1).astype(f32)

    grad_attn_gain = jnp.sum(d_hidden * branch_norm, axis=0)
    d_branch = rms_back(d_hidden, branch_norm, branch_inv, gain_attn).astype(bf16)
    d_branch_all = jnp.concatenate(spread(d_branch, seq_dims), axis=0)
    d_attended = dot_t(d_branch_all, out_weight).astype(bf16)
    grad_out = t_dot(attn_low, d_branch_all).astype(bf16)
    grad_out = scatter_blocks(
        grad_out.reshape(n_hi, n_lo, n_core, d_rows, width), z_dims, ("zhi", "zlo", "core")
    )
    d_query, d_key, d_value = attend_back(
        places, query, key, value, d_attended, attended, log_total, heads, tok
    )
    e_query = rotate(d_query, tables, heads, back=True)
    e_key = rotate(d_key, tables, heads, back=True)
    grad_query_gain = jnp.sum(e_query * query_norm, axis=0)
    grad_key_gain = jnp.sum(e_key * key_norm, axis=0)
    e_query, e_key = e_query * gain_query, e_key * gain_key
    means = jnp.stack(
        [jnp.sum(e_query * query_norm, -1), jnp.sum(e_key * key_norm, -1)]
    ).reshape(2, n_seq, tok)
    means = sum_all(jnp.transpose(means, (1, 0, 2)), seq_dims)
    means = jnp.transpose(means, (1, 0, 2)).reshape(2, length, 1) / width
    d_qkv = jnp.concatenate(
        [
            ((e_query - query_norm * means[0]) * inverse[0]).astype(bf16),
            ((e_key - key_norm * means[1]) * inverse[1]).astype(bf16),
            d_value.astype(bf16),
        ],
        axis=1,
    )
    grad_qkv = t_dot(x_all, d_qkv).astype(bf16)
    grad_qkv = grad_qkv.reshape(n_seq, n_hi, n_lo, n_core, d_rows, 3 * part)
    grad_qkv = jnp.transpose(grad_qkv, (1, 2, 3, 0, 4, 5))
    grad_qkv = scatter_blocks(grad_qkv, z_dims, ("zhi", "zlo", "core")).astype(bf16)
    grad_qkv = lax.all_to_all(grad_qkv, "seq", 0, 0, tiled=True)
    grad_qkv = grad_qkv.reshape(n_seq, d_rows, 3, part)
    grad_qkv = jnp.transpose(grad_qkv, (2, 1, 0, 3)).reshape(3, d_rows, width).astype(f32)

    input_grad = d_hidden + collect(
        [held(dot_t(rows_of(d_qkv, m), w_qkv).astype(bf16)) for m in range(n_seq)], seq_dims
    )

    full_row = lambda cols: lax.dynamic_update_slice(jnp.zeros((width,), f32), cols, (seq * part,))
    rows = jnp.stack(
        [full_row(grad_query_gain), full_row(grad_key_gain), grad_attn_gain, grad_ff_gain]
    )
    rows = jnp.transpose(rows.reshape(4, n_dev, d_rows), (1, 0, 2)).reshape(n_dev, 4 * d_rows)
    rows = lax.psum_scatter(rows, every, scatter_dimension=0, tiled=False).reshape(4, d_rows)

    return (
        mixed[None],
        input_grad[None],
        grad_qkv[0],
        grad_qkv[1],
        grad_qkv[2],
        grad_out,
        grad_gu[0],
        grad_gu[1],
        grad_down,
        rows[0],
        rows[1],
        rows[2],
        rows[3],
    )


def solution(mesh):
    n_seq, n_row = mesh.shape["seq"], mesh.shape["row"]
    n_core = 2
    n_lo = 2
    n_hi = n_row // (n_core * n_lo)
    cut = Mesh(
        mesh.devices.reshape(n_seq, n_hi, n_lo, n_core), ("seq", "zhi", "zlo", "core")
    )
    row = ("zhi", "zlo", "core")
    every = ("seq",) + row
    acts = P(row, "seq", None)
    matrix = P(every, None)
    vector = P(every)
    return jax.shard_map(
        per_device,
        mesh=cut,
        in_specs=(acts, P(row, "seq")) + (matrix,) * 7 + (vector,) * 4 + (acts,),
        out_specs=(acts, acts) + (matrix,) * 7 + (vector,) * 4,
        check_vma=False,
    )
```

time: 4450 us -> 1130 us (0.25)
  waiting for transfers between devices: 3690 us -> 432 us
  matrix products: 294 us -> 204 us
    reduce_scatter x4 -> x0, waiting for transfers between devices: 2310 us -> none  [the longest x3 2130 us: spread_grad(): lax.psum_scatter(jnp.einsum('tc,tf->cf', left_side, right_side, preferred...]
    all_gather x7 -> x0, waiting for transfers between devices: 606 us -> none  [the longest x1 178 us: per_device(): lax.all_gather(w_up, ('seq', 'row'), axis=0, tiled=True)]
    unnamed x17 -> x0, waiting for transfers between devices: 351 us -> none
    dot_general x28 -> x54, matrix products: 294 us -> 204 us  [the longest x29 77.3 us: dot(): return jnp.dot(left, right, preferred_element_type=f32)]
    unnamed x2 -> x1, blocking collectives: 101 us -> 37.9 us
    unnamed x157 -> x230, local copies, waits for them, and re-layouts: 81.4 us -> 31.8 us
    ppermute x22 -> x99, starting transfers between devices: 135 us -> 106 us  [swap(): lax.ppermute(block, axis, [(i, i ^ mask) for i in range(lax.axis_size(axi...]
    ppermute x22 -> x99, waiting for transfers between devices: 423 us -> 430 us  [swap(): lax.ppermute(block, axis, [(i, i ^ mask) for i in range(lax.axis_size(axi...]
  transfers between devices with their start and end apart: 36 -> 103, of which waited for: 34 -> 37; matrix products, arithmetic and copies ran while one was open for 7% -> 32% of each run, Pallas kernels for 0% -> 3%
where the time goes in v1:
time: 1130 us; the launch traced here: 1120 us
  waiting for transfers between devices  432 us (38%)
  matrix products  204 us (18%)
  local copies, waits for them, and re-layouts  140 us (12%)
  starting transfers between devices  133 us (12%)
  other arithmetic  91.6 us (8%)
  blocking collectives  78 us (7%)
  Pallas kernels  37.2 us (3%)
    ppermute x99, waiting for transfers between devices, swap(): lax.ppermute(block, axis, [(i, i ^ mask) for i in range(lax.axis_size(axi...  430 us
    ppermute x99, starting transfers between devices, swap(): lax.ppermute(block, axis, [(i, i ^ mask) for i in range(lax.axis_size(axi...  106 us
    dot_general x29, matrix products, dot(): return jnp.dot(left, right, preferred_element_type=f32)  77.3 us
    dot_general x21, matrix products, dot_t(): lax.dot_general(left, right, (((1,), (1,)), ((), ())), preferred_element_...  72.2 us
    dot_general x4, matrix products, t_dot(): lax.dot_general(left, right, (((0,), (0,)), ((), ())), preferred_element_...  54.1 us
    all_gather x1, blocking collectives, per_device(): gains = lax.all_gather(gains, every, axis=0, tiled=False)  40.1 us
    unnamed x1, blocking collectives  37.9 us
    unnamed x230, local copies, waits for them, and re-layouts  31.8 us
  transfers between devices with their start and end apart: 103, of which 37 were waited for; matrix products, arithmetic and copies ran while one was open for 32% of the time, Pallas kernels for 3%

profile of v1, /device:TPU:0, one launch (start us, length us, event | category | flops | bytes accessed | tf_op | source)
XLA Modules:
  0.0 1118.7 jit_solution(1168284275638103265)
XLA Ops:
  13.2 4.3 all-to-all-start
  20.1 40.1 %all-gather.1 = bf16[32,4,64]{2,1,0:T(4,128)(2,1)S(1)} all-gather(bf16[1,4,64]{2,1,0:T(4,128)(2,1)S(1)} %maximum_bitcast_fusion.4), channel_id=2, replica_groups=mesh['seq'=4,'zhi'=2,'zlo'=2,'core'=2] {'seq','zhi','zlo','core'}, dimensions={0}, use_global_device_ids=true | all-gather | bytes 16896 | tf_op jit(solution)/shard_map/all_gather | solution.py:323
  75.4 4.5 reshape.387
  92.8 23.4 %collective-permute-done.18 = bf16[64,2048]{1,0:T(8,128)(2,1)S(1)} collective-permute-done((bf16[64,2048]{1,0:T(8,128)(2,1)}, bf16[64,2048]{1,0:T(8,128)(2,1)S(1)}, u32[]{:S(2)}, u32[]{:S(2)}) %collective-permute-start.18) | collective-permute-done | bytes 262176 | tf_op jit(solution)/shard_map/ppermute | solution.py:29
  117.7 14.4 %all-to-all-start.1 = ((bf16[8,64,2048]{2,1,0:T(8,128)(2,1)}), bf16[8,64,2048]{2,1,0:T(8,128)(2,1)}, u32[]{:S(2)}, u32[]{:S(2)}) async-start(bf16[8,64,2048]{2,1,0:T(8,128)(2,1)} %reshape.387), calls=%async_computation.1 | async-start | bytes 4194304 | tf_op jit(solution)/shard_map/all_to_all | solution.py:351
  140.2 33.4 %collective-permute-done.7 = bf16[4,64,1536]{2,1,0:T(8,128)(2,1)S(1)} collective-permute-done((bf16[4,64,1536]{2,1,0:T(8,128)(2,1)S(1)}, bf16[4,64,1536]{2,1,0:T(8,128)(2,1)S(1)}, u32[]{:S(2)}, u32[]{:S(2)}) %collective-permute-start.7) | collective-permute-done | bytes 786464 | tf_op jit(solution)/shard_map/ppermute | solution.py:29
  173.6 6.9 collective-permute-start.9
  180.5 11.8 %collective-permute-done.8 = bf16[4,64,1536]{2,1,0:T(8,128)(2,1)S(1)} collective-permute-done((bf16[4,64,1536]{2,1,0:T(8,128)(2,1)S(1)}, bf16[4,64,1536]{2,1,0:T(8,128)(2,1)S(1)}, u32[]{:S(2)}, u32[]{:S(2)}) %collective-permute-start.8) | collective-permute-done | bytes 786464 | tf_op jit(solution)/shard_map/ppermute | solution.py:29
  195.2 13.8 %collective-permute-done.9 = bf16[4,64,1536]{2,1,0:T(8,128)(2,1)S(1)} collective-permute-done((bf16[4,64,1536]{2,1,0:T(8,128)(2,1)S(1)}, bf16[4,64,1536]{2,1,0:T(8,128)(2,1)S(1)}, u32[]{:S(2)}, u32[]{:S(2)}) %collective-permute-start.9) | collective-permute-done | bytes 786464 | tf_op jit(solution)/shard_map/ppermute | solution.py:29
  214.2 12.1 %collective-permute-done.6 = bf16[256,1024]{1,0:T(8,128)(2,1)S(1)} collective-permute-done((bf16[256,1024]{1,0:T(8,128)(2,1)S(1)}, bf16[256,1024]{1,0:T(8,128)(2,1)S(1)}, u32[]{:S(2)}, u32[]{:S(2)}) %collective-permute-start.6) | collective-permute-done | bytes 524320 | tf_op jit(solution)/shard_map/ppermute | solution.py:29
  226.3 8.4 fusion.103
  246.1 4.7 fusion.17
  253.7 5.4 fusion.110
  271.6 15.9 %attend.1 = (f32[1024,512]{1,0:T(8,128)}, f32[4,1024,1]{2,1,0:T(8,128)}) custom-call(s32[1024,1]{1,0:T(8,128)S(1)} %copy.98.rp, s32[1024,1]{1,0:T(8,128)S(1)} %copy.99.ri, s32[1,1024]{1,0:T(1,128)S(1)} %bitcast.342, s32[1,1024]{1,0:T(1,128)S(1)} %constant_dynamic-update-slice_fusion.ci, bf16[1024,512]{1,0:T(8,128)(2,1)S(1)} %get-tuple-element.114.q, ...), custom_call_target="tpu_custom_call" | custom-call | flops 2147483648 | bytes 7340032 | tf_op jit(solution)/shard_map/attend/pallas_call | solution.py:205
  321.1 7.0 collective-permute-done.24
  346.2 12.3 %collective-permute-done.39 = bf16[256,2048]{1,0:T(8,128)(2,1)S(1)} collective-permute-done((bf16[256,2048]{1,0:T(8,128)(2,1)S(1)}, bf16[256,2048]{1,0:T(8,128)(2,1)S(1)}, u32[]{:S(2)}, u32[]{:S(2)}) %collective-permute-start.39) | collective-permute-done | bytes 1048608 | tf_op jit(solution)/shard_map/ppermute | solution.py:29
  361.7 28.1 %collective-permute-done.33 = bf16[256,2048]{1,0:T(8,128)(2,1)S(1)} collective-permute-done((bf16[256,2048]{1,0:T(8,128)(2,1)S(1)}, bf16[256,2048]{1,0:T(8,128)(2,1)S(1)}, u32[]{:S(2)}, u32[]{:S(2)}) %collective-permute-start.33) | collective-permute-done | bytes 1048608 | tf_op jit(solution)/shard_map/ppermute | solution.py:29
  393.4 19.4 %collective-permute-done.27 = bf16[4,2,64,2048]{3,2,1,0:T(8,128)(2,1)S(1)} collective-permute-done((bf16[4,2,64,2048]{3,2,1,0:T(8,128)(2,1)}, bf16[4,2,64,2048]{3,2,1,0:T(8,128)(2,1)S(1)}, u32[]{:S(2)}, u32[]{:S(2)}) %collective-permute-start.27) | collective-permute-done | bytes 2097184 | tf_op jit(solution)/shard_map/ppermute | solution.py:29
  416.0 9.8 collective-permute-done.37
  466.5 5.0 convolution_convert_fusion.16
  500.3 18.0 %collective-permute-done.43 = bf16[256,2048]{1,0:T(8,128)(2,1)S(1)} collective-permute-done((bf16[256,2048]{1,0:T(8,128)(2,1)S(1)}, bf16[256,2048]{1,0:T(8,128)(2,1)S(1)}, u32[]{:S(2)}, u32[]{:S(2)}) %collective-permute-start.43) | collective-permute-done | bytes 1048608 | tf_op jit(solution)/shard_map/ppermute | solution.py:29
  527.7 13.4 %collective-permute-done.44 = bf16[256,2048]{1,0:T(8,128)(2,1)} collective-permute-done((bf16[256,2048]{1,0:T(8,128)(2,1)S(1)}, bf16[256,2048]{1,0:T(8,128)(2,1)}, u32[]{:S(2)}, u32[]{:S(2)}) %collective-permute-start.44) | collective-permute-done | bytes 1048608 | tf_op jit(solution)/shard_map/ppermute | solution.py:29
  561.7 9.5 collective-permute-done.51
  586.5 4.9 multiply_convert_fusion.6
  600.1 6.2 collective-permute-done.55
  641.6 4.0 multiply_convert_fusion.12
  654.4 13.1 %convolution_convert_fusion.2 = bf16[1024,2048]{1,0:T(8,128)(2,1)S(1)} fusion(bf16[2048,1024]{1,0:T(8,128)(2,1)} %copy-done.87, bf16[2048,2048]{1,0:T(8,128)(2,1)} %constant_dynamic-update-slice_fusion.33), kind=kOutput, calls=%fused_computation.9 | convolution fusion | flops 8592031744 | bytes 16777216 | tf_op jit(solution)/shard_map/dot_general | solution.py:253
  674.0 20.7 %collective-permute-done.61 = bf16[256,2048]{1,0:T(8,128)(2,1)S(1)} collective-permute-done((bf16[256,2048]{1,0:T(8,128)(2,1)S(1)}, bf16[256,2048]{1,0:T(8,128)(2,1)S(1)}, u32[]{:S(2)}, u32[]{:S(2)}) %collective-permute-start.61) | collective-permute-done | bytes 1048608 | tf_op jit(solution)/shard_map/ppermute | solution.py:29
  699.1 22.6 %convolution_convert_fusion = bf16[2048,2048]{1,0:T(8,128)(2,1)S(1)} fusion(bf16[2048,2048]{1,0:T(8,128)(2,1)} %get-tuple-element.137, bf16[2048,2048]{1,0:T(8,128)(2,1)} %fusion.74), kind=kOutput, calls=%fused_computation | convolution fusion | flops 17184063488 | bytes 25165824 | tf_op jit(solution)/shard_map/dot_general | solution.py:253
  737.2 4.5 fusion
  741.7 15.8 %collective-permute-done.70 = bf16[256,2048]{1,0:T(8,128)(2,1)} collective-permute-done((bf16[256,2048]{1,0:T(8,128)(2,1)}, bf16[256,2048]{1,0:T(8,128)(2,1)}, u32[]{:S(2)}, u32[]{:S(2)}) %collective-permute-start.70) | collective-permute-done | bytes 1048608 | tf_op jit(solution)/shard_map/ppermute | solution.py:29
  765.3 65.6 %collective-permute-done.98 = bf16[256,2048]{1,0:T(8,128)(2,1)} collective-permute-done((bf16[256,2048]{1,0:T(8,128)(2,1)}, bf16[256,2048]{1,0:T(8,128)(2,1)}, u32[]{:S(2)}, u32[]{:S(2)}) %collective-permute-start.98) | collective-permute-done | bytes 1048608 | tf_op jit(solution)/shard_map/ppermute | solution.py:29
  834.7 5.3 convolution_convert_fusion.28.d_out
  840.1 21.3 %attend_back.1 = (f32[1024,512]{1,0:T(8,128)}, f32[1024,512]{1,0:T(8,128)}, f32[1024,512]{1,0:T(8,128)}) custom-call(s32[1024,1]{1,0:T(8,128)S(1)} %copy.98.rp, s32[1024,1]{1,0:T(8,128)S(1)} %copy.99.ri, s32[1,1024]{1,0:T(1,128)S(1)} %bitcast.343, s32[1,1024]{1,0:T(1,128)S(1)} %constant_dynamic-update-slice_fusion.ci, bf16[1024,512]{1,0:T(8,128)(2,1)S(1)} %copy-done.3, ...), custom_call_target="tpu_custom_call" | custom-call | flops 5368709120 | bytes 12582912 | tf_op jit(solution)/shard_map/attend_back/pallas_call | solution.py:228
  880.5 37.9 %all-reduce = f32[32,256]{1,0:T(8,128)S(1)} all-reduce(f32[32,256]{1,0:T(8,128)S(1)} %reshape.410), channel_id=3, replica_groups=mesh['seq'=4,'zhi'=2,'zlo'=2,'core'=2] {'seq','zhi','zlo','core'}, use_global_device_ids=true, to_apply=%region_12.13.clone | all-reduce | flops 8192 | bytes 65536
  923.2 4.1 multiply_convert_fusion.1
  927.4 13.5 %convolution_convert_fusion.1 = bf16[2048,1536]{1,0:T(8,128)(2,1)S(1)} fusion(bf16[256,1024]{1,0:T(8,128)(2,1)} %copy-done.68, bf16[256,1024]{1,0:T(8,128)(2,1)S(1)} %copy-done.67, bf16[256,2048]{1,0:T(8,128)(2,1)} %collective-permute-done.4, bf16[256,2048]{1,0:T(8,128)(2,1)} %collective-permute-done.3, bf16[256,2048]{1,0:T(8,128)(2,1)} %bitcast.400, ...), kind=kOutput, calls=%fused_computation.1 | convolution fusion | flops 6476005376 | bytes 13631488 | tf_op jit(solution)/shard_map/dot_general | solution.py:253
  942.2 5.0 convolution_convert_fusion.3
  953.4 15.5 %collective-permute-done.84 = bf16[4,64,1536]{2,1,0:T(8,128)(2,1)S(1)} collective-permute-done((bf16[4,64,1536]{2,1,0:T(8,128)(2,1)S(1)}, bf16[4,64,1536]{2,1,0:T(8,128)(2,1)S(1)}, u32[]{:S(2)}, u32[]{:S(2)}) %collective-permute-start.84) | collective-permute-done | bytes 786464 | tf_op jit(solution)/shard_map/ppermute | solution.py:29
  975.1 29.8 %collective-permute-done.81 = bf16[4,64,1536]{2,1,0:T(8,128)(2,1)S(1)} collective-permute-done((bf16[4,64,1536]{2,1,0:T(8,128)(2,1)S(1)}, bf16[4,64,1536]{2,1,0:T(8,128)(2,1)S(1)}, u32[]{:S(2)}, u32[]{:S(2)}) %collective-permute-start.81) | collective-permute-done | bytes 786464 | tf_op jit(solution)/shard_map/ppermute | solution.py:29
  1014.4 5.6 add_convert_fusion
  1024.4 4.5 all-to-all-start.3
  1028.9 4.9 convolution_convert_fusion.8
  1040.6 24.8 %collective-permute-done.77 = bf16[256,1024]{1,0:T(8,128)(2,1)S(1)} collective-permute-done((bf16[256,1024]{1,0:T(8,128)(2,1)S(1)}, bf16[256,1024]{1,0:T(8,128)(2,1)S(1)}, u32[]{:S(2)}, u32[]{:S(2)}) %collective-permute-start.77) | collective-permute-done | bytes 524320 | tf_op jit(solution)/shard_map/ppermute | solution.py:29
  1067.6 5.0 convolution_convert_fusion.11
  1074.6 12.4 %collective-permute-done.76 = bf16[256,2048]{1,0:T(8,128)(2,1)S(1)} collective-permute-done((bf16[256,2048]{1,0:T(8,128)(2,1)S(1)}, bf16[256,2048]{1,0:T(8,128)(2,1)S(1)}, u32[]{:S(2)}, u32[]{:S(2)}) %collective-permute-start.76) | collective-permute-done | bytes 1048608 | tf_op jit(solution)/shard_map/ppermute | solution.py:29
  1097.6 6.6 reshape.425
  1104.2 5.0 fusion.106
  (654 shorter events, 435.5 us)
Async XLA Ops:
  0.7 136.7 %collective-permute-start.4 = (bf16[256,2048]{1,0:T(8,128)(2,1)}, bf16[256,2048]{1,0:T(8,128)(2,1)}, u32[]{:S(2)}, u32[]{:S(2)}) collective-permute-start(bf16[256,2048]{1,0:T(8,128)(2,1)} %bitcast.398), channel_id=1, source_target_pairs={{0,16},{8,24},{16,0},{24,8},{1,17},{9,25},{17,1},{25,9},{2,18},{10... | collective-permute-start | bytes 3145736 | tf_op jit(solution)/shard_map/ppermute | solution.py:29
  3.7 134.8 %collective-permute-start.3 = (bf16[256,2048]{1,0:T(8,128)(2,1)}, bf16[256,2048]{1,0:T(8,128)(2,1)}, u32[]{:S(2)}, u32[]{:S(2)}) collective-permute-start(bf16[256,2048]{1,0:T(8,128)(2,1)} %bitcast.399), channel_id=1, source_target_pairs={{0,8},{8,0},{16,24},{24,16},{1,9},{9,1},{17,25},{25,17},{2,10},{10... | collective-permute-start | bytes 3145736 | tf_op jit(solution)/shard_map/ppermute | solution.py:29
  5.2 74.8 %collective-permute-start.1 = (s32[1,256]{1,0:T(1,128)}, s32[1,256]{1,0:T(1,128)S(1)}, u32[]{:S(2)}, u32[]{:S(2)}) collective-permute-start(s32[1,256]{1,0:T(1,128)} %param.15), channel_id=1, source_target_pairs={{0,16},{8,24},{16,0},{24,8},{1,17},{9,25},{17,1},{25,9},{2,18},{10... | collective-permute-start | bytes 3080 | tf_op jit(solution)/shard_map/ppermute | solution.py:29
  5.7 76.1 %collective-permute-start = (s32[1,256]{1,0:T(1,128)}, s32[1,256]{1,0:T(1,128)S(1)}, u32[]{:S(2)}, u32[]{:S(2)}) collective-permute-start(s32[1,256]{1,0:T(1,128)} %param.15), channel_id=1, source_target_pairs={{0,8},{8,0},{16,24},{24,16},{1,9},{9,1},{17,25},{25,17},{2,10},{10... | collective-permute-start | bytes 3080 | tf_op jit(solution)/shard_map/ppermute | solution.py:29
  13.2 104.5 %all-to-all-start = ((bf16[4,64,1536]{2,1,0:T(8,128)(2,1)}), bf16[4,64,1536]{2,1,0:T(8,128)(2,1)S(1)}, u32[]{:S(2)}, u32[]{:S(2)}) async-start(bf16[4,64,1536]{2,1,0:T(8,128)(2,1)} %reshape.382), calls=%async_computation | async-start | bytes 1572864 | tf_op jit(solution)/shard_map/all_to_all | solution.py:331
  17.5 68.1 %collective-permute-start.16 = (bf16[64,2048]{1,0:T(8,128)(2,1)}, bf16[64,2048]{1,0:T(8,128)(2,1)}, u32[]{:S(2)}, u32[]{:S(2)}) collective-permute-start(bf16[64,2048]{1,0:T(8,128)(2,1)} %param.19), channel_id=1, source_target_pairs={{0,4},{4,0},{1,5},{5,1},{2,6},{6,2},{3,7},{7,3},{8,12},{12,8},{9,1... | collective-permute-start | bytes 786440 | tf_op jit(solution)/shard_map/ppermute | solution.py:29
  85.3 31.7 %collective-permute-start.19 = (bf16[64,2048]{1,0:T(8,128)(2,1)}, bf16[64,2048]{1,0:T(8,128)(2,1)S(1)}, u32[]{:S(2)}, u32[]{:S(2)}) collective-permute-start(bf16[64,2048]{1,0:T(8,128)(2,1)} %param.19), channel_id=1, source_target_pairs={{0,1},{1,0},{2,3},{3,2},{4,5},{5,4},{6,7},{7,6},{8,9},{9,8},{10,11... | collective-permute-start | bytes 786440 | tf_op jit(solution)/shard_map/ppermute | solution.py:29
  85.6 228.2 %collective-permute-start.30 = (bf16[256,2048]{1,0:T(8,128)(2,1)}, bf16[256,2048]{1,0:T(8,128)(2,1)}, u32[]{:S(2)}, u32[]{:S(2)}) collective-permute-start(bf16[256,2048]{1,0:T(8,128)(2,1)} %param.22), channel_id=1, source_target_pairs={{0,4},{4,0},{1,5},{5,1},{2,6},{6,2},{3,7},{7,3},{8,12},{12,8},{9,1... | collective-permute-start | bytes 3145736 | tf_op jit(solution)/shard_map/ppermute | solution.py:29
  117.7 200.8 %all-to-all-start.1 = ((bf16[8,64,2048]{2,1,0:T(8,128)(2,1)}), bf16[8,64,2048]{2,1,0:T(8,128)(2,1)}, u32[]{:S(2)}, u32[]{:S(2)}) async-start(bf16[8,64,2048]{2,1,0:T(8,128)(2,1)} %reshape.387), calls=%async_computation.1 | async-start | bytes 4194304 | tf_op jit(solution)/shard_map/all_to_all | solution.py:351
  132.1 41.4 %collective-permute-start.7 = (bf16[4,64,1536]{2,1,0:T(8,128)(2,1)S(1)}, bf16[4,64,1536]{2,1,0:T(8,128)(2,1)S(1)}, u32[]{:S(2)}, u32[]{:S(2)}) collective-permute-start(bf16[4,64,1536]{2,1,0:T(8,128)(2,1)S(1)} %all-to-all-done), channel_id=1, source_target_pairs={{0,4},{4,0},{1,5},{5,1},{2,6},{6,2},{3,7},{7,3},{8,12},{12,8},{9,1... | collective-permute-start | bytes 2359304 | tf_op jit(solution)/shard_map/ppermute | solution.py:29
  134.9 57.4 %collective-permute-start.8 = (bf16[4,64,1536]{2,1,0:T(8,128)(2,1)S(1)}, bf16[4,64,1536]{2,1,0:T(8,128)(2,1)S(1)}, u32[]{:S(2)}, u32[]{:S(2)}) collective-permute-start(bf16[4,64,1536]{2,1,0:T(8,128)(2,1)S(1)} %all-to-all-done), channel_id=1, source_target_pairs={{0,2},{2,0},{1,3},{3,1},{4,6},{6,4},{5,7},{7,5},{8,10},{10,8},{9,1... | collective-permute-start | bytes 2359304 | tf_op jit(solution)/shard_map/ppermute | solution.py:29
  137.4 197.0 %collective-permute-start.31 = (bf16[256,2048]{1,0:T(8,128)(2,1)}, bf16[256,2048]{1,0:T(8,128)(2,1)}, u32[]{:S(2)}, u32[]{:S(2)}) collective-permute-start(bf16[256,2048]{1,0:T(8,128)(2,1)} %param.22), channel_id=1, source_target_pairs={{0,1},{1,0},{2,3},{3,2},{4,5},{5,4},{6,7},{7,6},{8,9},{9,8},{10,11... | collective-permute-start | bytes 3145736 | tf_op jit(solution)/shard_map/ppermute | solution.py:29
  138.5 70.5 %collective-permute-start.10 = (bf16[4,64,1536]{2,1,0:T(8,128)(2,1)S(1)}, bf16[4,64,1536]{2,1,0:T(8,128)(2,1)S(1)}, u32[]{:S(2)}, u32[]{:S(2)}) collective-permute-start(bf16[4,64,1536]{2,1,0:T(8,128)(2,1)S(1)} %all-to-all-done), channel_id=1, source_target_pairs={{0,1},{1,0},{2,3},{3,2},{4,5},{5,4},{6,7},{7,6},{8,9},{9,8},{10,11... | collective-permute-start | bytes 2359304 | tf_op jit(solution)/shard_map/ppermute | solution.py:29
  173.6 35.4 %collective-permute-start.9 = (bf16[4,64,1536]{2,1,0:T(8,128)(2,1)S(1)}, bf16[4,64,1536]{2,1,0:T(8,128)(2,1)S(1)}, u32[]{:S(2)}, u32[]{:S(2)}) collective-permute-start(bf16[4,64,1536]{2,1,0:T(8,128)(2,1)S(1)} %collective-permute-done.7), channel_id=1, source_target_pairs={{0,2},{2,0},{1,3},{3,1},{4,6},{6,4},{5,7},{7,5},{8,10},{10,8},{9,1... | collective-permute-start | bytes 2359304 | tf_op jit(solution)/shard_map/ppermute | solution.py:29
  213.8 29.8 %collective-permute-start.22 = (bf16[64,2048]{1,0:T(8,128)(2,1)S(1)}, bf16[64,2048]{1,0:T(8,128)(2,1)S(1)}, u32[]{:S(2)}, u32[]{:S(2)}) collective-permute-start(bf16[64,2048]{1,0:T(8,128)(2,1)S(1)} %copy-done.46), channel_id=1, source_target_pairs={{0,1},{1,0},{2,3},{3,2},{4,5},{5,4},{6,7},{7,6},{8,9},{9,8},{10,11... | collective-permute-start | bytes 786440 | tf_op jit(solution)/shard_map/ppermute | solution.py:29
  318.5 94.2 %collective-permute-start.27 = (bf16[4,2,64,2048]{3,2,1,0:T(8,128)(2,1)}, bf16[4,2,64,2048]{3,2,1,0:T(8,128)(2,1)S(1)}, u32[]{:S(2)}, u32[]{:S(2)}) collective-permute-start(bf16[4,2,64,2048]{3,2,1,0:T(8,128)(2,1)} %bitcast.45), channel_id=1, source_target_pairs={{0,4},{4,0},{1,5},{5,1},{2,6},{6,2},{3,7},{7,3},{8,12},{12,8},{9,1... | collective-permute-start | bytes 6291464 | tf_op jit(solution)/shard_map/ppermute | solution.py:29
  328.1 85.0 %collective-permute-start.28 = (bf16[4,2,64,2048]{3,2,1,0:T(8,128)(2,1)}, bf16[4,2,64,2048]{3,2,1,0:T(8,128)(2,1)S(1)}, u32[]{:S(2)}, u32[]{:S(2)}) collective-permute-start(bf16[4,2,64,2048]{3,2,1,0:T(8,128)(2,1)} %bitcast.45), channel_id=1, source_target_pairs={{0,1},{1,0},{2,3},{3,2},{4,5},{5,4},{6,7},{7,6},{8,9},{9,8},{10,11... | collective-permute-start | bytes 6291464 | tf_op jit(solution)/shard_map/ppermute | solution.py:29
  336.2 53.6 %collective-permute-start.33 = (bf16[256,2048]{1,0:T(8,128)(2,1)S(1)}, bf16[256,2048]{1,0:T(8,128)(2,1)S(1)}, u32[]{:S(2)}, u32[]{:S(2)}) collective-permute-start(bf16[256,2048]{1,0:T(8,128)(2,1)S(1)} %get-tuple-element.58), channel_id=1, source_target_pairs={{0,2},{2,0},{1,3},{3,1},{4,6},{6,4},{5,7},{7,5},{8,10},{10,8},{9,1... | collective-permute-start | bytes 3145736 | tf_op jit(solution)/shard_map/ppermute | solution.py:29
  358.4 68.0 %collective-permute-start.40 = (bf16[256,2048]{1,0:T(8,128)(2,1)S(1)}, bf16[256,2048]{1,0:T(8,128)(2,1)S(1)}, u32[]{:S(2)}, u32[]{:S(2)}) collective-permute-start(bf16[256,2048]{1,0:T(8,128)(2,1)S(1)} %collective-permute-done.39), channel_id=1, source_target_pairs={{0,8},{8,0},{16,24},{24,16},{1,9},{9,1},{17,25},{25,17},{2,10},{10... | collective-permute-start | bytes 3145736 | tf_op jit(solution)/shard_map/ppermute | solution.py:29
  359.2 66.6 %collective-permute-start.37 = (bf16[256,2048]{1,0:T(8,128)(2,1)S(1)}, bf16[256,2048]{1,0:T(8,128)(2,1)S(1)}, u32[]{:S(2)}, u32[]{:S(2)}) collective-permute-start(bf16[256,2048]{1,0:T(8,128)(2,1)S(1)} %collective-permute-done.36), channel_id=1, source_target_pairs={{0,2},{2,0},{1,3},{3,1},{4,6},{6,4},{5,7},{7,5},{8,10},{10,8},{9,1... | collective-permute-start | bytes 3145736 | tf_op jit(solution)/shard_map/ppermute | solution.py:29
  551.2 34.9 %collective-permute-start.54 = (bf16[256,2048]{1,0:T(8,128)(2,1)S(1)}, bf16[256,2048]{1,0:T(8,128)(2,1)S(1)}, u32[]{:S(2)}, u32[]{:S(2)}) collective-permute-start(bf16[256,2048]{1,0:T(8,128)(2,1)S(1)} %get-tuple-element.40), channel_id=1, source_target_pairs={{0,8},{8,0},{16,24},{24,16},{1,9},{9,1},{17,25},{25,17},{2,10},{10... | collective-permute-start | bytes 3145736 | tf_op jit(solution)/shard_map/ppermute | solution.py:29
  571.2 36.0 %collective-permute-start.52 = (bf16[256,2048]{1,0:T(8,128)(2,1)S(1)}, bf16[256,2048]{1,0:T(8,128)(2,1)S(1)}, u32[]{:S(2)}, u32[]{:S(2)}) collective-permute-start(bf16[256,2048]{1,0:T(8,128)(2,1)S(1)} %collective-permute-done.51), channel_id=1, source_target_pairs={{0,16},{8,24},{16,0},{24,8},{1,17},{9,25},{17,1},{25,9},{2,18},{10... | collective-permute-start | bytes 3145736 | tf_op jit(solution)/shard_map/ppermute | solution.py:29
  579.1 30.0 %collective-permute-start.58 = (bf16[256,2048]{1,0:T(8,128)(2,1)S(1)}, bf16[256,2048]{1,0:T(8,128)(2,1)S(1)}, u32[]{:S(2)}, u32[]{:S(2)}) collective-permute-start(bf16[256,2048]{1,0:T(8,128)(2,1)S(1)} %collective-permute-done.57), channel_id=1, source_target_pairs={{0,8},{8,0},{16,24},{24,16},{1,9},{9,1},{17,25},{25,17},{2,10},{10... | collective-permute-start | bytes 3145736 | tf_op jit(solution)/shard_map/ppermute | solution.py:29
  607.1 34.5 %collective-permute-start.56 = (bf16[256,768]{1,0:T(8,128)(2,1)}, bf16[256,768]{1,0:T(8,128)(2,1)S(1)}, u32[]{:S(2)}, u32[]{:S(2)}) collective-permute-start(bf16[256,768]{1,0:T(8,128)(2,1)} %slice.524), channel_id=1, source_target_pairs={{0,16},{8,24},{16,0},{24,8},{1,17},{9,25},{17,1},{25,9},{2,18},{10... | collective-permute-start | bytes 1179656 | tf_op jit(solution)/shard_map/ppermute | solution.py:29
  607.9 31.8 %collective-permute-start.53 = (bf16[256,640]{1,0:T(8,128)(2,1)}, bf16[256,640]{1,0:T(8,128)(2,1)}, u32[]{:S(2)}, u32[]{:S(2)}) collective-permute-start(bf16[256,640]{1,0:T(8,128)(2,1)} %slice.523), channel_id=1, source_target_pairs={{0,8},{8,0},{16,24},{24,16},{1,9},{9,1},{17,25},{25,17},{2,10},{10... | collective-permute-start | bytes 983048 | tf_op jit(solution)/shard_map/ppermute | solution.py:29
  609.9 31.6 %collective-permute-start.59 = (bf16[256,640]{1,0:T(8,128)(2,1)}, bf16[256,640]{1,0:T(8,128)(2,1)}, u32[]{:S(2)}, u32[]{:S(2)}) collective-permute-start(bf16[256,640]{1,0:T(8,128)(2,1)} %slice.525), channel_id=1, source_target_pairs={{0,2},{2,0},{1,3},{3,1},{4,6},{6,4},{5,7},{7,5},{8,10},{10,8},{9,1... | collective-permute-start | bytes 983048 | tf_op jit(solution)/shard_map/ppermute | solution.py:29
  667.7 67.5 %collective-permute-start.97 = (bf16[256,2048]{1,0:T(8,128)(2,1)S(1)}, bf16[256,2048]{1,0:T(8,128)(2,1)S(1)}, u32[]{:S(2)}, u32[]{:S(2)}) collective-permute-start(bf16[256,2048]{1,0:T(8,128)(2,1)S(1)} %get-tuple-element.79), channel_id=1, source_target_pairs={{0,1},{1,0},{2,3},{3,2},{4,5},{5,4},{6,7},{7,6},{8,9},{9,8},{10,11... | collective-permute-start | bytes 3145736 | tf_op jit(solution)/shard_map/ppermute | solution.py:29
  667.7 95.8 %collective-permute-start.96 = (bf16[256,2048]{1,0:T(8,128)(2,1)S(1)}, bf16[256,2048]{1,0:T(8,128)(2,1)}, u32[]{:S(2)}, u32[]{:S(2)}) collective-permute-start(bf16[256,2048]{1,0:T(8,128)(2,1)S(1)} %get-tuple-element.78), channel_id=1, source_target_pairs={{0,1},{1,0},{2,3},{3,2},{4,5},{5,4},{6,7},{7,6},{8,9},{9,8},{10,11... | collective-permute-start | bytes 3145736 | tf_op jit(solution)/shard_map/ppermute | solution.py:29
  695.1 31.8 %collective-permute-start.62 = (bf16[256,2048]{1,0:T(8,128)(2,1)S(1)}, bf16[256,2048]{1,0:T(8,128)(2,1)S(1)}, u32[]{:S(2)}, u32[]{:S(2)}) collective-permute-start(bf16[256,2048]{1,0:T(8,128)(2,1)S(1)} %add_convert_fusion.3), channel_id=1, source_target_pairs={{0,2},{2,0},{1,3},{3,1},{4,6},{6,4},{5,7},{7,5},{8,10},{10,8},{9,1... | collective-permute-start | bytes 3145736 | tf_op jit(solution)/shard_map/ppermute | solution.py:29
  696.1 30.8 %collective-permute-start.65 = (bf16[256,2048]{1,0:T(8,128)(2,1)S(1)}, bf16[256,2048]{1,0:T(8,128)(2,1)S(1)}, u32[]{:S(2)}, u32[]{:S(2)}) collective-permute-start(bf16[256,2048]{1,0:T(8,128)(2,1)S(1)} %add_convert_fusion.2), channel_id=1, source_target_pairs={{0,16},{8,24},{16,0},{24,8},{1,17},{9,25},{17,1},{25,9},{2,18},{10... | collective-permute-start | bytes 3145736 | tf_op jit(solution)/shard_map/ppermute | solution.py:29
  698.4 28.5 %collective-permute-start.68 = (bf16[256,2048]{1,0:T(8,128)(2,1)S(1)}, bf16[256,2048]{1,0:T(8,128)(2,1)S(1)}, u32[]{:S(2)}, u32[]{:S(2)}) collective-permute-start(bf16[256,2048]{1,0:T(8,128)(2,1)S(1)} %add_convert_fusion.1), channel_id=1, source_target_pairs={{0,8},{8,0},{16,24},{24,16},{1,9},{9,1},{17,25},{25,17},{2,10},{10... | collective-permute-start | bytes 3145736 | tf_op jit(solution)/shard_map/ppermute | solution.py:29
  733.4 28.3 %collective-permute-start.69 = (bf16[256,2048]{1,0:T(8,128)(2,1)}, bf16[256,2048]{1,0:T(8,128)(2,1)}, u32[]{:S(2)}, u32[]{:S(2)}) collective-permute-start(bf16[256,2048]{1,0:T(8,128)(2,1)} %get-tuple-element.82), channel_id=1, source_target_pairs={{0,8},{8,0},{16,24},{24,16},{1,9},{9,1},{17,25},{25,17},{2,10},{10... | collective-permute-start | bytes 3145736 | tf_op jit(solution)/shard_map/ppermute | solution.py:29
  736.5 94.4 %collective-permute-start.98 = (bf16[256,2048]{1,0:T(8,128)(2,1)}, bf16[256,2048]{1,0:T(8,128)(2,1)}, u32[]{:S(2)}, u32[]{:S(2)}) collective-permute-start(bf16[256,2048]{1,0:T(8,128)(2,1)} %fusion.10), channel_id=1, source_target_pairs={{0,4},{4,0},{1,5},{5,1},{2,6},{6,2},{3,7},{7,3},{8,12},{12,8},{9,1... | collective-permute-start | bytes 3145736 | tf_op jit(solution)/shard_map/ppermute | solution.py:29
  737.1 275.1 %collective-permute-start.93 = (bf16[4,2,64,2048]{3,2,1,0:T(8,128)(2,1)}, bf16[4,2,64,2048]{3,2,1,0:T(8,128)(2,1)}, u32[]{:S(2)}, u32[]{:S(2)}) collective-permute-start(bf16[4,2,64,2048]{3,2,1,0:T(8,128)(2,1)} %get-tuple-element.66), channel_id=1, source_target_pairs={{0,1},{1,0},{2,3},{3,2},{4,5},{5,4},{6,7},{7,6},{8,9},{9,8},{10,11... | collective-permute-start | bytes 6291464 | tf_op jit(solution)/shard_map/ppermute | solution.py:29
  757.5 255.3 %collective-permute-start.95 = (bf16[4,2,64,2048]{3,2,1,0:T(8,128)(2,1)}, bf16[4,2,64,2048]{3,2,1,0:T(8,128)(2,1)}, u32[]{:S(2)}, u32[]{:S(2)}) collective-permute-start(bf16[4,2,64,2048]{3,2,1,0:T(8,128)(2,1)} %fusion), channel_id=1, source_target_pairs={{0,4},{4,0},{1,5},{5,1},{2,6},{6,2},{3,7},{7,3},{8,12},{12,8},{9,1... | collective-permute-start | bytes 6291464 | tf_op jit(solution)/shard_map/ppermute | solution.py:29
  761.6 73.1 %collective-permute-start.71 = (bf16[256,1024]{1,0:T(8,128)(2,1)}, bf16[256,1024]{1,0:T(8,128)(2,1)}, u32[]{:S(2)}, u32[]{:S(2)}) collective-permute-start(bf16[256,1024]{1,0:T(8,128)(2,1)} %slice.535), channel_id=1, source_target_pairs={{0,8},{8,0},{16,24},{24,16},{1,9},{9,1},{17,25},{25,17},{2,10},{10... | collective-permute-start | bytes 1572872 | tf_op jit(solution)/shard_map/ppermute | solution.py:29
  763.5 71.2 %collective-permute-start.72 = (bf16[256,1024]{1,0:T(8,128)(2,1)}, bf16[256,1024]{1,0:T(8,128)(2,1)S(1)}, u32[]{:S(2)}, u32[]{:S(2)}) collective-permute-start(bf16[256,1024]{1,0:T(8,128)(2,1)} %slice.536), channel_id=1, source_target_pairs={{0,16},{8,24},{16,0},{24,8},{1,17},{9,25},{17,1},{25,9},{2,18},{10... | collective-permute-start | bytes 1572872 | tf_op jit(solution)/shard_map/ppermute | solution.py:29
  880.1 38.3 %collective-permute-start.73 = (f32[4,2,256]{2,0,1:T(4,128)S(1)}, f32[4,2,256]{2,0,1:T(4,128)S(1)}, u32[]{:S(2)}, u32[]{:S(2)}) collective-permute-start(f32[4,2,256]{2,0,1:T(4,128)S(1)} %maximum_bitcast_fusion.3), channel_id=1, source_target_pairs={{0,8},{8,0},{16,24},{24,16},{1,9},{9,1},{17,25},{25,17},{2,10},{10... | collective-permute-start | bytes 24584 | tf_op jit(solution)/shard_map/ppermute | solution.py:29
  969.4 35.5 %collective-permute-start.81 = (bf16[4,64,1536]{2,1,0:T(8,128)(2,1)S(1)}, bf16[4,64,1536]{2,1,0:T(8,128)(2,1)S(1)}, u32[]{:S(2)}, u32[]{:S(2)}) collective-permute-start(bf16[4,64,1536]{2,1,0:T(8,128)(2,1)S(1)} %get-tuple-element.72), channel_id=1, source_target_pairs={{0,2},{2,0},{1,3},{3,1},{4,6},{6,4},{5,7},{7,5},{8,10},{10,8},{9,1... | collective-permute-start | bytes 2359304 | tf_op jit(solution)/shard_map/ppermute | solution.py:29
  971.2 36.1 %collective-permute-start.85 = (bf16[4,64,1536]{2,1,0:T(8,128)(2,1)S(1)}, bf16[4,64,1536]{2,1,0:T(8,128)(2,1)S(1)}, u32[]{:S(2)}, u32[]{:S(2)}) collective-permute-start(bf16[4,64,1536]{2,1,0:T(8,128)(2,1)S(1)} %get-tuple-element.73), channel_id=1, source_target_pairs={{0,4},{4,0},{1,5},{5,1},{2,6},{6,2},{3,7},{7,3},{8,12},{12,8},{9,1... | collective-permute-start | bytes 2359304 | tf_op jit(solution)/shard_map/ppermute | solution.py:29
  975.1 44.9 %collective-permute-start.87 = (bf16[64,2048]{1,0:T(8,128)(2,1)}, bf16[64,2048]{1,0:T(8,128)(2,1)S(1)}, u32[]{:S(2)}, u32[]{:S(2)}) collective-permute-start(bf16[64,2048]{1,0:T(8,128)(2,1)} %get-tuple-element.87), channel_id=1, source_target_pairs={{0,1},{1,0},{2,3},{3,2},{4,5},{5,4},{6,7},{7,6},{8,9},{9,8},{10,11... | collective-permute-start | bytes 786440 | tf_op jit(solution)/shard_map/ppermute | solution.py:29
  1007.4 28.6 %collective-permute-start.89 = (bf16[64,2048]{1,0:T(8,128)(2,1)}, bf16[64,2048]{1,0:T(8,128)(2,1)}, u32[]{:S(2)}, u32[]{:S(2)}) collective-permute-start(bf16[64,2048]{1,0:T(8,128)(2,1)} %get-tuple-element.86), channel_id=1, source_target_pairs={{0,1},{1,0},{2,3},{3,2},{4,5},{5,4},{6,7},{7,6},{8,9},{9,8},{10,11... | collective-permute-start | bytes 786440 | tf_op jit(solution)/shard_map/ppermute | solution.py:29
  1012.2 60.4 %collective-permute-start.86 = (bf16[64,2048]{1,0:T(8,128)(2,1)}, bf16[64,2048]{1,0:T(8,128)(2,1)}, u32[]{:S(2)}, u32[]{:S(2)}) collective-permute-start(bf16[64,2048]{1,0:T(8,128)(2,1)} %get-tuple-element.84), channel_id=1, source_target_pairs={{0,1},{1,0},{2,3},{3,2},{4,5},{5,4},{6,7},{7,6},{8,9},{9,8},{10,11... | collective-permute-start | bytes 786440 | tf_op jit(solution)/shard_map/ppermute | solution.py:29
  1024.4 73.3 %all-to-all-start.3 = ((bf16[8,64,2048]{2,1,0:T(8,128)(2,1)}), bf16[8,64,2048]{2,1,0:T(8,128)(2,1)}, u32[]{:S(2)}, u32[]{:S(2)}) async-start(bf16[8,64,2048]{2,1,0:T(8,128)(2,1)} %bitcast.90), calls=%async_computation.3 | async-start | bytes 4194304 | tf_op jit(solution)/shard_map/all_to_all | solution.py:418
  1033.9 31.5 %collective-permute-start.77 = (bf16[256,1024]{1,0:T(8,128)(2,1)S(1)}, bf16[256,1024]{1,0:T(8,128)(2,1)S(1)}, u32[]{:S(2)}, u32[]{:S(2)}) collective-permute-start(bf16[256,1024]{1,0:T(8,128)(2,1)S(1)} %get-tuple-element.120), channel_id=1, source_target_pairs={{0,16},{8,24},{16,0},{24,8},{1,17},{9,25},{17,1},{25,9},{2,18},{10... | collective-permute-start | bytes 1572872 | tf_op jit(solution)/shard_map/ppermute | solution.py:29
  1036.0 36.7 %collective-permute-start.88 = (bf16[64,2048]{1,0:T(8,128)(2,1)S(1)}, bf16[64,2048]{1,0:T(8,128)(2,1)S(1)}, u32[]{:S(2)}, u32[]{:S(2)}) collective-permute-start(bf16[64,2048]{1,0:T(8,128)(2,1)S(1)} %copy-done.48), channel_id=1, source_target_pairs={{0,2},{2,0},{1,3},{3,1},{4,6},{6,4},{5,7},{7,5},{8,10},{10,8},{9,1... | collective-permute-start | bytes 786440 | tf_op jit(solution)/shard_map/ppermute | solution.py:29
  1038.7 33.9 %collective-permute-start.92 = (bf16[64,2048]{1,0:T(8,128)(2,1)S(1)}, bf16[64,2048]{1,0:T(8,128)(2,1)S(1)}, u32[]{:S(2)}, u32[]{:S(2)}) collective-permute-start(bf16[64,2048]{1,0:T(8,128)(2,1)S(1)} %add_convert_fusion.21), channel_id=1, source_target_pairs={{0,4},{4,0},{1,5},{5,1},{2,6},{6,2},{3,7},{7,3},{8,12},{12,8},{9,1... | collective-permute-start | bytes 786440 | tf_op jit(solution)/shard_map/ppermute | solution.py:29
  1039.8 47.2 %collective-permute-start.76 = (bf16[256,2048]{1,0:T(8,128)(2,1)S(1)}, bf16[256,2048]{1,0:T(8,128)(2,1)S(1)}, u32[]{:S(2)}, u32[]{:S(2)}) collective-permute-start(bf16[256,2048]{1,0:T(8,128)(2,1)S(1)} %pad_maximum_fusion.18), channel_id=1, source_target_pairs={{0,16},{8,24},{16,0},{24,8},{1,17},{9,25},{17,1},{25,9},{2,18},{10... | collective-permute-start | bytes 3145736 | tf_op jit(solution)/shard_map/ppermute | solution.py:29
  (156 other events, 2350.1 us)

commit v2 on v1

v2 whole, which is shorter than its diff:
```python
import functools
import math

import jax
import jax.numpy as jnp
from jax import lax
from jax.experimental import pallas as pl
from jax.experimental.pallas import tpu as pltpu
from jax.sharding import Mesh
from jax.sharding import PartitionSpec as P

HEADS = 16

rope_base = 500000.0
norm_eps = 1e-06
masked_score = -1e30

bf16 = jnp.bfloat16
f32 = jnp.float32


def dims_of(axis):
    count = lax.axis_size(axis)
    return [(axis, 1 << bit) for bit in range(count.bit_length() - 1)]


def swap(block, dim):
    axis, mask = dim
    return lax.ppermute(block, axis, [(i, i ^ mask) for i in range(lax.axis_size(axis))])


def partner_index(dims, which):
    masks = {}
    for bit, (axis, mask) in enumerate(dims):
        if which >> bit & 1:
            masks[axis] = masks.get(axis, 0) | mask
    return masks


def column_cuts(width, count):
    tiles = width // 128
    return [round(tiles * i / count) * 128 for i in range(count + 1)]


def column_parts(block, count):
    cuts = column_cuts(block.shape[1], count)
    return [block[:, cuts[i] : cuts[i + 1]] for i in range(count)]


def route(which, count):
    bits = [i for i in range(count) if which >> i & 1]
    if len(bits) == 1:
        return bits[0]
    return bits[0] if bits[1] - bits[0] == 1 else bits[1]


def by_size(count):
    return sorted(range(1, 1 << count), key=lambda m: bin(m).count("1"))


class Spread:
    def __init__(self, block, dims, spare_last=False):
        self.dims, self.size, self.pieces, self.new = dims, 0, {0: block}, [0]
        self.spare_last = spare_last and len(dims) == 3

    def light_step(self):
        x, y, _ = self.dims
        half = lambda m, i: column_parts(self.pieces[m], 2)[i]
        if self.size == 2:
            self.new = [3]
            self.pieces[3] = jnp.concatenate([swap(half(2, 0), x), swap(half(1, 1), y)], axis=1)
        elif self.size == 3:
            self.new = [5, 6]
            self.pieces[5], self.pieces[6] = swap(self.pieces[4], x), swap(self.pieces[4], y)
        else:
            self.new = [7]
            self.pieces[7] = jnp.concatenate([swap(half(6, 0), x), swap(half(5, 1), y)], axis=1)

    def step(self):
        self.size += 1
        count = len(self.dims)
        if self.spare_last and self.size > 1:
            self.light_step()
            return self
        self.new = [m for m in by_size(count) if bin(m).count("1") == self.size]
        for which in self.new:
            if self.size == count and count > 1:
                parts = [
                    swap(column_parts(self.pieces[which ^ (1 << i)], count)[i], self.dims[i])
                    for i in range(count)
                ]
                self.pieces[which] = jnp.concatenate(parts, axis=1)
            else:
                via = route(which, count)
                self.pieces[which] = swap(self.pieces[which ^ (1 << via)], self.dims[via])
        return self

    def fresh(self):
        return [self.pieces[m] for m in self.new]

    def renew(self, values):
        self.pieces.update(zip(self.new, values, strict=True))

    def whole(self):
        while self.size < len(self.dims):
            self.step()
        return [self.pieces[m] for m in range(1 << len(self.dims))]


class Collect:
    def __init__(self, pieces, dims):
        self.dims, self.size, self.pieces = dims, len(dims), list(pieces)
        self.got, self.new = {m: [] for m in range(len(self.pieces))}, []

    def step(self):
        count = len(self.dims)
        self.new = []
        for which in by_size(count):
            if bin(which).count("1") != self.size:
                continue
            total = self.total(which)
            if self.size == count and count > 1:
                for i, cols in enumerate(column_parts(total, count)):
                    self.keep(which ^ (1 << i), i, swap(cols, self.dims[i]))
            else:
                via = route(which, count)
                self.keep(which ^ (1 << via), None, swap(total, self.dims[via]))
        self.size -= 1
        return self

    def keep(self, which, part, arrived):
        self.new.append((which, len(self.got[which])))
        self.got[which].append((part, arrived))

    def total(self, which):
        if not self.got[which]:
            return self.pieces[which]
        count = len(self.dims)
        total = self.pieces[which].astype(f32)
        for part, arrived in self.got[which]:
            if part is None:
                total = total + arrived.astype(f32)
            else:
                cols = column_parts(total, count)
                cols[part] = cols[part] + arrived.astype(f32)
                total = jnp.concatenate(cols, axis=1)
        return total.astype(bf16)

    def fresh(self):
        return [self.got[which][i][1] for which, i in self.new]

    def renew(self, values):
        for (which, i), value in zip(self.new, values, strict=True):
            self.got[which][i] = (self.got[which][i][0], value)

    def whole(self):
        while self.size > 0:
            self.step()
        total = self.pieces[0].astype(f32)
        for _, arrived in self.got[0]:
            total = total + arrived.astype(f32)
        return total


def tie(*items):
    steps = (Spread, Collect)
    values = [item.fresh() if isinstance(item, steps) else item for item in items]
    values = lax.optimization_barrier(values)
    rest = []
    for item, value in zip(items, values, strict=True):
        if isinstance(item, steps):
            item.renew(value)
        else:
            rest.append(value)
    return rest


def sum_all(table, dims):
    for bit, dim in enumerate(dims):
        there = swap(table, dim)
        order = [m ^ (1 << bit) for m in range(table.shape[0])]
        table = table + jnp.stack([there[m] for m in order])
    return table


def after(block, *earlier):
    return lax.optimization_barrier((block, earlier))[0]


def block_starts(blocks, rows, dims, axes, order):
    starts = []
    for m in range(1 << len(dims)):
        masks = partner_index(dims, m)
        at = [lax.axis_index(a) ^ masks.get(a, 0) for a in axes]
        starts += [order(block, *at) * rows for block in range(blocks)]
    return jnp.stack(starts).astype(jnp.int32)


def project(x_pieces, w_pieces, starts, out_starts, tok, part):
    n_x, n_w = len(x_pieces), len(w_pieces)
    width = x_pieces[0].shape[1]
    blocks, rows, _ = w_pieces[0].shape
    length = n_x * tok
    number = n_w * blocks

    def kernel(table, out_table, *refs):
        xs, ws = refs[:n_x], refs[n_x : n_x + n_w]
        raw, squares, x_out, w_out, o_out, x_all, w_all, o_all, sems = refs[n_x + n_w :]
        at = pl.program_id(0)
        arrive, later = [], []
        for i in range(n_x):
            source, target = xs[i].at[pl.ds(0, tok)], x_all.at[pl.ds(i * tok, tok)]
            arrive.append(pltpu.make_async_copy(source, target, sems.at[i]))
        for i in range(number):
            piece, block = ws[i // blocks], i % blocks
            here = pl.ds(pl.multiple_of(table[i], rows), rows)
            source = piece.at[block, :, pl.ds(0, 3 * part)]
            arrive.append(pltpu.make_async_copy(source, w_all.at[here], sems.at[n_x + i]))
            here = pl.ds(pl.multiple_of(out_table[i // blocks], rows), rows)
            source = piece.at[block, :, pl.ds(3 * part, part)]
            target = o_all.at[here, pl.ds(block * part, part)]
            later.append(pltpu.make_async_copy(source, target, sems.at[n_x + number + i]))
        sem = n_x + 2 * number
        keep = [
            pltpu.make_async_copy(x_all, x_out, sems.at[sem]),
            pltpu.make_async_copy(w_all, w_out, sems.at[sem + 1]),
        ]
        keep_out = pltpu.make_async_copy(o_all, o_out, sems.at[sem + 2])

        @pl.when(at == 0)
        def _():
            for copy in arrive + later:
                copy.start()
            for copy in arrive:
                copy.wait()
            for copy in keep:
                copy.start()

        for step in range(3):

            @pl.when(at == step)
            def _(step=step):
                product = dot(x_all[...], w_all[:, step * part : (step + 1) * part])
                raw[...] = product
                if step < 2:
                    squares[0] = jnp.sum(product * product, axis=-1, keepdims=True)
                if step == 0:
                    for copy in later:
                        copy.wait()
                    keep_out.start()

        @pl.when(at == 2)
        def _():
            for copy in keep + [keep_out]:
                copy.wait()

    somewhere = pl.BlockSpec(memory_space=pl.ANY)
    scalars = pl.BlockSpec(memory_space=pltpu.SMEM)
    return pl.pallas_call(
        kernel,
        grid=(3,),
        in_specs=[scalars] * 2 + [somewhere] * (n_x + n_w),
        out_specs=[
            pl.BlockSpec((length, part), lambda j: (0, j)),
            pl.BlockSpec((1, length, 1), lambda j: (jnp.minimum(j, 1), 0, 0)),
            somewhere,
            somewhere,
            somewhere,
        ],
        out_shape=[
            jax.ShapeDtypeStruct((length, 3 * part), f32),
            jax.ShapeDtypeStruct((2, length, 1), f32),
            jax.ShapeDtypeStruct((length, width), bf16),
            jax.ShapeDtypeStruct((width, 3 * part), bf16),
            jax.ShapeDtypeStruct((n_w * rows, blocks * part), bf16),
        ],
        scratch_shapes=[
            pltpu.VMEM((length, width), bf16),
            pltpu.VMEM((width, 3 * part), bf16),
            pltpu.VMEM((n_w * rows, blocks * part), bf16),
            pltpu.SemaphoreType.DMA((n_x + 2 * number + 3,)),
        ],
        compiler_params=pltpu.CompilerParams(vmem_limit_bytes=40 * 1024 * 1024),
        cost_estimate=pl.CostEstimate(
            flops=6 * length * width * part, bytes_accessed=20 * length * part, transcendentals=0
        ),
        name="project",
    )(starts, out_starts, *x_pieces, *w_pieces)


def regroup(blocks, order):
    number, rows, width = blocks.shape

    def kernel(ref, out, sems):
        copies = [
            pltpu.make_async_copy(ref.at[at], out.at[pl.ds(i * rows, rows)], sems.at[i])
            for i, at in enumerate(order)
        ]
        for copy in copies:
            copy.start()
        for copy in copies:
            copy.wait()

    return pl.pallas_call(
        kernel,
        in_specs=[pl.BlockSpec(memory_space=pltpu.HBM)],
        out_specs=pl.BlockSpec(memory_space=pltpu.VMEM),
        out_shape=jax.ShapeDtypeStruct((number * rows, width), blocks.dtype),
        scratch_shapes=[pltpu.SemaphoreType.DMA((number,))],
        compiler_params=pltpu.CompilerParams(vmem_limit_bytes=24 * 1024 * 1024),
        name="regroup",
    )(blocks)


def take_blocks(whole, dims, axes):
    shape = whole.shape[len(axes) :]
    pieces = []
    for m in range(1 << len(dims)):
        masks = partner_index(dims, m)
        at = tuple(lax.axis_index(a) ^ masks.get(a, 0) for a in axes)
        piece = lax.dynamic_slice(whole, at + (0,) * len(shape), (1,) * len(axes) + shape)
        pieces.append(piece.reshape(shape))
    return pieces


def add_low(kept, arrived):
    return (kept.astype(f32) + arrived.astype(f32)).astype(bf16)


def gather_row(row, dims):
    for axis, mask in dims:
        there = swap(row, (axis, mask))
        low = (lax.axis_index(axis) & mask) == 0
        row = jnp.concatenate([jnp.where(low, row, there), jnp.where(low, there, row)], axis=0)
    return row


def turned(raw, inverse, gain, cosine, sine):
    scaled = raw * inverse * gain
    return scaled * cosine + pltpu.roll(scaled, scaled.shape[1] // 2, 1) * sine


def turned_back(grad, raw, inverse, gain, cosine, sine):
    back = grad * cosine - pltpu.roll(grad, grad.shape[1] // 2, 1) * sine
    product = back * (raw * inverse)
    return back * gain, jnp.sum(product * gain, -1, keepdims=True), jnp.sum(product, 0, keepdims=True)


def block_scores(scale, last, a, j, q, k, row_ids, col_ids):
    scores = dot_t(q, k) * scale
    allowed = None
    if j == 0 or a == last:
        allowed = row_ids == col_ids
    if j == a:
        shape = scores.shape
        causal = lax.broadcasted_iota(jnp.int32, shape, 0) >= lax.broadcasted_iota(jnp.int32, shape, 1)
        allowed = causal if allowed is None else allowed & causal
    return scores if allowed is None else jnp.where(allowed, scores, masked_score)


def forward_kernel(
    scale, count, tok, place, q_raw, k_raw, v_raw, q_inv, k_inv, q_gain, k_gain, cosine, sine,
    row_ids, col_ids, out, low, log_total, k_all, v_all,
):
    rows = lambda j: pl.ds(pl.multiple_of((place[0] ^ j) * tok, tok), tok)
    cols = lambda j: slice(j * tok, (j + 1) * tok)
    for a in range(count):
        here = rows(a)
        table = (cosine[cols(a), :], sine[cols(a), :])
        k_all[cols(a), :] = turned(k_raw[here, :], k_inv[0, here, :], k_gain[...], *table).astype(bf16)
        v_all[cols(a), :] = v_raw[here, :].astype(bf16)
        q = turned(q_raw[here, :], q_inv[0, here, :], q_gain[...], *table).astype(bf16)
        scores = [
            block_scores(scale, count - 1, a, j, q, k_all[cols(j), :], row_ids[here, :], col_ids[j])
            for j in range(a + 1)
        ]
        top = jnp.max(functools.reduce(jnp.maximum, scores), axis=-1, keepdims=True)
        expo = [jnp.exp2(block - top) for block in scores]
        total = jnp.sum(functools.reduce(jnp.add, expo), axis=-1, keepdims=True)
        parts = [dot(expo[j].astype(bf16), v_all[cols(j), :]) for j in range(a + 1)]
        attended = functools.reduce(jnp.add, parts) * (1.0 / total)
        out[here, :] = attended
        low[here, :] = attended.astype(bf16)
        log_total[0, here, :] = top + jnp.log2(total)


def backward_kernel(
    scale, plain_scale, count, tok, place, q_raw, k_raw, v_raw, q_inv, k_inv, q_gain, k_gain,
    cosine, sine, row_ids, col_ids, d_out, out, log_total,
    e_q, e_k, d_v, q_sum, k_sum, q_gain_grad, k_gain_grad, k_all, v_all, d_k_all, d_v_all,
):
    rows = lambda j: pl.ds(pl.multiple_of((place[0] ^ j) * tok, tok), tok)
    cols = lambda j: slice(j * tok, (j + 1) * tok)
    q_gain_grad[...] = jnp.zeros_like(q_gain_grad)

    @pl.when(pl.program_id(0) == 0)
    def _():
        q_sum[...] = jnp.zeros_like(q_sum)
        k_sum[...] = jnp.zeros_like(k_sum)

    for a in range(count):
        here = rows(a)
        table = (cosine[cols(a), :], sine[cols(a), :])
        k_all[cols(a), :] = turned(k_raw[here, :], k_inv[0, here, :], k_gain[...], *table).astype(bf16)
        v_all[cols(a), :] = v_raw[here, :].astype(bf16)
        q_row, inverse = q_raw[here, :], q_inv[0, here, :]
        q = turned(q_row, inverse, q_gain[...], *table).astype(bf16)
        d_blk = d_out[here, :]
        row_dot = jnp.sum(d_blk.astype(f32) * out[here, :], axis=-1, keepdims=True)
        d_q = []
        for j in range(a + 1):
            k = k_all[cols(j), :]
            scores = block_scores(scale, count - 1, a, j, q, k, row_ids[here, :], col_ids[j])
            probability = jnp.exp2(scores - log_total[0, here, :])
            d_prob = dot_t(d_blk, v_all[cols(j), :])
            d_scores = (probability * (d_prob - row_dot)).astype(bf16)
            d_q.append(dot(d_scores, k))
            d_k = t_dot(d_scores, q)
            d_v_part = t_dot(probability.astype(bf16), d_blk)
            if j == a:
                d_k_all[cols(j), :] = d_k
                d_v_all[cols(j), :] = d_v_part
            else:
                d_k_all[cols(j), :] += d_k
                d_v_all[cols(j), :] += d_v_part
        e_q[here, :], row_sum, gain_grad = turned_back(
            functools.reduce(jnp.add, d_q) * plain_scale, q_row, inverse, q_gain[...], *table
        )
        q_sum[0, here, :] += row_sum
        q_gain_grad[...] += gain_grad
    k_gain_grad[...] = jnp.zeros_like(k_gain_grad)
    for j in range(count):
        here = rows(j)
        e_k[here, :], row_sum, gain_grad = turned_back(
            d_k_all[cols(j), :] * plain_scale, k_raw[here, :], k_inv[0, here, :],
            k_gain[...], cosine[cols(j), :], sine[cols(j), :],
        )
        k_sum[0, here, :] += row_sum
        k_gain_grad[...] += gain_grad
        d_v[here, :] = d_v_all[cols(j), :].astype(bf16)


def attention_specs(tokens, block, heads, head_dim):
    head = lambda i: pl.BlockSpec((tokens, head_dim), lambda h, s: (0, i * heads + h))
    whole = lambda shape: pl.BlockSpec(shape, lambda h, s: (0,) * len(shape))
    vector = pl.BlockSpec((1, head_dim), lambda h, s: (0, h))
    inverse = lambda i: pl.BlockSpec((1, tokens, 1), lambda h, s: (i, 0, 0))
    inputs = [head(0), head(1), head(2), inverse(0), inverse(1), vector, vector]
    inputs += [whole((tokens, head_dim))] * 2
    inputs += [whole((tokens, 1)), whole((tokens // block, 1, block))]
    logs = pl.BlockSpec((1, tokens, 1), lambda h, s: (h, 0, 0))
    return inputs, head(0), logs, vector


def attend(context, heads, block):
    place, raw, inverse, gains, tables, ids = context
    tokens, width = raw.shape[0], raw.shape[1] // 3
    head_dim = width // heads
    inputs, head, logs, _ = attention_specs(tokens, block, heads, head_dim)
    return pl.pallas_call(
        functools.partial(forward_kernel, head_dim**-0.5 * math.log2(math.e), tokens // block, block),
        grid_spec=pltpu.PrefetchScalarGridSpec(
            num_scalar_prefetch=1,
            grid=(heads,),
            in_specs=inputs,
            out_specs=[head, head, logs],
            scratch_shapes=[pltpu.VMEM((tokens, head_dim), bf16)] * 2,
        ),
        out_shape=[
            jax.ShapeDtypeStruct((tokens, width), f32),
            jax.ShapeDtypeStruct((tokens, width), bf16),
            jax.ShapeDtypeStruct((heads, tokens, 1), f32),
        ],
        compiler_params=pltpu.CompilerParams(vmem_limit_bytes=40 * 1024 * 1024),
        cost_estimate=pl.CostEstimate(
            flops=2 * tokens * tokens * width,
            bytes_accessed=18 * tokens * width,
            transcendentals=heads * tokens * tokens // 2,
        ),
        name="attend",
    )(place, raw, raw, raw, inverse, inverse, *gains, *tables, *ids)


def attend_back(context, d_out, out, log_total, heads, block):
    place, raw, inverse, gains, tables, ids = context
    tokens, width = raw.shape[0], raw.shape[1] // 3
    head_dim = width // heads
    inputs, head, logs, vector = attention_specs(tokens, block, heads, head_dim)
    sums = pl.BlockSpec((1, tokens, 1), lambda h, s: (0, 0, 0))
    scale = head_dim**-0.5
    return pl.pallas_call(
        functools.partial(
            backward_kernel, scale * math.log2(math.e), scale, tokens // block, block
        ),
        grid_spec=pltpu.PrefetchScalarGridSpec(
            num_scalar_prefetch=1,
            grid=(heads,),
            in_specs=inputs + [head, head, logs],
            out_specs=[head, head, head, sums, sums, vector, vector],
            scratch_shapes=[pltpu.VMEM((tokens, head_dim), bf16)] * 2
            + [pltpu.VMEM((tokens, head_dim), f32)] * 2,
        ),
        out_shape=[
            jax.ShapeDtypeStruct((tokens, width), f32),
            jax.ShapeDtypeStruct((tokens, width), f32),
            jax.ShapeDtypeStruct((tokens, width), bf16),
        ]
        + [jax.ShapeDtypeStruct((1, tokens, 1), f32)] * 2
        + [jax.ShapeDtypeStruct((1, width), f32)] * 2,
        compiler_params=pltpu.CompilerParams(vmem_limit_bytes=40 * 1024 * 1024),
        cost_estimate=pl.CostEstimate(
            flops=5 * tokens * tokens * width,
            bytes_accessed=30 * tokens * width,
            transcendentals=heads * tokens * tokens // 2,
        ),
        name="attend_back",
    )(place, raw, raw, raw, inverse, inverse, *gains, *tables, *ids, d_out, out, log_total)


def sigmoid(values):
    return 1.0 / (1.0 + jnp.exp(-values))


def feed_kernel(with_down, masks, tok, steps, refs):
    number = len(masks)
    pieces, refs = refs[:number], refs[number:]
    down = refs[2] if with_down else None
    w_gate, w_up, refs = refs[0], refs[1], refs[2 + with_down :]
    h_all, middle_all, refs = refs[0], refs[1], refs[2:]
    gates, ups, refs = refs[:number], refs[number : 2 * number], refs[2 * number :]
    partials, refs = refs[: len(refs) - 3 - with_down], refs[len(refs) - 3 - with_down :]
    held_h, held_middle, sems = refs[0], refs[1], refs[-1]
    held_down = refs[2] if with_down else None
    at = pl.program_id(0)
    part = gates[0].shape[1]
    block = lambda i: pl.ds(i * tok, tok)
    copies = lambda held, whole, first: [
        pltpu.make_async_copy(held.at[block(i)], whole.at[block(m)], sems.at[first + i])
        for i, m in enumerate(masks)
    ]
    arrive = [
        pltpu.make_async_copy(pieces[i], held_h.at[block(i)], sems.at[i]) for i in range(number)
    ]
    keep_h, keep_middle = copies(held_h, h_all, number), copies(held_middle, middle_all, 2 * number)
    weights = [pltpu.make_async_copy(down, held_down, sems.at[3 * number])] if with_down else []

    @pl.when(at == 0)
    def _():
        for copy in arrive + weights:
            copy.start()
        for copy in arrive:
            copy.wait()
        for copy in keep_h:
            copy.start()

    gate_act = dot(held_h[...], w_gate[...])
    up_act = dot(held_h[...], w_up[...])
    middle = (gate_act * sigmoid(gate_act) * up_act).astype(bf16)
    for i in range(number):
        gates[i][...] = gate_act[i * tok : (i + 1) * tok].astype(bf16)
        ups[i][...] = up_act[i * tok : (i + 1) * tok].astype(bf16)
    for step in range(steps):

        @pl.when(at == step)
        def _(step=step):
            held_middle[:, step * part : (step + 1) * part] = middle

    @pl.when(at == steps - 1)
    def _():
        for copy in keep_middle:
            copy.start()
        for copy in weights:
            copy.wait()
        for i, out in enumerate(partials):
            out[...] = dot(held_middle[i * tok : (i + 1) * tok, :], held_down[...]).astype(bf16)
        for copy in keep_h + keep_middle:
            copy.wait()


def feed_back_kernel(masks, tok, steps, refs):
    number = len(masks)
    pieces, refs = refs[:number], refs[number:]
    gates, ups, refs = refs[:number], refs[number : 2 * number], refs[2 * number :]
    down, w_gu, d_ff_all, d_gate_all, d_up_all = refs[:5]
    partials, (held_d, held_gu, held_w, sems) = refs[5 : 5 + number], refs[5 + number :]
    at = pl.program_id(0)
    part = gates[0].shape[1]
    units = steps * part
    block = lambda i: pl.ds(i * tok, tok)
    arrive, keep_d, keep_gu = [], [], []
    for i, m in enumerate(masks):
        arrive.append(pltpu.make_async_copy(pieces[i], held_d.at[block(i)], sems.at[i]))
        keep_d.append(
            pltpu.make_async_copy(held_d.at[block(i)], d_ff_all.at[block(m)], sems.at[number + i])
        )
        for j, whole in enumerate((d_gate_all, d_up_all)):
            source = held_gu.at[block(i), pl.ds(j * units, units)]
            sem = sems.at[(2 + j) * number + i]
            keep_gu.append(pltpu.make_async_copy(source, whole.at[block(m)], sem))
    weights = pltpu.make_async_copy(w_gu, held_w, sems.at[4 * number])

    @pl.when(at == 0)
    def _():
        for copy in arrive:
            copy.start()
        weights.start()
        for copy in arrive:
            copy.wait()
        for copy in keep_d:
            copy.start()

    d_middle_all = dot_t(held_d[...], down[...])
    d_gates, d_ups = [], []
    for i in range(number):
        d_middle = d_middle_all[i * tok : (i + 1) * tok]
        gate_act, up_act = gates[i][...].astype(f32), ups[i][...].astype(f32)
        sig = sigmoid(gate_act)
        d_gates.append((d_middle * up_act * (sig * (1.0 + gate_act * (1.0 - sig)))).astype(bf16))
        d_ups.append((d_middle * (gate_act * sig)).astype(bf16))
    for step in range(steps):

        @pl.when(at == step)
        def _(step=step):
            for i in range(number):
                rows = slice(i * tok, (i + 1) * tok)
                held_gu[rows, step * part : (step + 1) * part] = d_gates[i]
                held_gu[rows, units + step * part : units + (step + 1) * part] = d_ups[i]

    @pl.when(at == steps - 1)
    def _():
        for copy in keep_gu:
            copy.start()
        weights.wait()
        for i in range(number):
            partials[i][...] = dot_t(held_gu[i * tok : (i + 1) * tok, :], held_w[...]).astype(bf16)
        for copy in keep_d + keep_gu:
            copy.wait()


def feed_call(kernel, name, pieces, masks, total, ins, in_specs, earlier, widths, blocks, held):
    number = len(pieces)
    tok, width = pieces[0].shape
    steps, part = blocks
    made, given, scratch = held
    somewhere = pl.BlockSpec(memory_space=pl.ANY)
    rows = number * tok
    first_alias = number + len(ins)

    def body(*refs):
        refs = refs[:first_alias] + refs[first_alias + len(earlier) :]
        kernel(masks, tok, steps, refs)

    return pl.pallas_call(
        body,
        grid=(steps,),
        in_specs=[somewhere] * number + in_specs + [somewhere] * len(earlier),
        out_specs=[somewhere] * len(widths)
        + [pl.BlockSpec((tok, part), lambda j: (0, j))] * made
        + [pl.BlockSpec((tok, width), lambda j: (0, 0))] * given,
        out_shape=[jax.ShapeDtypeStruct((total * tok, w), bf16) for w in widths]
        + [jax.ShapeDtypeStruct((tok, steps * part), bf16)] * made
        + [jax.ShapeDtypeStruct((tok, width), bf16)] * given,
        scratch_shapes=[pltpu.VMEM((rows, width), bf16)]
        + [pltpu.VMEM(shape, bf16) for shape in scratch]
        + [pltpu.SemaphoreType.DMA((4 * number + 1,))],
        input_output_aliases={first_alias + i: i for i in range(len(earlier))},
        compiler_params=pltpu.CompilerParams(vmem_limit_bytes=50 * 1024 * 1024),
        cost_estimate=pl.CostEstimate(
            flops=6 * rows * width * steps * part,
            bytes_accessed=6 * width * steps * part + 10 * rows * width,
            transcendentals=rows * steps * part,
        ),
        name=name,
    )(*pieces, *ins, *earlier)


def feed(pieces, masks, total, w_gu, down, earlier):
    width, units = w_gu.shape[0], w_gu.shape[1] // 2
    part = math.gcd(units, 256)
    steps = units // part
    number = len(pieces)
    rows = number * pieces[0].shape[0]
    specs = [
        pl.BlockSpec((width, part), lambda j: (0, j)),
        pl.BlockSpec((width, part), lambda j: (0, steps + j)),
    ]
    ins, scratch, given = [w_gu, w_gu], [(rows, units)], 0
    if down is not None:
        specs.append(pl.BlockSpec(memory_space=pl.ANY))
        ins, scratch, given = ins + [down], scratch + [(units, width)], number
    outs = feed_call(
        functools.partial(feed_kernel, int(down is not None)), "feed", pieces, masks, total, ins,
        specs, earlier, (width, units), (steps, part), (2 * number, given, scratch),
    )
    acts = list(zip(outs[2 : 2 + number], outs[2 + number : 2 + 2 * number], strict=True))
    return outs[:2], acts, outs[2 + 2 * number :]


def feed_down(middle_all, masks, tok, down):
    units, width = down.shape
    number = len(masks)

    def kernel(at, middle, weight, *outs):
        for i, out in enumerate(outs):

            @pl.when(pl.program_id(0) == i)
            def _(out=out):
                out[...] = dot(middle[...], weight[...]).astype(bf16)

    return pl.pallas_call(
        kernel,
        grid_spec=pltpu.PrefetchScalarGridSpec(
            num_scalar_prefetch=1,
            grid=(number,),
            in_specs=[
                pl.BlockSpec((tok, units), lambda i, at: (at[i], 0)),
                pl.BlockSpec((units, width), lambda i, at: (0, 0)),
            ],
            out_specs=[pl.BlockSpec((tok, width), lambda i, at: (0, 0))] * number,
        ),
        out_shape=[jax.ShapeDtypeStruct((tok, width), bf16)] * number,
        compiler_params=pltpu.CompilerParams(vmem_limit_bytes=40 * 1024 * 1024),
        cost_estimate=pl.CostEstimate(
            flops=2 * number * tok * units * width,
            bytes_accessed=4 * units * width,
            transcendentals=0,
        ),
        name="feed_down",
    )(jnp.array(masks, jnp.int32), middle_all, down)


def feed_back(pieces, masks, total, acts, w_gu, down, earlier):
    units, width = down.shape
    part = math.gcd(units, 256)
    steps = units // part
    number = len(pieces)
    tok = pieces[0].shape[0]
    rows = number * tok
    specs = [pl.BlockSpec((tok, part), lambda j: (0, j))] * (2 * number) + [
        pl.BlockSpec((part, width), lambda j: (j, 0)),
        pl.BlockSpec(memory_space=pl.ANY),
    ]
    ins = [gate for gate, _ in acts] + [up for _, up in acts] + [down, w_gu]
    outs = feed_call(
        feed_back_kernel, "feed_back", pieces, masks, total, ins, specs, earlier,
        (width, units, units), (steps, part), (0, number, [(rows, 2 * units), (width, 2 * units)]),
    )
    return outs[:3], outs[3:]


def owner_grad(h_all, d_act, sizes, rows, which, earlier):
    n_seq, n_hi, n_lo, n_core = sizes
    tokens, width = h_all.shape
    units = d_act.shape[1]
    cols = width // n_seq

    def kernel(h, d, *refs):
        product = t_dot(h[...], d[...]).astype(bf16)
        at = 0
        for hi in range(n_hi):
            for lo in range(n_lo):
                for core in range(n_core):
                    refs[-1][hi, core, 0, lo] = product[at : at + rows]
                    at += rows

    return pl.pallas_call(
        kernel,
        grid=(n_seq,),
        in_specs=[
            pl.BlockSpec((tokens, cols), lambda s: (0, s)),
            pl.BlockSpec((tokens, units), lambda s: (0, 0)),
        ]
        + [pl.BlockSpec(memory_space=pl.ANY)] * len(earlier),
        out_specs=pl.BlockSpec(
            (n_hi, n_core, 1, n_lo, rows, units), lambda s: (0, 0, s, 0, 0, which)
        ),
        out_shape=jax.ShapeDtypeStruct((n_hi, n_core, n_seq, n_lo, rows, 2 * units), bf16),
        input_output_aliases={2: 0} if earlier else {},
        compiler_params=pltpu.CompilerParams(vmem_limit_bytes=40 * 1024 * 1024),
        cost_estimate=pl.CostEstimate(
            flops=2 * tokens * width * units,
            bytes_accessed=2 * (tokens * width + tokens * units + width * units),
            transcendentals=0,
        ),
        name="owner_grad",
    )(h_all, d_act, *earlier)


def pack_columns(weights, count):
    rows, width = weights[0].shape
    part = width // count

    def kernel(*refs):
        for i, ref in enumerate(refs[:-1]):
            refs[-1][0, :, i * part : (i + 1) * part] = ref[...]

    return pl.pallas_call(
        kernel,
        grid=(count,),
        in_specs=[pl.BlockSpec((rows, part), lambda s: (0, s))] * len(weights),
        out_specs=pl.BlockSpec((1, rows, len(weights) * part), lambda s: (s, 0, 0)),
        out_shape=jax.ShapeDtypeStruct((count, rows, len(weights) * part), weights[0].dtype),
        name="pack_columns",
    )(*weights)


def unpack_columns(packed, number):
    count, rows, width = packed.shape
    part = width // number

    def kernel(ref, *outs):
        for i, out in enumerate(outs):
            out[...] = ref[0, :, i * part : (i + 1) * part].astype(f32)

    return pl.pallas_call(
        kernel,
        grid=(count,),
        in_specs=[pl.BlockSpec((1, rows, width), lambda s: (s, 0, 0))],
        out_specs=[pl.BlockSpec((rows, part), lambda s: (0, s))] * number,
        out_shape=[jax.ShapeDtypeStruct((rows, count * part), f32)] * number,
        name="unpack_columns",
    )(packed)


def unit_slices(sizes, unit):
    n_hi, n_lo, n_core = sizes
    return [
        (lo, (hi * n_core + core) * unit, ((hi * n_lo + lo) * n_core + core) * unit)
        for hi in range(n_hi)
        for lo in range(n_lo)
        for core in range(n_core)
    ]


def pack_units(gate, up, n_seq, sizes, unit):
    rows = gate.shape[0]
    n_hi, n_lo, n_core = sizes
    units = n_hi * n_core * unit

    def kernel(gate_ref, up_ref, out):
        for i, ref in enumerate((gate_ref, up_ref)):
            for lo, packed, plain in unit_slices(sizes, unit):
                start = i * units + packed
                out[lo, :, start : start + unit] = ref[:, plain : plain + unit]

    return pl.pallas_call(
        kernel,
        grid=(n_seq,),
        in_specs=[pl.BlockSpec((rows, units * n_lo), lambda s: (0, s))] * 2,
        out_specs=pl.BlockSpec((n_lo, rows, 2 * units), lambda s: (s, 0, 0)),
        out_shape=jax.ShapeDtypeStruct((n_seq * n_lo, rows, 2 * units), gate.dtype),
        name="pack_units",
    )(gate, up)


def unpack_units(packed, n_seq, sizes, unit):
    _, rows, width = packed.shape
    n_lo = sizes[1]
    units = width // 2

    def kernel(ref, *outs):
        for i, out in enumerate(outs):
            for lo, at, plain in unit_slices(sizes, unit):
                start = i * units + at
                out[:, plain : plain + unit] = ref[lo, :, start : start + unit].astype(f32)

    return pl.pallas_call(
        kernel,
        grid=(n_seq,),
        in_specs=[pl.BlockSpec((n_lo, rows, width), lambda s: (s, 0, 0))],
        out_specs=[pl.BlockSpec((rows, units * n_lo), lambda s: (0, s))] * 2,
        out_shape=[jax.ShapeDtypeStruct((rows, n_seq * n_lo * units), f32)] * 2,
        name="unpack_units",
    )(packed)


def finish_kernel(q_in, k_in, q_raw, k_raw, q_inv, k_inv, q_mean, k_mean, d_v, out):
    width = q_in.shape[1]
    for i, (grad, raw, inverse, mean) in enumerate(
        ((q_in, q_raw, q_inv, q_mean), (k_in, k_raw, k_inv, k_mean))
    ):
        normed = raw[...] * inverse[0]
        low = ((grad[...] - normed * mean[0]) * inverse[0]).astype(bf16)
        out[:, i * width : (i + 1) * width] = low
    out[:, 2 * width :] = d_v[...]


def row_specs(block, part):
    cols = lambda i: pl.BlockSpec((block, part), lambda b: (b, i))
    rows = lambda i: pl.BlockSpec((1, block, 1), lambda b: (i, b, 0))
    vector = pl.BlockSpec((1, part), lambda b: (0, 0))
    return cols, rows, vector


def finish(e_query, e_key, raw, inverse, means, d_value, part, block):
    length = raw.shape[0]
    cols, rows, _ = row_specs(block, part)
    return pl.pallas_call(
        finish_kernel,
        grid=(length // block,),
        in_specs=[cols(0), cols(0), cols(0), cols(1)] + [rows(0), rows(1)] * 2 + [cols(0)],
        out_specs=pl.BlockSpec((block, 3 * part), lambda b: (b, 0)),
        out_shape=jax.ShapeDtypeStruct((length, 3 * part), bf16),
        name="finish",
    )(e_query, e_key, raw, raw, inverse, inverse, means, means, d_value)


def dot(left, right):
    return jnp.dot(left, right, preferred_element_type=f32)


def dot_t(left, right):
    return lax.dot_general(left, right, (((1,), (1,)), ((), ())), preferred_element_type=f32)


def t_dot(left, right):
    return lax.dot_general(left, right, (((0,), (0,)), ((), ())), preferred_element_type=f32)


def held(block):
    return lax.optimization_barrier(block)


def rope_tables(positions, head_dim):
    half_dim = head_dim // 2
    frequency = rope_base ** (-(jnp.arange(half_dim, dtype=f32) * 2.0 / head_dim))
    angles = positions.astype(f32)[:, None] * frequency[None, :]
    cosine, sine = jnp.cos(angles), jnp.sin(angles)
    return jnp.concatenate([cosine, cosine], 1), jnp.concatenate([-sine, sine], 1)


def rms(values):
    inverse = lax.rsqrt(jnp.mean(values * values, axis=-1, keepdims=True) + norm_eps)
    return values * inverse, inverse


def rms_back(grad, normed, inverse, gain):
    scaled = grad * gain
    return (scaled - normed * jnp.mean(scaled * normed, axis=-1, keepdims=True)) * inverse


def per_device(
    tokens,
    segment_ids,
    w_query,
    w_key,
    w_value,
    w_out,
    w_gate,
    w_up,
    w_down,
    query_gain,
    key_gain,
    attn_gain,
    ff_gain,
    cotangent,
):
    inputs = tokens[0]
    tok, width = inputs.shape
    n_seq, n_hi, n_lo, n_core = (lax.axis_size(a) for a in ("seq", "zhi", "zlo", "core"))
    n_dev = n_seq * n_hi * n_lo * n_core
    seq = lax.axis_index("seq")
    heads = HEADS // n_seq
    head_dim = width // HEADS
    part = width // n_seq
    length = n_seq * tok
    d_rows = w_query.shape[0]
    ff_rows = w_down.shape[0]
    units = ff_rows * n_hi * n_core

    sizes = (n_hi, n_lo, n_core)
    seq_dims = dims_of("seq")
    lo_dims, hi_dims, core_dims = dims_of("zlo"), dims_of("zhi"), dims_of("core")
    cube_dims = seq_dims + lo_dims
    z_dims = lo_dims + hi_dims
    all_dims = core_dims + lo_dims + hi_dims + seq_dims
    z_axes = ("zhi", "zlo", "core")
    rows_of = lambda block, m: block[m * tok : (m + 1) * tok]

    pair_axes = ("zhi", "core")
    core_swap = lambda piece: swap(piece, core_dims[0])
    lo_order = [
        ((hi * n_core + core) * n_seq + s) * n_lo + lo
        for s in range(n_seq)
        for hi in range(n_hi)
        for lo in range(n_lo)
        for core in range(n_core)
    ]
    hi_order = [lo_order.index(i) for i in range(len(lo_order))]

    qkv_mine = pack_columns((w_query, w_key, w_value), n_seq)
    gains = jnp.stack([query_gain, key_gain, attn_gain, ff_gain])[None]
    gains = gather_row(after(gains, qkv_mine), core_dims + z_dims)
    gains = jnp.transpose(gains, (1, 0, 2)).reshape(1, 4 * part)
    qkv_mine = lax.all_to_all(qkv_mine, "seq", 0, 0, tiled=True).reshape(n_seq * d_rows, 3 * part)
    gu_mine = pack_units(w_gate, w_up, n_seq, sizes, ff_rows)
    qkv_mine, gains, gu_mine = tie(qkv_mine, gains, gu_mine)

    out_mine = jnp.concatenate([w_out[:, i * part : (i + 1) * part] for i in range(n_seq)], axis=0)
    w_z = Spread(jnp.concatenate([qkv_mine, out_mine], axis=1), z_dims).step()
    to_width = lambda row: jnp.pad(row, ((0, 0), (0, width - row.shape[1])))
    ids = to_width(segment_ids.astype(bf16))
    more = jnp.concatenate([ids, to_width(gains), jnp.zeros((14, width), bf16)], axis=0)
    x_spread = Spread(jnp.concatenate([inputs, more], axis=0), seq_dims).step()
    x_pieces = x_spread.whole()
    x_pieces = tie(w_z, *x_pieces)
    w_sib = [core_swap(piece) for piece in (w_z.pieces[0], *w_z.fresh())]
    early = len(w_sib)
    w_z.step()
    (w_sib,) = tie(w_z, w_sib)
    w_z = w_z.whole()
    w_sib = w_sib + [core_swap(piece) for piece in w_z[early:]]

    gu_mine = lax.all_to_all(after(gu_mine, w_z), ("seq", "zlo"), 0, 0, tiled=True)

    row_ids = jnp.concatenate([piece[tok, :tok] for piece in x_pieces]).astype(jnp.int32)
    row_ids = row_ids.reshape(length, 1)
    col_ids = jnp.stack(
        [lax.dynamic_slice(row_ids, ((seq ^ m) * tok, 0), (tok, 1)) for m in range(n_seq)]
    ).reshape(n_seq, 1, tok)
    tables = rope_tables(jnp.arange(length, dtype=jnp.int32), head_dim)
    all_gains = jnp.concatenate([piece[tok + 1 : tok + 2, : 4 * part] for piece in x_pieces], axis=0)
    all_gains = jnp.concatenate(
        [lax.dynamic_slice(all_gains, (seq ^ m, 0), (1, 4 * part)) for m in range(n_seq)], axis=0
    ).reshape(n_seq, 4, part)
    all_gains = jnp.transpose(all_gains, (1, 0, 2)).reshape(4, width).astype(f32)
    my_gains = gains.reshape(4, 1, part).astype(f32)
    qk_gains = (my_gains[0], my_gains[1])
    gain_attn, gain_ff = all_gains[2], all_gains[3]

    raw, squares, x_all, w_qkv, out_weight = project(
        x_pieces,
        [piece.reshape(n_seq, d_rows, 4 * part) for piece in w_z + w_sib],
        block_starts(
            n_seq,
            d_rows,
            z_dims + core_dims,
            z_axes,
            lambda s, hi, lo, core: ((s * n_hi + hi) * n_lo + lo) * n_core + core,
        ),
        block_starts(
            1,
            d_rows,
            z_dims + core_dims,
            z_axes,
            lambda block, hi, lo, core: (hi * n_lo + lo) * n_core + core,
        ),
        tok,
        part,
    )
    squares = squares.reshape(2, n_seq, tok)
    squares = sum_all(jnp.transpose(squares, (1, 0, 2)), seq_dims)
    inverse = lax.rsqrt(jnp.transpose(squares, (1, 0, 2)).reshape(2, length, 1) / width + norm_eps)
    inverse, gu_mine = tie(inverse, gu_mine)
    w_gu = lax.all_gather(gu_mine, pair_axes, axis=0, tiled=True)
    down = lax.all_gather(after(w_down, gu_mine), pair_axes, axis=0, tiled=True)

    context = (seq.astype(jnp.int32).reshape(1), raw, inverse, qk_gains, tables, (row_ids, col_ids))
    attended, attn_low, log_total = attend(context, heads, tok)
    branch = Collect(
        [held(dot(rows_of(attn_low, m), out_weight).astype(bf16)) for m in range(n_seq)], seq_dims
    ).whole()
    branch_norm, branch_inv = rms(branch)
    hidden = inputs.astype(f32) + branch_norm * gain_attn
    hidden_low = hidden.astype(bf16)

    w_gu = regroup(w_gu.reshape(-1, d_rows, 2 * units), lo_order)
    total = 1 << len(cube_dims)
    by_bits = lambda size: [
        m for m in range(total) if bin(m).count("1") == size or (size == 1 and m == 0)
    ]
    fours = lambda masks: [masks[i : i + 4] for i in range(0, len(masks), 4)]
    groups = [masks for size in range(1, len(cube_dims) + 1) for masks in fours(by_bits(size))]
    light = total == 8
    h_spread = Spread(hidden_low, cube_dims, spare_last=light).step()
    acts, partials, kept, late = {}, {}, (), []
    for i, masks in enumerate([[0, 1, 2, 3], [4, 5, 6], [7]] if light else groups):
        while any(m not in h_spread.pieces for m in masks):
            h_spread.step()
        pieces = [h_spread.pieces[m] for m in masks]
        kept, act, sums = feed(pieces, masks, total, w_gu, down if i else None, kept)
        acts.update(zip(masks, act, strict=True))
        late += [] if i else masks
        partials.update(zip(masks if i else [], sums, strict=True))
        if light and i == 0:
            h_spread.pieces[4] = after(h_spread.pieces[4], act)
    h_all, middle_all = kept
    partials.update(zip(late, feed_down(middle_all, late, tok, down), strict=True))
    partials = [partials[m] for m in range(total)]
    ff_raw = Collect(partials, cube_dims).whole()
    ff_norm, ff_inv = rms(ff_raw)
    mixed = (hidden + ff_norm * gain_ff).astype(bf16)

    grad_output = cotangent[0].astype(f32)
    grad_ff_gain = jnp.sum(grad_output * ff_norm, axis=0)
    d_ff = rms_back(grad_output, ff_norm, ff_inv, gain_ff).astype(bf16)
    d_spread = Spread(d_ff, cube_dims).step()
    partials, kept = {}, ()
    for masks in groups:
        while any(m not in d_spread.pieces for m in masks):
            d_spread.step()
        pieces = [d_spread.pieces[m] for m in masks]
        act = [acts[m] for m in masks]
        kept, sums = feed_back(pieces, masks, total, act, w_gu, down, kept)
        partials.update(zip(masks, sums, strict=True))
    d_ff_all, d_gate_all, d_up_all = kept
    partials = [partials[m] for m in range(total)]
    d_hidden = Collect(partials, cube_dims).step()

    owned = lambda grad: lax.psum_scatter(grad, pair_axes, scatter_dimension=0, tiled=True)
    order = (n_seq, n_hi, n_lo, n_core)
    grad_gu = owner_grad(h_all, after(d_gate_all, partials), order, d_rows, 0, [])
    (grad_gu,) = tie(d_hidden, grad_gu)
    d_hidden.step()
    grad_gu = owner_grad(h_all, after(d_up_all, grad_gu), order, d_rows, 1, [grad_gu])
    (grad_gu,) = tie(d_hidden, grad_gu)
    grad_gu = owned(grad_gu.reshape(-1, d_rows, 2 * units))
    d_hidden = d_hidden.whole()

    d_hidden = grad_output + d_hidden
    grad_attn_gain = jnp.sum(d_hidden * branch_norm, axis=0)
    d_branch = rms_back(d_hidden, branch_norm, branch_inv, gain_attn).astype(bf16)
    d_branch_pieces = Spread(d_branch, seq_dims).whole()
    grad_down = t_dot(middle_all, after(d_ff_all, d_branch)).astype(bf16)
    d_branch_pieces, grad_down = tie(d_branch_pieces, grad_down)
    grad_down = owned(grad_down).astype(f32)
    d_attended = jnp.concatenate(
        [dot_t(piece, out_weight).astype(bf16) for piece in d_branch_pieces], axis=0
    )
    e_query, e_key, d_value, q_sum, k_sum, grad_query_gain, grad_key_gain = attend_back(
        context, d_attended, attended, log_total, heads, tok
    )
    means = jnp.stack([q_sum[0], k_sum[0]]).reshape(2, n_seq, tok)
    means = sum_all(jnp.transpose(means, (1, 0, 2)), seq_dims)
    means = jnp.transpose(means, (1, 0, 2)).reshape(2, length, 1) / width

    n_z = n_hi * n_lo
    z_blocks = lambda grad: take_blocks(
        jnp.transpose(
            grad.reshape(n_seq, n_hi, n_lo, n_core, d_rows, grad.shape[1]), (1, 2, 3, 0, 4, 5)
        ),
        z_dims + core_dims,
        z_axes,
    )
    d_branch_all = jnp.concatenate(d_branch_pieces, axis=0)
    grad_out = t_dot(attn_low, after(d_branch_all, d_value)).astype(bf16)
    grad_out = jnp.concatenate([grad_out[:, i * part : (i + 1) * part] for i in range(n_seq)], axis=0)
    means, grad_out = tie(means, grad_out)
    d_qkv = finish(e_query, e_key, raw, inverse, means, d_value, part, tok)
    grad_qkv = t_dot(x_all, d_qkv).astype(bf16)
    both = [
        jnp.concatenate([a, b], axis=-1)
        for a, b in zip(z_blocks(grad_qkv), z_blocks(grad_out), strict=True)
    ]
    theirs = [core_swap(piece) for piece in both[n_z:]]
    low_rows, theirs = tie(d_qkv, theirs)
    input_grad = Collect(
        [held(dot_t(rows_of(low_rows, m), w_qkv).astype(bf16)) for m in range(n_seq)], seq_dims
    )
    both = [
        add_low(a, b).reshape(-1, 4 * part) for a, b in zip(both[:n_z], theirs, strict=True)
    ]
    both = Collect(both, z_dims).step()
    input_grad.step()
    full_row = lambda cols: lax.dynamic_update_slice(jnp.zeros((width,), f32), cols, (seq * part,))
    rows = jnp.stack(
        [full_row(grad_query_gain[0]), full_row(grad_key_gain[0]), grad_attn_gain, grad_ff_gain]
    )
    rows = jnp.transpose(rows.reshape(4, n_dev, d_rows), (1, 0, 2))
    rows = lax.all_to_all(after(rows, low_rows), ("seq",) + z_axes, 0, 0, tiled=True)
    rows, grad_gu = tie(both, input_grad, rows, grad_gu)
    grad_gu = grad_gu.reshape(n_seq * n_lo, d_rows, 2 * units)
    grad_gu = lax.all_to_all(grad_gu, ("seq", "zlo"), 0, 0, tiled=True)
    rows = jnp.sum(rows, axis=0)
    both.step()
    input_grad.step()
    grad_gu, grad_down, rows = tie(both, input_grad, grad_gu, grad_down, rows)
    both = both.whole().astype(bf16).reshape(n_seq, d_rows, 4 * part)
    grad_qkv, grad_out = both[..., : 3 * part], both[..., 3 * part :]
    grad_qkv = lax.all_to_all(grad_qkv, "seq", 0, 0, tiled=True)
    input_grad = d_hidden + input_grad.whole()
    grad_out = jnp.concatenate([grad_out[i] for i in range(n_seq)], axis=1).astype(f32)
    grad_gate, grad_up = unpack_units(grad_gu, n_seq, sizes, ff_rows)
    grad_query, grad_key, grad_value = unpack_columns(grad_qkv, 3)

    return (
        mixed[None],
        input_grad[None],
        grad_query,
        grad_key,
        grad_value,
        grad_out,
        grad_gate,
        grad_up,
        grad_down,
        rows[0],
        rows[1],
        rows[2],
        rows[3],
    )


def solution(mesh):
    n_seq, n_row = mesh.shape["seq"], mesh.shape["row"]
    n_core = 2
    n_lo = 2
    n_hi = n_row // (n_core * n_lo)
    cut = Mesh(
        mesh.devices.reshape(n_seq, n_hi, n_lo, n_core), ("seq", "zhi", "zlo", "core")
    )
    row = ("zhi", "zlo", "core")
    every = ("seq",) + row
    acts = P(row, "seq", None)
    matrix = P(every, None)
    vector = P(every)
    return jax.shard_map(
        per_device,
        mesh=cut,
        in_specs=(acts, P(row, "seq")) + (matrix,) * 7 + (vector,) * 4 + (acts,),
        out_specs=(acts, acts) + (matrix,) * 7 + (vector,) * 4,
        check_vma=False,
    )
```

time: 1130 us -> 859 us (0.76)
  Pallas kernels: 37.2 us -> 197 us
  matrix products: 204 us -> 58.6 us
  waiting for transfers between devices: 432 us -> 320 us
  blocking collectives: 78 us -> 0 us
  local copies, waits for them, and re-layouts: 140 us -> 76.7 us
  starting transfers between devices: 133 us -> 106 us
  other arithmetic: 91.6 us -> 75.5 us
  between operations: 3.48 us -> 16.3 us
    pallas_call x2 -> x18, Pallas kernels: 37.2 us -> 197 us  [the longest x6 91.6 us: feed_call(): pl.pallas_call(body, grid=(steps,), in_specs=[somewhere] * number + in_sp...]
    ppermute x99 -> x75, waiting for transfers between devices: 430 us -> 315 us  [swap(): lax.ppermute(block, axis, [(i, i ^ mask) for i in range(lax.axis_size(axi...]
    dot_general x29 -> x4, matrix products: 77.3 us -> 4.54 us  [dot(): return jnp.dot(left, right, preferred_element_type=f32)]
    dot_general x21 -> x8, matrix products: 72.2 us -> 25.6 us  [dot_t(): lax.dot_general(left, right, (((1,), (1,)), ((), ())), preferred_element_...]
    all_gather x1 -> x0, blocking collectives: 40.1 us -> none  [per_device(): gains = lax.all_gather(gains, every, axis=0, tiled=False)]
    unnamed x1 -> x0, blocking collectives: 37.9 us -> none
    dot_general x4 -> x3, matrix products: 54.1 us -> 28.5 us  [t_dot(): lax.dot_general(left, right, (((0,), (0,)), ((), ())), preferred_element_...]
    dynamic_update_slice x24 -> x0, local copies, waits for them, and re-layouts: 21.1 us -> none  [gather_blocks(): lax.dynamic_update_slice(whole, pieces[m][(None,) * len(axes)], place)]
  transfers between devices with their start and end apart: 103 -> 84, of which waited for: 37 -> 40; matrix products, arithmetic and copies ran while one was open for 32% -> 18% of each run, Pallas kernels for 3% -> 20%
where the time goes in v2:
time: 859 us; the launch traced here: 850 us
  waiting for transfers between devices  320 us (37%)
  Pallas kernels  197 us (23%)
  starting transfers between devices  106 us (12%)
  local copies, waits for them, and re-layouts  76.7 us (9%)
  other arithmetic  75.5 us (9%)
  matrix products  58.6 us (7%)
  between operations  16.3 us (2%)
    ppermute x75, waiting for transfers between devices, swap(): lax.ppermute(block, axis, [(i, i ^ mask) for i in range(lax.axis_size(axi...  315 us
    pallas_call x6, Pallas kernels, feed_call(): pl.pallas_call(body, grid=(steps,), in_specs=[somewhere] * number + in_sp...  91.6 us
    ppermute x75, starting transfers between devices, swap(): lax.ppermute(block, axis, [(i, i ^ mask) for i in range(lax.axis_size(axi...  86.7 us
    unnamed x225, local copies, waits for them, and re-layouts  46.8 us
    dot_general x3, matrix products, t_dot(): lax.dot_general(left, right, (((0,), (0,)), ((), ())), preferred_element_...  28.5 us
    pallas_call x1, Pallas kernels, attend_back(): pl.pallas_call(functools.partial(backward_kernel, scale * math.log2(math....  26.3 us
    dot_general x8, matrix products, dot_t(): lax.dot_general(left, right, (((1,), (1,)), ((), ())), preferred_element_...  25.6 us
    pallas_call x2, Pallas kernels, owner_grad(): pl.pallas_call(kernel, grid=(n_seq,), in_specs=[pl.BlockSpec((tokens, col...  23 us
  transfers between devices with their start and end apart: 84, of which 40 were waited for; matrix products, arithmetic and copies ran while one was open for 18% of the time, Pallas kernels for 20%

profile of v2, /device:TPU:0, one launch (start us, length us, event | category | flops | bytes accessed | tf_op | source)
XLA Modules:
  0.0 850.5 jit_solution(2771976016806894262)
XLA Ops:
  21.9 3.9 pack_units.1
  25.9 4.1 all-to-all-done
  35.7 20.2 %collective-permute-done.6.refs_2_ = bf16[272,2048]{1,0:T(8,128)(2,1)S(1)} collective-permute-done((bf16[272,2048]{1,0:T(8,128)(2,1)S(1)}, bf16[272,2048]{1,0:T(8,128)(2,1)S(1)}, u32[]{:S(2)}, u32[]{:S(2)}) %collective-permute-start.6) | collective-permute-done | bytes 1114144 | tf_op jit(solution)/shard_map/ppermute | solution.py:29
  58.0 10.9 %collective-permute-done.7 = bf16[272,1024]{1,0:T(8,128)(2,1)S(1)} collective-permute-done((bf16[272,1024]{1,0:T(8,128)(2,1)S(1)}, bf16[272,1024]{1,0:T(8,128)(2,1)S(1)}, u32[]{:S(2)}, u32[]{:S(2)}) %collective-permute-start.7) | collective-permute-done | bytes 557088 | tf_op jit(solution)/shard_map/ppermute | solution.py:29
  69.5 9.0 %collective-permute-done.3 = bf16[256,2048]{1,0:T(8,128)(2,1)S(1)} collective-permute-done((bf16[256,2048]{1,0:T(8,128)(2,1)S(1)}, bf16[256,2048]{1,0:T(8,128)(2,1)S(1)}, u32[]{:S(2)}, u32[]{:S(2)}) %collective-permute-start.3) | collective-permute-done | bytes 1048608 | tf_op jit(solution)/shard_map/ppermute | solution.py:29
  80.5 3.9 collective-permute-start.9
  84.4 20.9 %collective-permute-done.10 = bf16[256,1024]{1,0:T(8,128)(2,1)S(1)} collective-permute-done((bf16[256,1024]{1,0:T(8,128)(2,1)S(1)}, bf16[256,1024]{1,0:T(8,128)(2,1)S(1)}, u32[]{:S(2)}, u32[]{:S(2)}) %collective-permute-start.10) | collective-permute-done | bytes 524320 | tf_op jit(solution)/shard_map/ppermute | solution.py:29
  108.5 4.4 all-to-all-start.1
  125.7 12.9 %project.1 = (f32[1024,1536]{1,0:T(8,128)}, f32[2,1024,1]{2,1,0:T(8,128)S(1)}, bf16[1024,2048]{1,0:T(8,128)(2,1)}, bf16[2048,1536]{1,0:T(8,128)(2,1)}, bf16[512,2048]{1,0:T(8,128)(2,1)}) custom-call(s32[32]{0:T(128)S(1)} %stack.206.table, s32[8]{0:T(128)S(1)} %stack.207.out_table, bf16[272,2048]{1,0:T(8,128)(2,1)S(1)} %fusion.13.refs_0_, ...), custom_call_target="tpu_custom_call" | custom-call | flops 6442450944 | bytes 10485760 | tf_op jit(solution)/shard_map/project/pallas_call | solution.py:259
  156.1 4.0 copy-done
  160.2 14.3 %attend.1 = (f32[1024,512]{1,0:T(8,128)S(1)}, bf16[1024,512]{1,0:T(8,128)(2,1)S(1)}, f32[4,1024,1]{2,1,0:T(8,128)S(1)}) custom-call(s32[1]{0:T(128)} %bitcast.1.place, f32[1024,1536]{1,0:T(8,128)S(1)} %copy-done, f32[1024,1536]{1,0:T(8,128)S(1)} %copy-done, f32[1024,1536]{1,0:T(8,128)S(1)} %copy-done, f32[2,1024,1]{2,1,0:T(8,128)S(1)} %copy.55.q_inv.k_inv, ...), custom_call_target="tpu_custom_call" | custom-call | flops 1073741824 | bytes 9437184 | tf_op jit(solution)/shard_map/attend/pallas_call | solution.py:460
  182.9 5.4 collective-permute-done.17
  199.9 13.9 %collective-permute-done.18 = bf16[256,2048]{1,0:T(8,128)(2,1)} collective-permute-done((bf16[256,2048]{1,0:T(8,128)(2,1)}, bf16[256,2048]{1,0:T(8,128)(2,1)}, u32[]{:S(2)}, u32[]{:S(2)}) %collective-permute-start.18) | collective-permute-done | bytes 1048608 | tf_op jit(solution)/shard_map/ppermute | solution.py:29
  223.4 20.0 %collective-permute-done.23.refs_2_ = bf16[256,2048]{1,0:T(8,128)(2,1)S(1)} collective-permute-done((bf16[256,2048]{1,0:T(8,128)(2,1)}, bf16[256,2048]{1,0:T(8,128)(2,1)S(1)}, u32[]{:S(2)}, u32[]{:S(2)}) %collective-permute-start.23) | collective-permute-done | bytes 1048608 | tf_op jit(solution)/shard_map/ppermute | solution.py:29
  248.6 5.9 collective-permute-done.24
  265.6 16.5 %feed.3 = (bf16[2048,2048]{1,0:T(8,128)(2,1)}, bf16[2048,1024]{1,0:T(8,128)(2,1)}, bf16[256,1024]{1,0:T(8,128)(2,1)S(1)}, bf16[256,1024]{1,0:T(8,128)(2,1)S(1)},...) custom-call(bf16[256,2048]{1,0:T(8,128)(2,1)} %fusion.10.refs_0_, ...), custom_call_target="tpu_custom_call" | custom-call | flops 12884901888 | bytes 33554432 | tf_op jit(solution)/shard_map/feed/pallas_call | solution.py:653
  287.8 21.6 %collective-permute-done.26.refs_2_ = bf16[256,2048]{1,0:T(8,128)(2,1)S(1)} collective-permute-done((bf16[256,2048]{1,0:T(8,128)(2,1)}, bf16[256,2048]{1,0:T(8,128)(2,1)S(1)}, u32[]{:S(2)}, u32[]{:S(2)}) %collective-permute-start.26) | collective-permute-done | bytes 1048608 | tf_op jit(solution)/shard_map/ppermute | solution.py:29
  316.1 16.9 %feed.4 = (bf16[2048,2048]{1,0:T(8,128)(2,1)}, bf16[2048,1024]{1,0:T(8,128)(2,1)}, bf16[256,1024]{1,0:T(8,128)(2,1)S(1)}, bf16[256,1024]{1,0:T(8,128)(2,1)S(1)},...) custom-call(bf16[256,2048]{1,0:T(8,128)(2,1)} %collective-permute-do, ...), custom_call_target="tpu_custom_call", output_to_operand_aliasing={{0}: (6, {}), {1}: (7, {})} | custom-call | flops 9663676416 | bytes 28311552 | tf_op jit(solution)/shard_map/feed/pallas_call | solution.py:653
  336.9 7.9 feed.5
  347.8 5.9 feed_down.1
  356.1 8.3 collective-permute-done.36
  369.6 13.9 %collective-permute-done.34 = bf16[256,2048]{1,0:T(8,128)(2,1)S(1)} collective-permute-done((bf16[256,2048]{1,0:T(8,128)(2,1)S(1)}, bf16[256,2048]{1,0:T(8,128)(2,1)S(1)}, u32[]{:S(2)}, u32[]{:S(2)}) %collective-permute-start.34) | collective-permute-done | bytes 1048608 | tf_op jit(solution)/shard_map/ppermute | solution.py:29
  389.6 17.0 %collective-permute-done.35 = bf16[256,2048]{1,0:T(8,128)(2,1)S(1)} collective-permute-done((bf16[256,2048]{1,0:T(8,128)(2,1)S(1)}, bf16[256,2048]{1,0:T(8,128)(2,1)S(1)}, u32[]{:S(2)}, u32[]{:S(2)}) %collective-permute-start.35) | collective-permute-done | bytes 1048608 | tf_op jit(solution)/shard_map/ppermute | solution.py:29
  415.3 17.4 %collective-permute-done.40.refs_2_ = bf16[256,2048]{1,0:T(8,128)(2,1)} collective-permute-done((bf16[256,2048]{1,0:T(8,128)(2,1)S(1)}, bf16[256,2048]{1,0:T(8,128)(2,1)}, u32[]{:S(2)}, u32[]{:S(2)}) %collective-permute-start.40) | collective-permute-done | bytes 1048608 | tf_op jit(solution)/shard_map/ppermute | solution.py:29
  438.6 23.0 %feed_back.3 = (bf16[2048,2048]{1,0:T(8,128)(2,1)}, bf16[2048,1024]{1,0:T(8,128)(2,1)}, bf16[2048,1024]{1,0:T(8,128)(2,1)}, bf16[256,2048]{1,0:T(8,128)(2,1)}, b...) custom-call(bf16[256,2048]{1,0:T(8,128)(2,1)} %copy-done.101, ...), custom_call_target="tpu_custom_call" | custom-call | flops 12884901888 | bytes 33554432 | tf_op jit(solution)/shard_map/feed_back/pallas_call | solution.py:653
  467.6 18.6 %feed_back.4 = (bf16[2048,2048]{1,0:T(8,128)(2,1)}, bf16[2048,1024]{1,0:T(8,128)(2,1)}, bf16[2048,1024]{1,0:T(8,128)(2,1)}, bf16[256,2048]{1,0:T(8,128)(2,1)}, b...) custom-call(bf16[256,2048]{1,0:T(8,128)(2,1)} %copy-done.107, ...), custom_call_target="tpu_custom_call", output_to_operand_aliasing={{0}: (11, {}), {1}: (12, {}), {2}: (13, {})} | custom-call | flops 9663676416 | bytes 28311552 | tf_op jit(solution)/shard_map/feed_back/pallas_call | solution.py:653
  488.8 8.8 %feed_back.5 = (bf16[2048,2048]{1,0:T(8,128)(2,1)}, bf16[2048,1024]{1,0:T(8,128)(2,1)}, bf16[2048,1024]{1,0:T(8,128)(2,1)}, bf16[256,2048]{1,0:T(8,128)(2,1)S(1)}) custom-call(bf16[256,2048]{1,0:T(8,128)(2,1)S(1)} %pad_maximum_fusion.11.refs_0_, ...), custom_call_target="tpu_custom_call", output_to_operand_aliasing={{0}: (5, {}), {1}: (6, {}), {2}: (7, {})} | custom-call | flops 3221225472 | bytes 17825792 | tf_op jit(solution)/shard_map/feed_back/pallas_call | solution.py:653
  501.6 11.7 %owner_grad.2.refs_0_ = bf16[2,2,4,2,64,2048]{5,4,3,2,1,0:T(8,128)(2,1)S(1)} custom-call(bf16[2048,2048]{1,0:T(8,128)(2,1)} %get-tuple-element.199.h, bf16[2048,1024]{1,0:T(8,128)(2,1)S(1)} %copy-done.7), custom_call_target="tpu_custom_call" | custom-call | flops 8589934592 | bytes 16777216 | tf_op jit(solution)/shard_map/owner_grad/pallas_call | solution.py:766
  520.7 11.3 %owner_grad.3 = bf16[2,2,4,2,64,2048]{5,4,3,2,1,0:T(8,128)(2,1)S(1)} custom-call(bf16[2048,2048]{1,0:T(8,128)(2,1)} %get-tuple-element.199.h, bf16[2048,1024]{1,0:T(8,128)(2,1)S(1)} %copy-done.8, bf16[2,2,4,2,64,2048]{5,4,3,2,1,0:T(8,128)(2,1)S(1)} %owner_grad.2.refs_0_), custom_call_target="tpu_custom_call", output_to_operand_aliasing={{}: (2, {})} | custom-call | flops 8589934592 | bytes 16777216 | tf_op jit(solution)/shard_map/owner_grad/pallas_call | solution.py:766
  535.3 4.4 collective-permute-done.51
  548.9 10.2 %collective-permute-done.54 = bf16[256,2048]{1,0:T(8,128)(2,1)S(1)} collective-permute-done((bf16[256,2048]{1,0:T(8,128)(2,1)S(1)}, bf16[256,2048]{1,0:T(8,128)(2,1)S(1)}, u32[]{:S(2)}, u32[]{:S(2)}) %collective-permute-start.54) | collective-permute-done | bytes 1048608 | tf_op jit(solution)/shard_map/ppermute | solution.py:29
  559.1 6.9 collective-permute-done.55
  569.9 20.7 %collective-permute-done.58 = bf16[256,2048]{1,0:T(8,128)(2,1)} collective-permute-done((bf16[256,2048]{1,0:T(8,128)(2,1)}, bf16[256,2048]{1,0:T(8,128)(2,1)}, u32[]{:S(2)}, u32[]{:S(2)}) %collective-permute-start.58) | collective-permute-done | bytes 1048608 | tf_op jit(solution)/shard_map/ppermute | solution.py:29
  594.2 14.2 %convolution_convert_fusion.1 = bf16[1024,2048]{1,0:T(8,128)(2,1)} fusion(bf16[2048,1024]{1,0:T(8,128)(2,1)} %get-tuple-element.172.middle, bf16[2048,2048]{1,0:T(8,128)(2,1)} %get-tuple-element.216), kind=kOutput, calls=%fused_computation.2 | convolution fusion | flops 8592031744 | bytes 16777216 | tf_op jit(solution)/shard_map/dot_general | solution.py:917
  618.6 26.3 %attend_back.1 = (f32[1024,512]{1,0:T(8,128)S(1)}, f32[1024,512]{1,0:T(8,128)S(1)}, bf16[1024,512]{1,0:T(8,128)(2,1)S(1)}, f32[1,1024,1]{2,1,0:T(8,128)S(1)}, f3...) custom-call(s32[1]{0:T(128)} %bitcast.1.place, ...), custom_call_target="tpu_custom_call" | custom-call | flops 2684354560 | bytes 15728640 | tf_op jit(solution)/shard_map/attend_back/pallas_call | solution.py:491
  645.1 5.7 pad_maximum_fusion
  653.8 4.6 convolution_convert_fusion.2
  664.9 7.7 finish.1
  672.7 9.8 %convolution_convert_fusion = bf16[2048,1536]{1,0:T(8,128)(2,1)S(1)} fusion(bf16[1024,2048]{1,0:T(8,128)(2,1)} %get-tuple-element.230, bf16[1024,1536]{1,0:T(8,128)(2,1)} %finish.1), kind=kOutput, calls=%fused_computation | convolution fusion | flops 6445596672 | bytes 13631488 | tf_op jit(solution)/shard_map/dot_general | solution.py:917
  698.1 4.6 convolution_convert_fusion.9
  713.7 5.6 convolution_convert_fusion.7
  723.5 13.1 %collective-permute-done.67 = bf16[256,1024]{1,0:T(8,128)(2,1)} collective-permute-done((bf16[256,1024]{1,0:T(8,128)(2,1)}, bf16[256,1024]{1,0:T(8,128)(2,1)}, u32[]{:S(2)}, u32[]{:S(2)}) %collective-permute-start.67) | collective-permute-done | bytes 524320 | tf_op jit(solution)/shard_map/ppermute | solution.py:29
  736.6 11.8 %collective-permute-done.68 = bf16[256,1024]{1,0:T(8,128)(2,1)} collective-permute-done((bf16[256,1024]{1,0:T(8,128)(2,1)}, bf16[256,1024]{1,0:T(8,128)(2,1)}, u32[]{:S(2)}, u32[]{:S(2)}) %collective-permute-start.68) | collective-permute-done | bytes 524320 | tf_op jit(solution)/shard_map/ppermute | solution.py:29
  772.1 5.9 convolution_convert_fusion.10
  782.5 16.5 %collective-permute-done.74 = bf16[256,2048]{1,0:T(8,128)(2,1)} collective-permute-done((bf16[256,2048]{1,0:T(8,128)(2,1)}, bf16[256,2048]{1,0:T(8,128)(2,1)}, u32[]{:S(2)}, u32[]{:S(2)}) %collective-permute-start.74) | collective-permute-done | bytes 1048608 | tf_op jit(solution)/shard_map/ppermute | solution.py:29
  799.9 14.3 %collective-permute-done.72 = bf16[256,2048]{1,0:T(8,128)(2,1)} collective-permute-done((bf16[256,2048]{1,0:T(8,128)(2,1)}, bf16[256,2048]{1,0:T(8,128)(2,1)}, u32[]{:S(2)}, u32[]{:S(2)}) %collective-permute-start.72) | collective-permute-done | bytes 1048608 | tf_op jit(solution)/shard_map/ppermute | solution.py:29
  814.1 8.2 collective-permute-done.71
  829.9 4.2 unpack_units.1
  (560 shorter events, 286.9 us)
Async XLA Ops:
  30.4 25.6 %collective-permute-start.6 = (bf16[272,2048]{1,0:T(8,128)(2,1)S(1)}, bf16[272,2048]{1,0:T(8,128)(2,1)S(1)}, u32[]{:S(2)}, u32[]{:S(2)}) collective-permute-start(bf16[272,2048]{1,0:T(8,128)(2,1)S(1)} %fusion.13.refs_0_), channel_id=1, source_target_pairs={{0,16},{8,24},{16,0},{24,8},{1,17},{9,25},{17,1},{25,9},{2,18},{10... | collective-permute-start | bytes 3342344 | tf_op jit(solution)/shard_map/ppermute | solution.py:29
  31.9 25.3 %collective-permute-start.5 = (bf16[272,2048]{1,0:T(8,128)(2,1)S(1)}, bf16[272,2048]{1,0:T(8,128)(2,1)S(1)}, u32[]{:S(2)}, u32[]{:S(2)}) collective-permute-start(bf16[272,2048]{1,0:T(8,128)(2,1)S(1)} %fusion.13.refs_0_), channel_id=1, source_target_pairs={{0,8},{8,0},{16,24},{24,16},{1,9},{9,1},{17,25},{25,17},{2,10},{10... | collective-permute-start | bytes 3342344 | tf_op jit(solution)/shard_map/ppermute | solution.py:29
  32.6 45.9 %collective-permute-start.3 = (bf16[256,2048]{1,0:T(8,128)(2,1)S(1)}, bf16[256,2048]{1,0:T(8,128)(2,1)S(1)}, u32[]{:S(2)}, u32[]{:S(2)}) collective-permute-start(bf16[256,2048]{1,0:T(8,128)(2,1)S(1)} %maximum_maximum_fusion), channel_id=1, source_target_pairs={{0,2},{2,0},{1,3},{3,1},{4,6},{6,4},{5,7},{7,5},{8,10},{10,8},{9,1... | collective-permute-start | bytes 3145736 | tf_op jit(solution)/shard_map/ppermute | solution.py:29
  33.1 45.4 %collective-permute-start.4 = (bf16[256,2048]{1,0:T(8,128)(2,1)S(1)}, bf16[256,2048]{1,0:T(8,128)(2,1)S(1)}, u32[]{:S(2)}, u32[]{:S(2)}) collective-permute-start(bf16[256,2048]{1,0:T(8,128)(2,1)S(1)} %maximum_maximum_fusion), channel_id=1, source_target_pairs={{0,4},{4,0},{1,5},{5,1},{2,6},{6,2},{3,7},{7,3},{8,12},{12,8},{9,1... | collective-permute-start | bytes 3145736 | tf_op jit(solution)/shard_map/ppermute | solution.py:29
  58.0 47.6 %collective-permute-start.11 = (bf16[256,2048]{1,0:T(8,128)(2,1)S(1)}, bf16[256,2048]{1,0:T(8,128)(2,1)S(1)}, u32[]{:S(2)}, u32[]{:S(2)}) collective-permute-start(bf16[256,2048]{1,0:T(8,128)(2,1)S(1)} %maximum_maximum_fusion), channel_id=1, source_target_pairs={{0,1},{1,0},{2,3},{3,2},{4,5},{5,4},{6,7},{7,6},{8,9},{9,8},{10,11... | collective-permute-start | bytes 3145736 | tf_op jit(solution)/shard_map/ppermute | solution.py:29
  78.5 28.1 %collective-permute-start.12 = (bf16[256,2048]{1,0:T(8,128)(2,1)S(1)}, bf16[256,2048]{1,0:T(8,128)(2,1)S(1)}, u32[]{:S(2)}, u32[]{:S(2)}) collective-permute-start(bf16[256,2048]{1,0:T(8,128)(2,1)S(1)} %collective-permute-done.3), channel_id=1, source_target_pairs={{0,1},{1,0},{2,3},{3,2},{4,5},{5,4},{6,7},{7,6},{8,9},{9,8},{10,11... | collective-permute-start | bytes 3145736 | tf_op jit(solution)/shard_map/ppermute | solution.py:29
  78.6 28.9 %collective-permute-start.13 = (bf16[256,2048]{1,0:T(8,128)(2,1)S(1)}, bf16[256,2048]{1,0:T(8,128)(2,1)S(1)}, u32[]{:S(2)}, u32[]{:S(2)}) collective-permute-start(bf16[256,2048]{1,0:T(8,128)(2,1)S(1)} %collective-permute-done.4), channel_id=1, source_target_pairs={{0,1},{1,0},{2,3},{3,2},{4,5},{5,4},{6,7},{7,6},{8,9},{9,8},{10,11... | collective-permute-start | bytes 3145736 | tf_op jit(solution)/shard_map/ppermute | solution.py:29
  79.2 26.2 %collective-permute-start.10 = (bf16[256,1024]{1,0:T(8,128)(2,1)S(1)}, bf16[256,1024]{1,0:T(8,128)(2,1)S(1)}, u32[]{:S(2)}, u32[]{:S(2)}) collective-permute-start(bf16[256,1024]{1,0:T(8,128)(2,1)S(1)} %slice.382), channel_id=1, source_target_pairs={{0,4},{4,0},{1,5},{5,1},{2,6},{6,2},{3,7},{7,3},{8,12},{12,8},{9,1... | collective-permute-start | bytes 1572872 | tf_op jit(solution)/shard_map/ppermute | solution.py:29
  80.5 24.9 %collective-permute-start.9 = (bf16[256,1024]{1,0:T(8,128)(2,1)S(1)}, bf16[256,1024]{1,0:T(8,128)(2,1)S(1)}, u32[]{:S(2)}, u32[]{:S(2)}) collective-permute-start(bf16[256,1024]{1,0:T(8,128)(2,1)S(1)} %slice.381), channel_id=1, source_target_pairs={{0,2},{2,0},{1,3},{3,1},{4,6},{6,4},{5,7},{7,5},{8,10},{10,8},{9,1... | collective-permute-start | bytes 1572872 | tf_op jit(solution)/shard_map/ppermute | solution.py:29
  108.5 40.1 %all-to-all-start.1 = ((bf16[8,64,2048]{2,1,0:T(8,128)(2,1)}), bf16[8,64,2048]{2,1,0:T(8,128)(2,1)}, u32[]{:S(2)}, u32[]{:S(2)}) async-start(bf16[8,64,2048]{2,1,0:T(8,128)(2,1)} %pack_units.1), calls=%async_computation.1 | async-start | bytes 4194304 | tf_op jit(solution)/shard_map/all_to_all | solution.py:1014
  112.9 144.7 %all-gather.3.cloned.1.call-start = ((), (), s32[]{:S(2)}) async-start(), calls=%async_computation.7 | async-start | bytes 10485760 | tf_op jit(solution)/shard_map/all_gather | solution.py:1055
  148.7 167.4 %all-gather.5.cloned.1.call-start = ((), (), s32[]{:S(2)}) async-start(), calls=%async_computation.8 | async-start | bytes 5242880 | tf_op jit(solution)/shard_map/all_gather | solution.py:1056
  182.7 565.7 %reduce-scatter.3.cloned.1.call-start = ((), (), s32[]{:S(2)}) async-start(), calls=%async_computation.9 | async-start | bytes 10485760 | tf_op jit(solution)/shard_map/reduce_scatter | solution.py:1110
  191.8 22.1 %collective-permute-start.18 = (bf16[256,2048]{1,0:T(8,128)(2,1)}, bf16[256,2048]{1,0:T(8,128)(2,1)}, u32[]{:S(2)}, u32[]{:S(2)}) collective-permute-start(bf16[256,2048]{1,0:T(8,128)(2,1)} %pad_maximum_fusion.4), channel_id=1, source_target_pairs={{0,8},{8,0},{16,24},{24,16},{1,9},{9,1},{17,25},{25,17},{2,10},{10... | collective-permute-start | bytes 3145736 | tf_op jit(solution)/shard_map/ppermute | solution.py:29
  195.8 21.7 %collective-permute-start.20 = (bf16[256,2048]{1,0:T(8,128)(2,1)}, bf16[256,2048]{1,0:T(8,128)(2,1)}, u32[]{:S(2)}, u32[]{:S(2)}) collective-permute-start(bf16[256,2048]{1,0:T(8,128)(2,1)} %pad_maximum_fusion.5), channel_id=1, source_target_pairs={{0,16},{8,24},{16,0},{24,8},{1,17},{9,25},{17,1},{25,9},{2,18},{10... | collective-permute-start | bytes 3145736 | tf_op jit(solution)/shard_map/ppermute | solution.py:29
  221.2 22.2 %collective-permute-start.23 = (bf16[256,2048]{1,0:T(8,128)(2,1)}, bf16[256,2048]{1,0:T(8,128)(2,1)S(1)}, u32[]{:S(2)}, u32[]{:S(2)}) collective-permute-start(bf16[256,2048]{1,0:T(8,128)(2,1)} %fusion.10.refs_0_), channel_id=1, source_target_pairs={{0,16},{8,24},{16,0},{24,8},{1,17},{9,25},{17,1},{25,9},{2,18},{10... | collective-permute-start | bytes 3145736 | tf_op jit(solution)/shard_map/ppermute | solution.py:29
  222.8 24.4 %collective-permute-start.22 = (bf16[256,2048]{1,0:T(8,128)(2,1)}, bf16[256,2048]{1,0:T(8,128)(2,1)S(1)}, u32[]{:S(2)}, u32[]{:S(2)}) collective-permute-start(bf16[256,2048]{1,0:T(8,128)(2,1)} %fusion.10.refs_0_), channel_id=1, source_target_pairs={{0,8},{8,0},{16,24},{24,16},{1,9},{9,1},{17,25},{25,17},{2,10},{10... | collective-permute-start | bytes 3145736 | tf_op jit(solution)/shard_map/ppermute | solution.py:29
  247.4 39.5 %collective-permute-start.21 = (bf16[256,2048]{1,0:T(8,128)(2,1)}, bf16[256,2048]{1,0:T(8,128)(2,1)}, u32[]{:S(2)}, u32[]{:S(2)}) collective-permute-start(bf16[256,2048]{1,0:T(8,128)(2,1)} %fusion.10.refs_0_), channel_id=1, source_target_pairs={{0,2},{2,0},{1,3},{3,1},{4,6},{6,4},{5,7},{7,5},{8,10},{10,8},{9,1... | collective-permute-start | bytes 3145736 | tf_op jit(solution)/shard_map/ppermute | solution.py:29
  286.9 22.5 %collective-permute-start.26 = (bf16[256,2048]{1,0:T(8,128)(2,1)}, bf16[256,2048]{1,0:T(8,128)(2,1)S(1)}, u32[]{:S(2)}, u32[]{:S(2)}) collective-permute-start(bf16[256,2048]{1,0:T(8,128)(2,1)} %collective-permute-done.21.refs_0_), channel_id=1, source_target_pairs={{0,16},{8,24},{16,0},{24,8},{1,17},{9,25},{17,1},{25,9},{2,18},{10... | collective-permute-start | bytes 3145736 | tf_op jit(solution)/shard_map/ppermute | solution.py:29
  287.3 25.5 %collective-permute-start.28 = (bf16[256,2048]{1,0:T(8,128)(2,1)}, bf16[256,2048]{1,0:T(8,128)(2,1)S(1)}, u32[]{:S(2)}, u32[]{:S(2)}) collective-permute-start(bf16[256,2048]{1,0:T(8,128)(2,1)} %collective-permute-done.21.refs_0_), channel_id=1, source_target_pairs={{0,8},{8,0},{16,24},{24,16},{1,9},{9,1},{17,25},{25,17},{2,10},{10... | collective-permute-start | bytes 3145736 | tf_op jit(solution)/shard_map/ppermute | solution.py:29
  311.2 24.3 %collective-permute-start.27 = (bf16[256,1024]{1,0:T(8,128)(2,1)}, bf16[256,1024]{1,0:T(8,128)(2,1)}, u32[]{:S(2)}, u32[]{:S(2)}) collective-permute-start(bf16[256,1024]{1,0:T(8,128)(2,1)} %slice.506), channel_id=1, source_target_pairs={{0,8},{8,0},{16,24},{24,16},{1,9},{9,1},{17,25},{25,17},{2,10},{10... | collective-permute-start | bytes 1572872 | tf_op jit(solution)/shard_map/ppermute | solution.py:29
  314.6 21.0 %collective-permute-start.29 = (bf16[256,1024]{1,0:T(8,128)(2,1)}, bf16[256,1024]{1,0:T(8,128)(2,1)}, u32[]{:S(2)}, u32[]{:S(2)}) collective-permute-start(bf16[256,1024]{1,0:T(8,128)(2,1)} %slice.507), channel_id=1, source_target_pairs={{0,16},{8,24},{16,0},{24,8},{1,17},{9,25},{17,1},{25,9},{2,18},{10... | collective-permute-start | bytes 1572872 | tf_op jit(solution)/shard_map/ppermute | solution.py:29
  345.0 22.3 %collective-permute-start.30 = (bf16[256,768]{1,0:T(8,128)(2,1)S(1)}, bf16[256,768]{1,0:T(8,128)(2,1)S(1)}, u32[]{:S(2)}, u32[]{:S(2)}) collective-permute-start(bf16[256,768]{1,0:T(8,128)(2,1)S(1)} %slice.419), channel_id=1, source_target_pairs={{0,16},{8,24},{16,0},{24,8},{1,17},{9,25},{17,1},{25,9},{2,18},{10... | collective-permute-start | bytes 1179656 | tf_op jit(solution)/shard_map/ppermute | solution.py:29
  354.5 29.0 %collective-permute-start.34 = (bf16[256,2048]{1,0:T(8,128)(2,1)S(1)}, bf16[256,2048]{1,0:T(8,128)(2,1)S(1)}, u32[]{:S(2)}, u32[]{:S(2)}) collective-permute-start(bf16[256,2048]{1,0:T(8,128)(2,1)S(1)} %pad_maximum_fusion.9), channel_id=1, source_target_pairs={{0,8},{8,0},{16,24},{24,16},{1,9},{9,1},{17,25},{25,17},{2,10},{10... | collective-permute-start | bytes 3145736 | tf_op jit(solution)/shard_map/ppermute | solution.py:29
  383.9 22.7 %collective-permute-start.35 = (bf16[256,2048]{1,0:T(8,128)(2,1)S(1)}, bf16[256,2048]{1,0:T(8,128)(2,1)S(1)}, u32[]{:S(2)}, u32[]{:S(2)}) collective-permute-start(bf16[256,2048]{1,0:T(8,128)(2,1)S(1)} %add_convert_fusion.9), channel_id=1, source_target_pairs={{0,16},{8,24},{16,0},{24,8},{1,17},{9,25},{17,1},{25,9},{2,18},{10... | collective-permute-start | bytes 3145736 | tf_op jit(solution)/shard_map/ppermute | solution.py:29
  386.0 22.5 %collective-permute-start.38 = (bf16[256,2048]{1,0:T(8,128)(2,1)S(1)}, bf16[256,2048]{1,0:T(8,128)(2,1)S(1)}, u32[]{:S(2)}, u32[]{:S(2)}) collective-permute-start(bf16[256,2048]{1,0:T(8,128)(2,1)S(1)} %add_convert_fusion.8), channel_id=1, source_target_pairs={{0,2},{2,0},{1,3},{3,1},{4,6},{6,4},{5,7},{7,5},{8,10},{10,8},{9,1... | collective-permute-start | bytes 3145736 | tf_op jit(solution)/shard_map/ppermute | solution.py:29
  388.2 21.2 %collective-permute-start.32 = (bf16[256,2048]{1,0:T(8,128)(2,1)S(1)}, bf16[256,2048]{1,0:T(8,128)(2,1)S(1)}, u32[]{:S(2)}, u32[]{:S(2)}) collective-permute-start(bf16[256,2048]{1,0:T(8,128)(2,1)S(1)} %add_convert_fusion.10), channel_id=1, source_target_pairs={{0,8},{8,0},{16,24},{24,16},{1,9},{9,1},{17,25},{25,17},{2,10},{10... | collective-permute-start | bytes 3145736 | tf_op jit(solution)/shard_map/ppermute | solution.py:29
  412.0 20.7 %collective-permute-start.40 = (bf16[256,2048]{1,0:T(8,128)(2,1)S(1)}, bf16[256,2048]{1,0:T(8,128)(2,1)}, u32[]{:S(2)}, u32[]{:S(2)}) collective-permute-start(bf16[256,2048]{1,0:T(8,128)(2,1)S(1)} %fusion.6.refs_0_), channel_id=1, source_target_pairs={{0,16},{8,24},{16,0},{24,8},{1,17},{9,25},{17,1},{25,9},{2,18},{10... | collective-permute-start | bytes 3145736 | tf_op jit(solution)/shard_map/ppermute | solution.py:29
  413.0 24.3 %collective-permute-start.39 = (bf16[256,2048]{1,0:T(8,128)(2,1)S(1)}, bf16[256,2048]{1,0:T(8,128)(2,1)}, u32[]{:S(2)}, u32[]{:S(2)}) collective-permute-start(bf16[256,2048]{1,0:T(8,128)(2,1)S(1)} %fusion.6.refs_0_), channel_id=1, source_target_pairs={{0,8},{8,0},{16,24},{24,16},{1,9},{9,1},{17,25},{25,17},{2,10},{10... | collective-permute-start | bytes 3145736 | tf_op jit(solution)/shard_map/ppermute | solution.py:29
  414.7 23.8 %collective-permute-start.41 = (bf16[256,2048]{1,0:T(8,128)(2,1)S(1)}, bf16[256,2048]{1,0:T(8,128)(2,1)}, u32[]{:S(2)}, u32[]{:S(2)}) collective-permute-start(bf16[256,2048]{1,0:T(8,128)(2,1)S(1)} %fusion.6.refs_0_), channel_id=1, source_target_pairs={{0,2},{2,0},{1,3},{3,1},{4,6},{6,4},{5,7},{7,5},{8,10},{10,8},{9,1... | collective-permute-start | bytes 3145736 | tf_op jit(solution)/shard_map/ppermute | solution.py:29
  432.7 33.3 %collective-permute-start.42 = (bf16[256,2048]{1,0:T(8,128)(2,1)}, bf16[256,2048]{1,0:T(8,128)(2,1)S(1)}, u32[]{:S(2)}, u32[]{:S(2)}) collective-permute-start(bf16[256,2048]{1,0:T(8,128)(2,1)} %collective-permute-done.40.refs_2_), channel_id=1, source_target_pairs={{0,8},{8,0},{16,24},{24,16},{1,9},{9,1},{17,25},{25,17},{2,10},{10... | collective-permute-start | bytes 3145736 | tf_op jit(solution)/shard_map/ppermute | solution.py:29
  437.2 24.4 %collective-permute-start.43 = (bf16[256,2048]{1,0:T(8,128)(2,1)}, bf16[256,2048]{1,0:T(8,128)(2,1)S(1)}, u32[]{:S(2)}, u32[]{:S(2)}) collective-permute-start(bf16[256,2048]{1,0:T(8,128)(2,1)} %collective-permute-done.39.refs_1_), channel_id=1, source_target_pairs={{0,2},{2,0},{1,3},{3,1},{4,6},{6,4},{5,7},{7,5},{8,10},{10,8},{9,1... | collective-permute-start | bytes 3145736 | tf_op jit(solution)/shard_map/ppermute | solution.py:29
  438.5 25.3 %collective-permute-start.44 = (bf16[256,2048]{1,0:T(8,128)(2,1)}, bf16[256,2048]{1,0:T(8,128)(2,1)S(1)}, u32[]{:S(2)}, u32[]{:S(2)}) collective-permute-start(bf16[256,2048]{1,0:T(8,128)(2,1)} %collective-permute-done.41.refs_3_), channel_id=1, source_target_pairs={{0,16},{8,24},{16,0},{24,8},{1,17},{9,25},{17,1},{25,9},{2,18},{10... | collective-permute-start | bytes 3145736 | tf_op jit(solution)/shard_map/ppermute | solution.py:29
  461.7 27.0 %collective-permute-start.46 = (bf16[256,768]{1,0:T(8,128)(2,1)S(1)}, bf16[256,768]{1,0:T(8,128)(2,1)S(1)}, u32[]{:S(2)}, u32[]{:S(2)}) collective-permute-start(bf16[256,768]{1,0:T(8,128)(2,1)S(1)} %slice.510), channel_id=1, source_target_pairs={{0,16},{8,24},{16,0},{24,8},{1,17},{9,25},{17,1},{25,9},{2,18},{10... | collective-permute-start | bytes 1179656 | tf_op jit(solution)/shard_map/ppermute | solution.py:29
  464.8 23.8 %collective-permute-start.45 = (bf16[256,640]{1,0:T(8,128)(2,1)S(1)}, bf16[256,640]{1,0:T(8,128)(2,1)S(1)}, u32[]{:S(2)}, u32[]{:S(2)}) collective-permute-start(bf16[256,640]{1,0:T(8,128)(2,1)S(1)} %slice.509), channel_id=1, source_target_pairs={{0,8},{8,0},{16,24},{24,16},{1,9},{9,1},{17,25},{25,17},{2,10},{10... | collective-permute-start | bytes 983048 | tf_op jit(solution)/shard_map/ppermute | solution.py:29
  466.1 22.6 %collective-permute-start.47 = (bf16[256,640]{1,0:T(8,128)(2,1)S(1)}, bf16[256,640]{1,0:T(8,128)(2,1)S(1)}, u32[]{:S(2)}, u32[]{:S(2)}) collective-permute-start(bf16[256,640]{1,0:T(8,128)(2,1)S(1)} %slice.511), channel_id=1, source_target_pairs={{0,2},{2,0},{1,3},{3,1},{4,6},{6,4},{5,7},{7,5},{8,10},{10,8},{9,1... | collective-permute-start | bytes 983048 | tf_op jit(solution)/shard_map/ppermute | solution.py:29
  514.5 20.8 %collective-permute-start.53 = (bf16[256,2048]{1,0:T(8,128)(2,1)S(1)}, bf16[256,2048]{1,0:T(8,128)(2,1)}, u32[]{:S(2)}, u32[]{:S(2)}) collective-permute-start(bf16[256,2048]{1,0:T(8,128)(2,1)S(1)} %pad_maximum_fusion.14), channel_id=1, source_target_pairs={{0,16},{8,24},{16,0},{24,8},{1,17},{9,25},{17,1},{25,9},{2,18},{10... | collective-permute-start | bytes 3145736 | tf_op jit(solution)/shard_map/ppermute | solution.py:29
  539.8 239.8 %reduce-scatter.5.cloned.1.call-start = ((), (), s32[]{:S(2)}) async-start(), calls=%async_computation.10 | async-start | bytes 5242880 | tf_op jit(solution)/shard_map/reduce_scatter | solution.py:1110
  569.9 20.7 %collective-permute-start.58 = (bf16[256,2048]{1,0:T(8,128)(2,1)}, bf16[256,2048]{1,0:T(8,128)(2,1)}, u32[]{:S(2)}, u32[]{:S(2)}) collective-permute-start(bf16[256,2048]{1,0:T(8,128)(2,1)} %get-tuple-element.217), channel_id=1, source_target_pairs={{0,16},{8,24},{16,0},{24,8},{1,17},{9,25},{17,1},{25,9},{2,18},{10... | collective-permute-start | bytes 3145736 | tf_op jit(solution)/shard_map/ppermute | solution.py:29
  569.9 21.9 %collective-permute-start.57 = (bf16[256,2048]{1,0:T(8,128)(2,1)}, bf16[256,2048]{1,0:T(8,128)(2,1)}, u32[]{:S(2)}, u32[]{:S(2)}) collective-permute-start(bf16[256,2048]{1,0:T(8,128)(2,1)} %get-tuple-element.217), channel_id=1, source_target_pairs={{0,8},{8,0},{16,24},{24,16},{1,9},{9,1},{17,25},{25,17},{2,10},{10... | collective-permute-start | bytes 3145736 | tf_op jit(solution)/shard_map/ppermute | solution.py:29
  694.6 27.5 %all-to-all-start.2 = ((f32[32,1,256]{2,1,0:T(1,128)}), f32[32,1,256]{2,1,0:T(1,128)S(1)}, u32[]{:S(2)}, u32[]{:S(2)}) async-start(f32[32,1,256]{2,1,0:T(1,128)} %reshape.416), calls=%async_computation.2 | async-start | bytes 65536 | tf_op jit(solution)/shard_map/all_to_all | solution.py:1170
  709.7 26.9 %collective-permute-start.67 = (bf16[256,1024]{1,0:T(8,128)(2,1)}, bf16[256,1024]{1,0:T(8,128)(2,1)}, u32[]{:S(2)}, u32[]{:S(2)}) collective-permute-start(bf16[256,1024]{1,0:T(8,128)(2,1)} %get-tuple-element.307), channel_id=1, source_target_pairs={{0,2},{2,0},{1,3},{3,1},{4,6},{6,4},{5,7},{7,5},{8,10},{10,8},{9,1... | collective-permute-start | bytes 1572872 | tf_op jit(solution)/shard_map/ppermute | solution.py:29
  711.2 37.2 %collective-permute-start.68 = (bf16[256,1024]{1,0:T(8,128)(2,1)}, bf16[256,1024]{1,0:T(8,128)(2,1)}, u32[]{:S(2)}, u32[]{:S(2)}) collective-permute-start(bf16[256,1024]{1,0:T(8,128)(2,1)} %get-tuple-element.306), channel_id=1, source_target_pairs={{0,4},{4,0},{1,5},{5,1},{2,6},{6,2},{3,7},{7,3},{8,12},{12,8},{9,1... | collective-permute-start | bytes 1572872 | tf_op jit(solution)/shard_map/ppermute | solution.py:29
  748.4 74.0 %all-to-all-start.3 = ((bf16[8,64,2048]{2,1,0:T(8,128)(2,1)}), bf16[8,64,2048]{2,1,0:T(8,128)(2,1)S(1)}, u32[]{:S(2)}, u32[]{:S(2)}) async-start(bf16[8,64,2048]{2,1,0:T(8,128)(2,1)} %reduce-scatter.3.cloned.1.call-done), calls=%async_computation.4 | async-start | bytes 4194304 | tf_op jit(solution)/shard_map/all_to_all | solution.py:1173
  758.9 40.0 %collective-permute-start.74 = (bf16[256,2048]{1,0:T(8,128)(2,1)}, bf16[256,2048]{1,0:T(8,128)(2,1)}, u32[]{:S(2)}, u32[]{:S(2)}) collective-permute-start(bf16[256,2048]{1,0:T(8,128)(2,1)} %pad_maximum_fusion.24), channel_id=1, source_target_pairs={{0,16},{8,24},{16,0},{24,8},{1,17},{9,25},{17,1},{25,9},{2,18},{10... | collective-permute-start | bytes 3145736 | tf_op jit(solution)/shard_map/ppermute | solution.py:29
  763.2 36.7 %collective-permute-start.73 = (bf16[256,2048]{1,0:T(8,128)(2,1)}, bf16[256,2048]{1,0:T(8,128)(2,1)}, u32[]{:S(2)}, u32[]{:S(2)}) collective-permute-start(bf16[256,2048]{1,0:T(8,128)(2,1)} %pad_maximum_fusion.23), channel_id=1, source_target_pairs={{0,8},{8,0},{16,24},{24,16},{1,9},{9,1},{17,25},{25,17},{2,10},{10... | collective-permute-start | bytes 3145736 | tf_op jit(solution)/shard_map/ppermute | solution.py:29
  766.9 47.2 %collective-permute-start.72 = (bf16[256,2048]{1,0:T(8,128)(2,1)}, bf16[256,2048]{1,0:T(8,128)(2,1)}, u32[]{:S(2)}, u32[]{:S(2)}) collective-permute-start(bf16[256,2048]{1,0:T(8,128)(2,1)} %pad_maximum_fusion.22), channel_id=1, source_target_pairs={{0,4},{4,0},{1,5},{5,1},{2,6},{6,2},{3,7},{7,3},{8,12},{12,8},{9,1... | collective-permute-start | bytes 3145736 | tf_op jit(solution)/shard_map/ppermute | solution.py:29
  770.6 51.8 %collective-permute-start.71 = (bf16[256,2048]{1,0:T(8,128)(2,1)}, bf16[256,2048]{1,0:T(8,128)(2,1)}, u32[]{:S(2)}, u32[]{:S(2)}) collective-permute-start(bf16[256,2048]{1,0:T(8,128)(2,1)} %pad_maximum_fusion.21), channel_id=1, source_target_pairs={{0,2},{2,0},{1,3},{3,1},{4,6},{6,4},{5,7},{7,5},{8,10},{10,8},{9,1... | collective-permute-start | bytes 3145736 | tf_op jit(solution)/shard_map/ppermute | solution.py:29
  (151 other events, 1911.0 us)
Sparse Core Ops, SparseCore 0:
  148.8 105.4 all-gather.2
  255.9 56.8 all-gather.4
  539.9 116.2 reduce-scatter.2
  659.9 89.5 reduce-scatter.4

commit v3 on v2

--- a/solution.py
+++ b/solution.py
@@ -111,14 +111,19 @@
     def __init__(self, pieces, dims):
         self.dims, self.size, self.pieces = dims, len(dims), list(pieces)
         self.got, self.new = {m: [] for m in range(len(self.pieces))}, []
+        self.sums = None
+
+    def ready(self):
+        masks = [m for m in by_size(len(self.dims)) if bin(m).count("1") == self.size]
+        self.sums = {m: self.total(m) for m in masks}
+        return self
 
     def step(self):
         count = len(self.dims)
-        self.new = []
-        for which in by_size(count):
-            if bin(which).count("1") != self.size:
-                continue
-            total = self.total(which)
+        if self.sums is None:
+            self.ready()
+        sums, self.sums, self.new = self.sums, None, []
+        for which, total in sums.items():
             if self.size == count and count > 1:
                 for i, cols in enumerate(column_parts(total, count)):
                     self.keep(which ^ (1 << i), i, swap(cols, self.dims[i]))
@@ -147,9 +152,14 @@
         return total.astype(bf16)
 
     def fresh(self):
+        if self.sums is not None:
+            return list(self.sums.values())
         return [self.got[which][i][1] for which, i in self.new]
 
     def renew(self, values):
+        if self.sums is not None:
+            self.sums = dict(zip(self.sums, values, strict=True))
+            return
         for (which, i), value in zip(self.new, values, strict=True):
             self.got[which][i] = (self.got[which][i][0], value)
 
@@ -346,21 +356,21 @@
     return back * gain, jnp.sum(product * gain, -1, keepdims=True), jnp.sum(product, 0, keepdims=True)
 
 
-def block_scores(scale, last, a, j, q, k, row_ids, col_ids):
-    scores = dot_t(q, k) * scale
+def block_scores(scale, last, a, j, k, q, key_ids, query_ids):
+    scores = dot_t(k, q) * scale
     allowed = None
     if j == 0 or a == last:
-        allowed = row_ids == col_ids
+        allowed = key_ids == query_ids
     if j == a:
         shape = scores.shape
-        causal = lax.broadcasted_iota(jnp.int32, shape, 0) >= lax.broadcasted_iota(jnp.int32, shape, 1)
+        causal = lax.broadcasted_iota(jnp.int32, shape, 0) <= lax.broadcasted_iota(jnp.int32, shape, 1)
         allowed = causal if allowed is None else allowed & causal
     return scores if allowed is None else jnp.where(allowed, scores, masked_score)
 
 
 def forward_kernel(
     scale, count, tok, place, q_raw, k_raw, v_raw, q_inv, k_inv, q_gain, k_gain, cosine, sine,
-    row_ids, col_ids, out, low, log_total, k_all, v_all,
+    row_ids, col_ids, out, low, log_total, k_all, v_across,
 ):
     rows = lambda j: pl.ds(pl.multiple_of((place[0] ^ j) * tok, tok), tok)
     cols = lambda j: slice(j * tok, (j + 1) * tok)
@@ -368,26 +378,26 @@
         here = rows(a)
         table = (cosine[cols(a), :], sine[cols(a), :])
         k_all[cols(a), :] = turned(k_raw[here, :], k_inv[0, here, :], k_gain[...], *table).astype(bf16)
-        v_all[cols(a), :] = v_raw[here, :].astype(bf16)
+        v_across[:, cols(a)] = v_raw[here, :].T.astype(bf16)
         q = turned(q_raw[here, :], q_inv[0, here, :], q_gain[...], *table).astype(bf16)
         scores = [
-            block_scores(scale, count - 1, a, j, q, k_all[cols(j), :], row_ids[here, :], col_ids[j])
+            block_scores(scale, count - 1, a, j, k_all[cols(j), :], q, row_ids[rows(j), :], col_ids[a])
             for j in range(a + 1)
         ]
-        top = jnp.max(functools.reduce(jnp.maximum, scores), axis=-1, keepdims=True)
+        top = jnp.max(functools.reduce(jnp.maximum, scores), axis=0, keepdims=True)
         expo = [jnp.exp2(block - top) for block in scores]
-        total = jnp.sum(functools.reduce(jnp.add, expo), axis=-1, keepdims=True)
-        parts = [dot(expo[j].astype(bf16), v_all[cols(j), :]) for j in range(a + 1)]
-        attended = functools.reduce(jnp.add, parts) * (1.0 / total)
+        total = jnp.sum(functools.reduce(jnp.add, expo), axis=0, keepdims=True)
+        parts = [dot(v_across[:, cols(j)], expo[j].astype(bf16)) for j in range(a + 1)]
+        attended = (functools.reduce(jnp.add, parts) * (1.0 / total)).T
         out[here, :] = attended
         low[here, :] = attended.astype(bf16)
-        log_total[0, here, :] = top + jnp.log2(total)
+        log_total[0, place[0] ^ a] = top + jnp.log2(total)
 
 
 def backward_kernel(
     scale, plain_scale, count, tok, place, q_raw, k_raw, v_raw, q_inv, k_inv, q_gain, k_gain,
     cosine, sine, row_ids, col_ids, d_out, out, log_total,
-    e_q, e_k, d_v, q_sum, k_sum, q_gain_grad, k_gain_grad, k_all, v_all, d_k_all, d_v_all,
+    e_q, e_k, d_v, q_sum, k_sum, q_gain_grad, k_gain_grad, k_all, k_across, v_all, d_k_all, d_v_all,
 ):
     rows = lambda j: pl.ds(pl.multiple_of((place[0] ^ j) * tok, tok), tok)
     cols = lambda j: slice(j * tok, (j + 1) * tok)
@@ -401,22 +411,27 @@
     for a in range(count):
         here = rows(a)
         table = (cosine[cols(a), :], sine[cols(a), :])
-        k_all[cols(a), :] = turned(k_raw[here, :], k_inv[0, here, :], k_gain[...], *table).astype(bf16)
+        k = turned(k_raw[here, :], k_inv[0, here, :], k_gain[...], *table)
+        k_all[cols(a), :] = k.astype(bf16)
+        k_across[:, cols(a)] = k.T.astype(bf16)
         v_all[cols(a), :] = v_raw[here, :].astype(bf16)
         q_row, inverse = q_raw[here, :], q_inv[0, here, :]
         q = turned(q_row, inverse, q_gain[...], *table).astype(bf16)
         d_blk = d_out[here, :]
         row_dot = jnp.sum(d_blk.astype(f32) * out[here, :], axis=-1, keepdims=True)
+        row_dot = jnp.broadcast_to(row_dot, q_row.shape).T[0:1, :]
+        log_row = log_total[0, place[0] ^ a]
         d_q = []
         for j in range(a + 1):
-            k = k_all[cols(j), :]
-            scores = block_scores(scale, count - 1, a, j, q, k, row_ids[here, :], col_ids[j])
-            probability = jnp.exp2(scores - log_total[0, here, :])
-            d_prob = dot_t(d_blk, v_all[cols(j), :])
+            scores = block_scores(
+                scale, count - 1, a, j, k_all[cols(j), :], q, row_ids[rows(j), :], col_ids[a]
+            )
+            probability = jnp.exp2(scores - log_row)
+            d_prob = dot_t(v_all[cols(j), :], d_blk)
             d_scores = (probability * (d_prob - row_dot)).astype(bf16)
-            d_q.append(dot(d_scores, k))
-            d_k = t_dot(d_scores, q)
-            d_v_part = t_dot(probability.astype(bf16), d_blk)
+            d_q.append(dot(k_across[:, cols(j)], d_scores))
+            d_k = dot(d_scores, q)
+            d_v_part = dot(probability.astype(bf16), d_blk)
             if j == a:
                 d_k_all[cols(j), :] = d_k
                 d_v_all[cols(j), :] = d_v_part
@@ -424,7 +439,7 @@
                 d_k_all[cols(j), :] += d_k
                 d_v_all[cols(j), :] += d_v_part
         e_q[here, :], row_sum, gain_grad = turned_back(
-            functools.reduce(jnp.add, d_q) * plain_scale, q_row, inverse, q_gain[...], *table
+            functools.reduce(jnp.add, d_q).T * plain_scale, q_row, inverse, q_gain[...], *table
         )
         q_sum[0, here, :] += row_sum
         q_gain_grad[...] += gain_grad
@@ -448,7 +463,7 @@
     inputs = [head(0), head(1), head(2), inverse(0), inverse(1), vector, vector]
     inputs += [whole((tokens, head_dim))] * 2
     inputs += [whole((tokens, 1)), whole((tokens // block, 1, block))]
-    logs = pl.BlockSpec((1, tokens, 1), lambda h, s: (h, 0, 0))
+    logs = pl.BlockSpec((1, tokens // block, 1, block), lambda h, s: (h, 0, 0, 0))
     return inputs, head(0), logs, vector
 
 
@@ -464,12 +479,15 @@
             grid=(heads,),
             in_specs=inputs,
             out_specs=[head, head, logs],
-            scratch_shapes=[pltpu.VMEM((tokens, head_dim), bf16)] * 2,
+            scratch_shapes=[
+                pltpu.VMEM((tokens, head_dim), bf16),
+                pltpu.VMEM((head_dim, tokens), bf16),
+            ],
         ),
         out_shape=[
             jax.ShapeDtypeStruct((tokens, width), f32),
             jax.ShapeDtypeStruct((tokens, width), bf16),
-            jax.ShapeDtypeStruct((heads, tokens, 1), f32),
+            jax.ShapeDtypeStruct((heads, tokens // block, 1, block), f32),
         ],
         compiler_params=pltpu.CompilerParams(vmem_limit_bytes=40 * 1024 * 1024),
         cost_estimate=pl.CostEstimate(
@@ -497,8 +515,13 @@
             grid=(heads,),
             in_specs=inputs + [head, head, logs],
             out_specs=[head, head, head, sums, sums, vector, vector],
-            scratch_shapes=[pltpu.VMEM((tokens, head_dim), bf16)] * 2
-            + [pltpu.VMEM((tokens, head_dim), f32)] * 2,
+            scratch_shapes=[
+                pltpu.VMEM((tokens, head_dim), bf16),
+                pltpu.VMEM((head_dim, tokens), bf16),
+                pltpu.VMEM((tokens, head_dim), bf16),
+                pltpu.VMEM((tokens, head_dim), f32),
+                pltpu.VMEM((tokens, head_dim), f32),
+            ],
         ),
         out_shape=[
             jax.ShapeDtypeStruct((tokens, width), f32),
@@ -521,18 +544,14 @@
     return 1.0 / (1.0 + jnp.exp(-values))
 
 
-def feed_kernel(with_down, masks, tok, steps, refs):
+def feed_kernel(masks, tok, steps, refs):
     number = len(masks)
     pieces, refs = refs[:number], refs[number:]
-    down = refs[2] if with_down else None
-    w_gate, w_up, refs = refs[0], refs[1], refs[2 + with_down :]
-    h_all, middle_all, refs = refs[0], refs[1], refs[2:]
-    gates, ups, refs = refs[:number], refs[number : 2 * number], refs[2 * number :]
-    partials, refs = refs[: len(refs) - 3 - with_down], refs[len(refs) - 3 - with_down :]
-    held_h, held_middle, sems = refs[0], refs[1], refs[-1]
-    held_down = refs[2] if with_down else None
+    w_gate, w_up, h_all, middle_all, refs = *refs[:4], refs[4:]
+    slopes, silus, refs = refs[:number], refs[number : 2 * number], refs[2 * number :]
+    held_h, held_middle, sems = refs
     at = pl.program_id(0)
-    part = gates[0].shape[1]
+    part = slopes[0].shape[1]
     block = lambda i: pl.ds(i * tok, tok)
     copies = lambda held, whole, first: [
         pltpu.make_async_copy(held.at[block(i)], whole.at[block(m)], sems.at[first + i])
@@ -542,11 +561,10 @@
         pltpu.make_async_copy(pieces[i], held_h.at[block(i)], sems.at[i]) for i in range(number)
     ]
     keep_h, keep_middle = copies(held_h, h_all, number), copies(held_middle, middle_all, 2 * number)
-    weights = [pltpu.make_async_copy(down, held_down, sems.at[3 * number])] if with_down else []
 
     @pl.when(at == 0)
     def _():
-        for copy in arrive + weights:
+        for copy in arrive:
             copy.start()
         for copy in arrive:
             copy.wait()
@@ -555,10 +573,13 @@
 
     gate_act = dot(held_h[...], w_gate[...])
     up_act = dot(held_h[...], w_up[...])
-    middle = (gate_act * sigmoid(gate_act) * up_act).astype(bf16)
+    sig = sigmoid(gate_act)
+    silu = gate_act * sig
+    middle = (silu * up_act).astype(bf16)
+    slope = up_act * (sig + silu * (1.0 - sig))
     for i in range(number):
-        gates[i][...] = gate_act[i * tok : (i + 1) * tok].astype(bf16)
-        ups[i][...] = up_act[i * tok : (i + 1) * tok].astype(bf16)
+        slopes[i][...] = slope[i * tok : (i + 1) * tok].astype(bf16)
+        silus[i][...] = silu[i * tok : (i + 1) * tok].astype(bf16)
     for step in range(steps):
 
         @pl.when(at == step)
@@ -569,10 +590,6 @@
     def _():
         for copy in keep_middle:
             copy.start()
-        for copy in weights:
-            copy.wait()
-        for i, out in enumerate(partials):
-            out[...] = dot(held_middle[i * tok : (i + 1) * tok, :], held_down[...]).astype(bf16)
         for copy in keep_h + keep_middle:
             copy.wait()
 
@@ -580,11 +597,11 @@
 def feed_back_kernel(masks, tok, steps, refs):
     number = len(masks)
     pieces, refs = refs[:number], refs[number:]
-    gates, ups, refs = refs[:number], refs[number : 2 * number], refs[2 * number :]
+    slopes, silus, refs = refs[:number], refs[number : 2 * number], refs[2 * number :]
     down, w_gu, d_ff_all, d_gate_all, d_up_all = refs[:5]
     partials, (held_d, held_gu, held_w, sems) = refs[5 : 5 + number], refs[5 + number :]
     at = pl.program_id(0)
-    part = gates[0].shape[1]
+    part = slopes[0].shape[1]
     units = steps * part
     block = lambda i: pl.ds(i * tok, tok)
     arrive, keep_d, keep_gu = [], [], []
@@ -613,10 +630,8 @@
     d_gates, d_ups = [], []
     for i in range(number):
         d_middle = d_middle_all[i * tok : (i + 1) * tok]
-        gate_act, up_act = gates[i][...].astype(f32), ups[i][...].astype(f32)
-        sig = sigmoid(gate_act)
-        d_gates.append((d_middle * up_act * (sig * (1.0 + gate_act * (1.0 - sig)))).astype(bf16))
-        d_ups.append((d_middle * (gate_act * sig)).astype(bf16))
+        d_gates.append((d_middle * slopes[i][...].astype(f32)).astype(bf16))
+        d_ups.append((d_middle * silus[i][...].astype(f32)).astype(bf16))
     for step in range(steps):
 
         @pl.when(at == step)
@@ -631,8 +646,12 @@
         for copy in keep_gu:
             copy.start()
         weights.wait()
-        for i in range(number):
-            partials[i][...] = dot_t(held_gu[i * tok : (i + 1) * tok, :], held_w[...]).astype(bf16)
+        width = held_d.shape[1]
+        cols = math.gcd(width, 512)
+        for n in range(0, width, cols):
+            product = dot_t(held_gu[...], held_w[n : n + cols, :]).astype(bf16)
+            for i, out in enumerate(partials):
+                out[:, n : n + cols] = product[i * tok : (i + 1) * tok]
         for copy in keep_d + keep_gu:
             copy.wait()
 
@@ -674,7 +693,7 @@
     )(*pieces, *ins, *earlier)
 
 
-def feed(pieces, masks, total, w_gu, down, earlier):
+def feed(pieces, masks, total, w_gu, earlier):
     width, units = w_gu.shape[0], w_gu.shape[1] // 2
     part = math.gcd(units, 256)
     steps = units // part
@@ -684,16 +703,11 @@
         pl.BlockSpec((width, part), lambda j: (0, j)),
         pl.BlockSpec((width, part), lambda j: (0, steps + j)),
     ]
-    ins, scratch, given = [w_gu, w_gu], [(rows, units)], 0
-    if down is not None:
-        specs.append(pl.BlockSpec(memory_space=pl.ANY))
-        ins, scratch, given = ins + [down], scratch + [(units, width)], number
     outs = feed_call(
-        functools.partial(feed_kernel, int(down is not None)), "feed", pieces, masks, total, ins,
-        specs, earlier, (width, units), (steps, part), (2 * number, given, scratch),
+        feed_kernel, "feed", pieces, masks, total, [w_gu, w_gu], specs, earlier,
+        (width, units), (steps, part), (2 * number, 0, [(rows, units)]),
     )
-    acts = list(zip(outs[2 : 2 + number], outs[2 + number : 2 + 2 * number], strict=True))
-    return outs[:2], acts, outs[2 + 2 * number :]
+    return outs[:2], list(zip(outs[2 : 2 + number], outs[2 + number :], strict=True))
 
 
 def feed_down(middle_all, masks, tok, down):
@@ -740,7 +754,7 @@
         pl.BlockSpec((part, width), lambda j: (j, 0)),
         pl.BlockSpec(memory_space=pl.ANY),
     ]
-    ins = [gate for gate, _ in acts] + [up for _, up in acts] + [down, w_gu]
+    ins = [slope for slope, _ in acts] + [silu for _, silu in acts] + [down, w_gu]
     outs = feed_call(
         feed_back_kernel, "feed_back", pieces, masks, total, ins, specs, earlier,
         (width, units, units), (steps, part), (0, number, [(rows, 2 * units), (width, 2 * units)]),
@@ -988,6 +1002,8 @@
     ]
     hi_order = [lo_order.index(i) for i in range(len(lo_order))]
 
+    tables = rope_tables(jnp.arange(length, dtype=jnp.int32), head_dim)
+
     qkv_mine = pack_columns((w_query, w_key, w_value), n_seq)
     gains = jnp.stack([query_gain, key_gain, attn_gain, ff_gain])[None]
     gains = gather_row(after(gains, qkv_mine), core_dims + z_dims)
@@ -1003,30 +1019,29 @@
     more = jnp.concatenate([ids, to_width(gains), jnp.zeros((14, width), bf16)], axis=0)
     x_spread = Spread(jnp.concatenate([inputs, more], axis=0), seq_dims).step()
     x_pieces = x_spread.whole()
-    x_pieces = tie(w_z, *x_pieces)
+    tables, *x_pieces = tie(w_z, tables, *x_pieces)
     w_sib = [core_swap(piece) for piece in (w_z.pieces[0], *w_z.fresh())]
     early = len(w_sib)
     w_z.step()
-    (w_sib,) = tie(w_z, w_sib)
-    w_z = w_z.whole()
-    w_sib = w_sib + [core_swap(piece) for piece in w_z[early:]]
-
-    gu_mine = lax.all_to_all(after(gu_mine, w_z), ("seq", "zlo"), 0, 0, tiled=True)
-
-    row_ids = jnp.concatenate([piece[tok, :tok] for piece in x_pieces]).astype(jnp.int32)
+    small = after(x_pieces, w_z.fresh())
+    row_ids = jnp.concatenate([piece[tok, :tok] for piece in small]).astype(jnp.int32)
     row_ids = row_ids.reshape(length, 1)
     col_ids = jnp.stack(
         [lax.dynamic_slice(row_ids, ((seq ^ m) * tok, 0), (tok, 1)) for m in range(n_seq)]
     ).reshape(n_seq, 1, tok)
-    tables = rope_tables(jnp.arange(length, dtype=jnp.int32), head_dim)
-    all_gains = jnp.concatenate([piece[tok + 1 : tok + 2, : 4 * part] for piece in x_pieces], axis=0)
+    all_gains = jnp.concatenate([piece[tok + 1 : tok + 2, : 4 * part] for piece in small], axis=0)
     all_gains = jnp.concatenate(
         [lax.dynamic_slice(all_gains, (seq ^ m, 0), (1, 4 * part)) for m in range(n_seq)], axis=0
     ).reshape(n_seq, 4, part)
     all_gains = jnp.transpose(all_gains, (1, 0, 2)).reshape(4, width).astype(f32)
     my_gains = gains.reshape(4, 1, part).astype(f32)
     qk_gains = (my_gains[0], my_gains[1])
+    (w_sib,) = tie(w_z, w_sib)
     gain_attn, gain_ff = all_gains[2], all_gains[3]
+    w_z = w_z.whole()
+    w_sib = w_sib + [core_swap(piece) for piece in w_z[early:]]
+
+    gu_mine = lax.all_to_all(after(gu_mine, w_z), ("seq", "zlo"), 0, 0, tiled=True)
 
     raw, squares, x_all, w_qkv, out_weight = project(
         x_pieces,
@@ -1048,12 +1063,11 @@
         tok,
         part,
     )
+    squares, gu_mine = tie(squares, gu_mine)
+    w_gu = lax.all_gather(gu_mine, pair_axes, axis=0, tiled=True)
     squares = squares.reshape(2, n_seq, tok)
     squares = sum_all(jnp.transpose(squares, (1, 0, 2)), seq_dims)
     inverse = lax.rsqrt(jnp.transpose(squares, (1, 0, 2)).reshape(2, length, 1) / width + norm_eps)
-    inverse, gu_mine = tie(inverse, gu_mine)
-    w_gu = lax.all_gather(gu_mine, pair_axes, axis=0, tiled=True)
-    down = lax.all_gather(after(w_down, gu_mine), pair_axes, axis=0, tiled=True)
 
     context = (seq.astype(jnp.int32).reshape(1), raw, inverse, qk_gains, tables, (row_ids, col_ids))
     attended, attn_low, log_total = attend(context, heads, tok)
@@ -1073,19 +1087,28 @@
     groups = [masks for size in range(1, len(cube_dims) + 1) for masks in fours(by_bits(size))]
     light = total == 8
     h_spread = Spread(hidden_low, cube_dims, spare_last=light).step()
-    acts, partials, kept, late = {}, {}, (), []
-    for i, masks in enumerate([[0, 1, 2, 3], [4, 5, 6], [7]] if light else groups):
+    if light:
+        h_spread.step()
+        near = [h_spread.pieces[m] for m in (1, 2, 3)]
+        near, w_gu = tie(near, w_gu)
+        h_spread.pieces.update(zip((1, 2, 3), near, strict=True))
+    acts, partials, kept = {}, {}, ()
+    order = [[0, 1], [2, 3], [4, 5, 6], [7]] if light else groups
+    for i, masks in enumerate(order):
         while any(m not in h_spread.pieces for m in masks):
             h_spread.step()
         pieces = [h_spread.pieces[m] for m in masks]
-        kept, act, sums = feed(pieces, masks, total, w_gu, down if i else None, kept)
+        kept, act = feed(pieces, masks, total, w_gu, kept)
+        if i == 0:
+            last = h_spread.pieces[total // 2] = after(h_spread.pieces[total // 2], act)
+            down = lax.all_gather(after(w_down, last), pair_axes, axis=0, tiled=True)
+        if light and i == 1:
+            (act,) = tie(h_spread.step(), act)
         acts.update(zip(masks, act, strict=True))
-        late += [] if i else masks
-        partials.update(zip(masks if i else [], sums, strict=True))
-        if light and i == 0:
-            h_spread.pieces[4] = after(h_spread.pieces[4], act)
     h_all, middle_all = kept
-    partials.update(zip(late, feed_down(middle_all, late, tok, down), strict=True))
+    for masks in fours(sorted(range(total), key=lambda m: -bin(m).count("1"))):
+        sums = feed_down(middle_all, masks, tok, down)
+        partials.update(zip(masks, sums, strict=True))
     partials = [partials[m] for m in range(total)]
     ff_raw = Collect(partials, cube_dims).whole()
     ff_norm, ff_inv = rms(ff_raw)
@@ -1108,8 +1131,12 @@
     d_hidden = Collect(partials, cube_dims).step()
 
     owned = lambda grad: lax.psum_scatter(grad, pair_axes, scatter_dimension=0, tiled=True)
+    grad_down = t_dot(middle_all, after(d_ff_all, partials)).astype(bf16)
+    (grad_down,) = tie(d_hidden, grad_down)
+    grad_down = owned(grad_down)
     order = (n_seq, n_hi, n_lo, n_core)
-    grad_gu = owner_grad(h_all, after(d_gate_all, partials), order, d_rows, 0, [])
+    d_hidden.step()
+    grad_gu = owner_grad(h_all, d_gate_all, order, d_rows, 0, [])
     (grad_gu,) = tie(d_hidden, grad_gu)
     d_hidden.step()
     grad_gu = owner_grad(h_all, after(d_up_all, grad_gu), order, d_rows, 1, [grad_gu])
@@ -1121,9 +1148,7 @@
     grad_attn_gain = jnp.sum(d_hidden * branch_norm, axis=0)
     d_branch = rms_back(d_hidden, branch_norm, branch_inv, gain_attn).astype(bf16)
     d_branch_pieces = Spread(d_branch, seq_dims).whole()
-    grad_down = t_dot(middle_all, after(d_ff_all, d_branch)).astype(bf16)
     d_branch_pieces, grad_down = tie(d_branch_pieces, grad_down)
-    grad_down = owned(grad_down).astype(f32)
     d_attended = jnp.concatenate(
         [dot_t(piece, out_weight).astype(bf16) for piece in d_branch_pieces], axis=0
     )
@@ -1142,46 +1167,47 @@
         z_dims + core_dims,
         z_axes,
     )
-    d_branch_all = jnp.concatenate(d_branch_pieces, axis=0)
-    grad_out = t_dot(attn_low, after(d_branch_all, d_value)).astype(bf16)
-    grad_out = jnp.concatenate([grad_out[:, i * part : (i + 1) * part] for i in range(n_seq)], axis=0)
-    means, grad_out = tie(means, grad_out)
+    def to_core(grad):
+        blocks = z_blocks(grad)
+        theirs = [core_swap(piece) for piece in blocks[n_z:]]
+        return [
+            add_low(a, b).reshape(-1, a.shape[-1]) for a, b in zip(blocks[:n_z], theirs, strict=True)
+        ]
+
     d_qkv = finish(e_query, e_key, raw, inverse, means, d_value, part, tok)
     grad_qkv = t_dot(x_all, d_qkv).astype(bf16)
-    both = [
-        jnp.concatenate([a, b], axis=-1)
-        for a, b in zip(z_blocks(grad_qkv), z_blocks(grad_out), strict=True)
-    ]
-    theirs = [core_swap(piece) for piece in both[n_z:]]
-    low_rows, theirs = tie(d_qkv, theirs)
-    input_grad = Collect(
-        [held(dot_t(rows_of(low_rows, m), w_qkv).astype(bf16)) for m in range(n_seq)], seq_dims
-    )
-    both = [
-        add_low(a, b).reshape(-1, 4 * part) for a, b in zip(both[:n_z], theirs, strict=True)
-    ]
-    both = Collect(both, z_dims).step()
+    back = lambda rows, m: held(dot_t(rows_of(rows, m), w_qkv).astype(bf16))
+    far = back(after(d_qkv, grad_qkv), n_seq - 1)
+    grad_qkv, far, low_rows = tie(to_core(grad_qkv), far, d_qkv)
+    grad_qkv = Collect(grad_qkv, z_dims).step()
+    low_rows, far = tie(grad_qkv, low_rows, far)
+    low_rows, far = tie(grad_qkv.ready(), low_rows, far)
+    grad_qkv.step()
+    input_grad = Collect([back(low_rows, m) for m in range(n_seq - 1)] + [far], seq_dims)
     input_grad.step()
     full_row = lambda cols: lax.dynamic_update_slice(jnp.zeros((width,), f32), cols, (seq * part,))
     rows = jnp.stack(
         [full_row(grad_query_gain[0]), full_row(grad_key_gain[0]), grad_attn_gain, grad_ff_gain]
     )
     rows = jnp.transpose(rows.reshape(4, n_dev, d_rows), (1, 0, 2))
-    rows = lax.all_to_all(after(rows, low_rows), ("seq",) + z_axes, 0, 0, tiled=True)
-    rows, grad_gu = tie(both, input_grad, rows, grad_gu)
-    grad_gu = grad_gu.reshape(n_seq * n_lo, d_rows, 2 * units)
+    grad_gu = after(grad_gu, low_rows).reshape(n_seq * n_lo, d_rows, 2 * units)
     grad_gu = lax.all_to_all(grad_gu, ("seq", "zlo"), 0, 0, tiled=True)
-    rows = jnp.sum(rows, axis=0)
-    both.step()
+    d_branch_all = jnp.concatenate(after(d_branch_pieces, low_rows), axis=0)
+    grad_out = t_dot(attn_low, d_branch_all).astype(bf16)
+    grad_out = jnp.concatenate([grad_out[:, i * part : (i + 1) * part] for i in range(n_seq)], axis=0)
+    grad_out, grad_gu = tie(grad_qkv, input_grad, to_core(grad_out), grad_gu)
     input_grad.step()
-    grad_gu, grad_down, rows = tie(both, input_grad, grad_gu, grad_down, rows)
-    both = both.whole().astype(bf16).reshape(n_seq, d_rows, 4 * part)
-    grad_qkv, grad_out = both[..., : 3 * part], both[..., 3 * part :]
+    grad_qkv = grad_qkv.whole().astype(bf16).reshape(n_seq, d_rows, 3 * part)
     grad_qkv = lax.all_to_all(grad_qkv, "seq", 0, 0, tiled=True)
+    grad_out = Collect(grad_out, z_dims).step()
+    rows = lax.all_to_all(after(rows, grad_qkv), ("seq",) + z_axes, 0, 0, tiled=True)
     input_grad = d_hidden + input_grad.whole()
-    grad_out = jnp.concatenate([grad_out[i] for i in range(n_seq)], axis=1).astype(f32)
+    grad_down = after(grad_down, grad_qkv).astype(f32)
+    grad_out = grad_out.whole().reshape(n_seq, d_rows, part)
     grad_gate, grad_up = unpack_units(grad_gu, n_seq, sizes, ff_rows)
     grad_query, grad_key, grad_value = unpack_columns(grad_qkv, 3)
+    rows = jnp.sum(rows, axis=0)
+    grad_out = jnp.concatenate([grad_out[i] for i in range(n_seq)], axis=1)
 
     return (
         mixed[None],

time: 859 us -> 836 us (0.973)
  other arithmetic: 75.5 us -> 55 us
  Pallas kernels: 197 us -> 188 us
    unnamed x225 -> x251, local copies, waits for them, and re-layouts: 46.8 us -> 60.7 us
    concatenate x7 -> x3, other arithmetic: 10.2 us -> 0.88 us  [the longest x1 0.83 us: per_device(): grad_out = jnp.concatenate([grad_out[i] for i in range(n_seq)], axis=1)]
    ppermute x75 -> x83, starting transfers between devices: 86.7 us -> 91.8 us  [swap(): lax.ppermute(block, axis, [(i, i ^ mask) for i in range(lax.axis_size(axi...]
    ppermute x75 -> x83, waiting for transfers between devices: 315 us -> 311 us  [swap(): lax.ppermute(block, axis, [(i, i ^ mask) for i in range(lax.axis_size(axi...]
    pallas_call x6 -> x7, Pallas kernels: 91.6 us -> 90.9 us  [feed_call(): pl.pallas_call(body, grid=(steps,), in_specs=[somewhere] * number + in_sp...]
  transfers between devices with their start and end apart: 84 -> 92, of which waited for: 40 -> 41; matrix products, arithmetic and copies ran while one was open for 18% -> 14% of each run, Pallas kernels for 20% -> 21%
where the time goes in v3:
time: 836 us; the launch traced here: 826 us
  waiting for transfers between devices  321 us (38%)
  Pallas kernels  188 us (22%)
  starting transfers between devices  111 us (13%)
  local copies, waits for them, and re-layouts  78.8 us (9%)
  matrix products  56 us (7%)
  other arithmetic  55 us (7%)
  between operations  16.4 us (2%)
    ppermute x83, waiting for transfers between devices, swap(): lax.ppermute(block, axis, [(i, i ^ mask) for i in range(lax.axis_size(axi...  311 us
    ppermute x83, starting transfers between devices, swap(): lax.ppermute(block, axis, [(i, i ^ mask) for i in range(lax.axis_size(axi...  91.8 us
    pallas_call x7, Pallas kernels, feed_call(): pl.pallas_call(body, grid=(steps,), in_specs=[somewhere] * number + in_sp...  90.9 us
    unnamed x251, local copies, waits for them, and re-layouts  60.7 us
    dot_general x3, matrix products, t_dot(): lax.dot_general(left, right, (((0,), (0,)), ((), ())), preferred_element_...  27.3 us
    dot_general x8, matrix products, dot_t(): lax.dot_general(left, right, (((1,), (1,)), ((), ())), preferred_element_...  24.1 us
    pallas_call x2, Pallas kernels, owner_grad(): pl.pallas_call(kernel, grid=(n_seq,), in_specs=[pl.BlockSpec((tokens, col...  22.8 us
    pallas_call x1, Pallas kernels, attend_back(): pl.pallas_call(functools.partial(backward_kernel, scale * math.log2(math....  18.3 us
  transfers between devices with their start and end apart: 92, of which 41 were waited for; matrix products, arithmetic and copies ran while one was open for 14% of the time, Pallas kernels for 21%

profile of v3, /device:TPU:0, one launch (start us, length us, event | category | flops | bytes accessed | tf_op | source)
XLA Modules:
  0.0 826.1 jit_solution(5557060374693326885)
XLA Ops:
  21.9 3.9 pack_units.1
  25.9 4.1 all-to-all-done
  35.7 20.2 %collective-permute-done.6.refs_2_ = bf16[272,2048]{1,0:T(8,128)(2,1)S(1)} collective-permute-done((bf16[272,2048]{1,0:T(8,128)(2,1)S(1)}, bf16[272,2048]{1,0:T(8,128)(2,1)S(1)}, u32[]{:S(2)}, u32[]{:S(2)}) %collective-permute-start.6) | collective-permute-done | bytes 1114144 | tf_op jit(solution)/shard_map/ppermute | solution.py:29
  60.4 8.5 %collective-permute-done.7 = bf16[272,1024]{1,0:T(8,128)(2,1)S(1)} collective-permute-done((bf16[272,1024]{1,0:T(8,128)(2,1)S(1)}, bf16[272,1024]{1,0:T(8,128)(2,1)S(1)}, u32[]{:S(2)}, u32[]{:S(2)}) %collective-permute-start.7) | collective-permute-done | bytes 557088 | tf_op jit(solution)/shard_map/ppermute | solution.py:29
  69.5 9.0 %collective-permute-done.3 = bf16[256,2048]{1,0:T(8,128)(2,1)S(1)} collective-permute-done((bf16[256,2048]{1,0:T(8,128)(2,1)S(1)}, bf16[256,2048]{1,0:T(8,128)(2,1)S(1)}, u32[]{:S(2)}, u32[]{:S(2)}) %collective-permute-start.3) | collective-permute-done | bytes 1048608 | tf_op jit(solution)/shard_map/ppermute | solution.py:29
  84.5 20.2 %collective-permute-done.9 = bf16[256,1024]{1,0:T(8,128)(2,1)S(1)} collective-permute-done((bf16[256,1024]{1,0:T(8,128)(2,1)S(1)}, bf16[256,1024]{1,0:T(8,128)(2,1)S(1)}, u32[]{:S(2)}, u32[]{:S(2)}) %collective-permute-start.9) | collective-permute-done | bytes 524320 | tf_op jit(solution)/shard_map/ppermute | solution.py:29
  111.0 4.4 all-to-all-start.1
  129.6 12.9 %project.1 = (f32[1024,1536]{1,0:T(8,128)}, f32[2,1024,1]{2,1,0:T(8,128)S(1)}, bf16[1024,2048]{1,0:T(8,128)(2,1)}, bf16[2048,1536]{1,0:T(8,128)(2,1)}, bf16[512,2048]{1,0:T(8,128)(2,1)}) custom-call(s32[32]{0:T(128)S(1)} %stack.206.table, s32[8]{0:T(128)S(1)} %stack.207.out_table, bf16[272,2048]{1,0:T(8,128)(2,1)S(1)} %fusion.26.refs_0_, ...), custom_call_target="tpu_custom_call" | custom-call | flops 6442450944 | bytes 10485760 | tf_op jit(solution)/shard_map/project/pallas_call | solution.py:269
  158.7 9.9 %attend.1 = (f32[1024,512]{1,0:T(8,128)S(1)}, bf16[1024,512]{1,0:T(8,128)(2,1)S(1)}, f32[4,4,1,256]{3,2,1,0:T(1,128)S(1)}) custom-call(s32[1]{0:T(128)} %bitcast.1.place, f32[1024,1536]{1,0:T(8,128)S(1)} %copy-done, f32[1024,1536]{1,0:T(8,128)S(1)} %copy-done, f32[1024,1536]{1,0:T(8,128)S(1)} %copy-done, f32[2,1024,1]{2,1,0:T(8,128)S(1)} %rsqrt.28.q_inv.k_inv, ...), custom_call_target="tpu_custom_call" | custom-call | flops 1073741824 | bytes 9437184 | tf_op jit(solution)/shard_map/attend/pallas_call | solution.py:475
  174.8 8.3 %collective-permute-done.17 = bf16[256,1024]{1,0:T(8,128)(2,1)S(1)} collective-permute-done((bf16[256,1024]{1,0:T(8,128)(2,1)S(1)}, bf16[256,1024]{1,0:T(8,128)(2,1)S(1)}, u32[]{:S(2)}, u32[]{:S(2)}) %collective-permute-start.17) | collective-permute-done | bytes 524320 | tf_op jit(solution)/shard_map/ppermute | solution.py:29
  191.2 17.0 %collective-permute-done.18 = bf16[256,2048]{1,0:T(8,128)(2,1)} collective-permute-done((bf16[256,2048]{1,0:T(8,128)(2,1)}, bf16[256,2048]{1,0:T(8,128)(2,1)}, u32[]{:S(2)}, u32[]{:S(2)}) %collective-permute-start.18) | collective-permute-done | bytes 1048608 | tf_op jit(solution)/shard_map/ppermute | solution.py:29
  216.1 21.0 %collective-permute-done.23.refs_0_ = bf16[256,2048]{1,0:T(8,128)(2,1)S(1)} collective-permute-done((bf16[256,2048]{1,0:T(8,128)(2,1)}, bf16[256,2048]{1,0:T(8,128)(2,1)S(1)}, u32[]{:S(2)}, u32[]{:S(2)}) %collective-permute-start.23) | collective-permute-done | bytes 1048608 | tf_op jit(solution)/shard_map/ppermute | solution.py:29
  241.8 6.9 collective-permute-done.24
  257.4 10.4 %feed.4 = (bf16[2048,2048]{1,0:T(8,128)(2,1)}, bf16[2048,1024]{1,0:T(8,128)(2,1)}, bf16[256,1024]{1,0:T(8,128)(2,1)S(1)}, bf16[256,1024]{1,0:T(8,128)(2,1)S(1)},...) custom-call(bf16[256,2048]{1,0:T(8,128)(2,1)} %fusion.23.refs_0_, bf16[256,2048]{1,0:T(8,128)(2,1)} %copy-done.113, ...), custom_call_target="tpu_custom_call" | custom-call | flops 6442450944 | bytes 23068672 | tf_op jit(solution)/shard_map/feed/pallas_call | solution.py:672
  273.9 10.4 %feed.5 = (bf16[2048,2048]{1,0:T(8,128)(2,1)}, bf16[2048,1024]{1,0:T(8,128)(2,1)}, bf16[256,1024]{1,0:T(8,128)(2,1)S(1)}, bf16[256,1024]{1,0:T(8,128)(2,1)S(1)},...) custom-call(bf16[256,2048]{1,0:T(8,128)(2,1)S(1)} %copy-done.11, ...), custom_call_target="tpu_custom_call", output_to_operand_aliasing={{0}: (4, {}), {1}: (5, {})} | custom-call | flops 6442450944 | bytes 23068672 | tf_op jit(solution)/shard_map/feed/pallas_call | solution.py:672
  286.8 7.6 collective-permute-done.26.refs_1_
  297.8 13.4 %feed.6 = (bf16[2048,2048]{1,0:T(8,128)(2,1)}, bf16[2048,1024]{1,0:T(8,128)(2,1)}, bf16[256,1024]{1,0:T(8,128)(2,1)S(1)}, bf16[256,1024]{1,0:T(8,128)(2,1)S(1)},...) custom-call(bf16[256,2048]{1,0:T(8,128)(2,1)} %collective-permute-do, ...), custom_call_target="tpu_custom_call", output_to_operand_aliasing={{0}: (5, {}), {1}: (6, {})} | custom-call | flops 9663676416 | bytes 28311552 | tf_op jit(solution)/shard_map/feed/pallas_call | solution.py:672
  314.2 6.8 feed.7
  321.8 5.4 all-gather.5.cloned.1.call-done.weight.refs_12_.refs_9_.refs_3_
  331.6 5.7 feed_down.3
  340.6 5.8 feed_down.2
  352.8 20.3 %collective-permute-done.34 = bf16[256,2048]{1,0:T(8,128)(2,1)S(1)} collective-permute-done((bf16[256,2048]{1,0:T(8,128)(2,1)S(1)}, bf16[256,2048]{1,0:T(8,128)(2,1)S(1)}, u32[]{:S(2)}, u32[]{:S(2)}) %collective-permute-start.34) | collective-permute-done | bytes 1048608 | tf_op jit(solution)/shard_map/ppermute | solution.py:29
  377.3 19.7 %collective-permute-done.35 = bf16[256,2048]{1,0:T(8,128)(2,1)S(1)} collective-permute-done((bf16[256,2048]{1,0:T(8,128)(2,1)S(1)}, bf16[256,2048]{1,0:T(8,128)(2,1)S(1)}, u32[]{:S(2)}, u32[]{:S(2)}) %collective-permute-start.35) | collective-permute-done | bytes 1048608 | tf_op jit(solution)/shard_map/ppermute | solution.py:29
  405.5 19.0 %collective-permute-done.40.refs_2_ = bf16[256,2048]{1,0:T(8,128)(2,1)} collective-permute-done((bf16[256,2048]{1,0:T(8,128)(2,1)S(1)}, bf16[256,2048]{1,0:T(8,128)(2,1)}, u32[]{:S(2)}, u32[]{:S(2)}) %collective-permute-start.40) | collective-permute-done | bytes 1048608 | tf_op jit(solution)/shard_map/ppermute | solution.py:29
  430.1 22.2 %feed_back.3 = (bf16[2048,2048]{1,0:T(8,128)(2,1)}, bf16[2048,1024]{1,0:T(8,128)(2,1)}, bf16[2048,1024]{1,0:T(8,128)(2,1)}, bf16[256,2048]{1,0:T(8,128)(2,1)}, b...) custom-call(bf16[256,2048]{1,0:T(8,128)(2,1)} %copy-done.98, ...), custom_call_target="tpu_custom_call" | custom-call | flops 12884901888 | bytes 33554432 | tf_op jit(solution)/shard_map/feed_back/pallas_call | solution.py:672
  455.4 18.5 %feed_back.4 = (bf16[2048,2048]{1,0:T(8,128)(2,1)}, bf16[2048,1024]{1,0:T(8,128)(2,1)}, bf16[2048,1024]{1,0:T(8,128)(2,1)}, bf16[256,2048]{1,0:T(8,128)(2,1)}, b...) custom-call(bf16[256,2048]{1,0:T(8,128)(2,1)} %copy-done.118, ...), custom_call_target="tpu_custom_call", output_to_operand_aliasing={{0}: (11, {}), {1}: (12, {}), {2}: (13, {})} | custom-call | flops 9663676416 | bytes 28311552 | tf_op jit(solution)/shard_map/feed_back/pallas_call | solution.py:672
  475.0 9.1 %feed_back.5 = (bf16[2048,2048]{1,0:T(8,128)(2,1)}, bf16[2048,1024]{1,0:T(8,128)(2,1)}, bf16[2048,1024]{1,0:T(8,128)(2,1)}, bf16[256,2048]{1,0:T(8,128)(2,1)S(1)}) custom-call(bf16[256,2048]{1,0:T(8,128)(2,1)S(1)} %pad_maximum_fusion.9.refs_0_, ...), custom_call_target="tpu_custom_call", output_to_operand_aliasing={{0}: (5, {}), {1}: (6, {}), {2}: (7, {})} | custom-call | flops 3221225472 | bytes 17825792 | tf_op jit(solution)/shard_map/feed_back/pallas_call | solution.py:672
  488.5 12.7 %convolution_convert_fusion.1 = bf16[1024,2048]{1,0:T(8,128)(2,1)} fusion(bf16[2048,1024]{1,0:T(8,128)(2,1)S(1)} %copy-done.4, bf16[2048,2048]{1,0:T(8,128)(2,1)} %get-tuple-element.252), kind=kOutput, calls=%fused_computation.9 | convolution fusion | flops 8592031744 | bytes 16777216 | tf_op jit(solution)/shard_map/dot_general | solution.py:931
  511.8 11.5 %owner_grad.2.refs_0_ = bf16[2,2,4,2,64,2048]{5,4,3,2,1,0:T(8,128)(2,1)S(1)} custom-call(bf16[2048,2048]{1,0:T(8,128)(2,1)} %get-tuple-element.256.h, bf16[2048,1024]{1,0:T(8,128)(2,1)S(1)} %copy-done.8), custom_call_target="tpu_custom_call" | custom-call | flops 8589934592 | bytes 16777216 | tf_op jit(solution)/shard_map/owner_grad/pallas_call | solution.py:780
  524.4 12.9 %collective-permute-done.52 = bf16[256,2048]{1,0:T(8,128)(2,1)S(1)} collective-permute-done((bf16[256,2048]{1,0:T(8,128)(2,1)S(1)}, bf16[256,2048]{1,0:T(8,128)(2,1)S(1)}, u32[]{:S(2)}, u32[]{:S(2)}) %collective-permute-start.52) | collective-permute-done | bytes 1048608 | tf_op jit(solution)/shard_map/ppermute | solution.py:29
  542.5 11.3 %owner_grad.3 = bf16[2,2,4,2,64,2048]{5,4,3,2,1,0:T(8,128)(2,1)S(1)} custom-call(bf16[2048,2048]{1,0:T(8,128)(2,1)} %get-tuple-element.256.h, bf16[2048,1024]{1,0:T(8,128)(2,1)S(1)} %copy-done.9, bf16[2,2,4,2,64,2048]{5,4,3,2,1,0:T(8,128)(2,1)S(1)} %owner_grad.2.refs_0_), custom_call_target="tpu_custom_call", output_to_operand_aliasing={{}: (2, {})} | custom-call | flops 8589934592 | bytes 16777216 | tf_op jit(solution)/shard_map/owner_grad/pallas_call | solution.py:780
  557.0 12.2 %collective-permute-done.56 = bf16[256,2048]{1,0:T(8,128)(2,1)S(1)} collective-permute-done((bf16[256,2048]{1,0:T(8,128)(2,1)S(1)}, bf16[256,2048]{1,0:T(8,128)(2,1)S(1)}, u32[]{:S(2)}, u32[]{:S(2)}) %collective-permute-start.56) | collective-permute-done | bytes 1048608 | tf_op jit(solution)/shard_map/ppermute | solution.py:29
  571.6 4.5 multiply_reduce_fusion
  581.2 17.8 %collective-permute-done.58 = bf16[256,2048]{1,0:T(8,128)(2,1)S(1)} collective-permute-done((bf16[256,2048]{1,0:T(8,128)(2,1)S(1)}, bf16[256,2048]{1,0:T(8,128)(2,1)S(1)}, u32[]{:S(2)}, u32[]{:S(2)}) %collective-permute-start.58) | collective-permute-done | bytes 1048608 | tf_op jit(solution)/shard_map/ppermute | solution.py:29
  603.9 5.4 collective-permute-done.59
  619.8 18.3 %attend_back.1 = (f32[1024,512]{1,0:T(8,128)S(1)}, f32[1024,512]{1,0:T(8,128)S(1)}, bf16[1024,512]{1,0:T(8,128)(2,1)S(1)}, f32[1,1024,1]{2,1,0:T(8,128)S(1)}, f3...) custom-call(s32[1]{0:T(128)} %bitcast.1.place, ...), custom_call_target="tpu_custom_call" | custom-call | flops 2684354560 | bytes 15728640 | tf_op jit(solution)/shard_map/attend_back/pallas_call | solution.py:509
  653.4 6.4 finish.1
  659.8 10.1 %convolution_convert_fusion = bf16[2048,1536]{1,0:T(8,128)(2,1)S(1)} fusion(bf16[1024,2048]{1,0:T(8,128)(2,1)} %get-tuple-element.267, bf16[1024,1536]{1,0:T(8,128)(2,1)} %finish.1), kind=kOutput, calls=%fused_computation | convolution fusion | flops 6445596672 | bytes 13631488 | tf_op jit(solution)/shard_map/dot_general | solution.py:931
  673.8 6.0 convolution_convert_fusion.9
  685.8 16.1 %collective-permute-done.67 = bf16[256,768]{1,0:T(8,128)(2,1)S(1)} collective-permute-done((bf16[256,768]{1,0:T(8,128)(2,1)S(1)}, bf16[256,768]{1,0:T(8,128)(2,1)S(1)}, u32[]{:S(2)}, u32[]{:S(2)}) %collective-permute-start.67) | collective-permute-done | bytes 393248 | tf_op jit(solution)/shard_map/ppermute | solution.py:29
  701.9 3.9 collective-permute-done.68
  714.0 4.5 fusion.8
  720.6 5.4 convolution_convert_fusion.7
  735.7 8.3 %collective-permute-done.71 = bf16[256,1024]{1,0:T(8,128)(2,1)S(1)} collective-permute-done((bf16[256,1024]{1,0:T(8,128)(2,1)S(1)}, bf16[256,1024]{1,0:T(8,128)(2,1)S(1)}, u32[]{:S(2)}, u32[]{:S(2)}) %collective-permute-start.71) | collective-permute-done | bytes 524320 | tf_op jit(solution)/shard_map/ppermute | solution.py:29
  744.0 25.9 %collective-permute-done.69 = bf16[256,1536]{1,0:T(8,128)(2,1)S(1)} collective-permute-done((bf16[256,1536]{1,0:T(8,128)(2,1)S(1)}, bf16[256,1536]{1,0:T(8,128)(2,1)S(1)}, u32[]{:S(2)}, u32[]{:S(2)}) %collective-permute-start.69) | collective-permute-done | bytes 786464 | tf_op jit(solution)/shard_map/ppermute | solution.py:29
  774.1 3.8 all-to-all-start.3
  792.5 5.9 convolution_convert_fusion.8
  798.4 4.1 unpack_units.1
  (601 shorter events, 281.9 us)
Async XLA Ops:
  30.4 25.6 %collective-permute-start.6 = (bf16[272,2048]{1,0:T(8,128)(2,1)S(1)}, bf16[272,2048]{1,0:T(8,128)(2,1)S(1)}, u32[]{:S(2)}, u32[]{:S(2)}) collective-permute-start(bf16[272,2048]{1,0:T(8,128)(2,1)S(1)} %fusion.26.refs_0_), channel_id=1, source_target_pairs={{0,16},{8,24},{16,0},{24,8},{1,17},{9,25},{17,1},{25,9},{2,18},{10... | collective-permute-start | bytes 3342344 | tf_op jit(solution)/shard_map/ppermute | solution.py:29
  31.9 25.3 %collective-permute-start.5 = (bf16[272,2048]{1,0:T(8,128)(2,1)S(1)}, bf16[272,2048]{1,0:T(8,128)(2,1)S(1)}, u32[]{:S(2)}, u32[]{:S(2)}) collective-permute-start(bf16[272,2048]{1,0:T(8,128)(2,1)S(1)} %fusion.26.refs_0_), channel_id=1, source_target_pairs={{0,8},{8,0},{16,24},{24,16},{1,9},{9,1},{17,25},{25,17},{2,10},{10... | collective-permute-start | bytes 3342344 | tf_op jit(solution)/shard_map/ppermute | solution.py:29
  32.6 45.9 %collective-permute-start.3 = (bf16[256,2048]{1,0:T(8,128)(2,1)S(1)}, bf16[256,2048]{1,0:T(8,128)(2,1)S(1)}, u32[]{:S(2)}, u32[]{:S(2)}) collective-permute-start(bf16[256,2048]{1,0:T(8,128)(2,1)S(1)} %maximum_maximum_fusion), channel_id=1, source_target_pairs={{0,2},{2,0},{1,3},{3,1},{4,6},{6,4},{5,7},{7,5},{8,10},{10,8},{9,1... | collective-permute-start | bytes 3145736 | tf_op jit(solution)/shard_map/ppermute | solution.py:29
  33.1 45.4 %collective-permute-start.4 = (bf16[256,2048]{1,0:T(8,128)(2,1)S(1)}, bf16[256,2048]{1,0:T(8,128)(2,1)S(1)}, u32[]{:S(2)}, u32[]{:S(2)}) collective-permute-start(bf16[256,2048]{1,0:T(8,128)(2,1)S(1)} %maximum_maximum_fusion), channel_id=1, source_target_pairs={{0,4},{4,0},{1,5},{5,1},{2,6},{6,2},{3,7},{7,3},{8,12},{12,8},{9,1... | collective-permute-start | bytes 3145736 | tf_op jit(solution)/shard_map/ppermute | solution.py:29
  60.3 47.4 %collective-permute-start.11 = (bf16[256,2048]{1,0:T(8,128)(2,1)S(1)}, bf16[256,2048]{1,0:T(8,128)(2,1)S(1)}, u32[]{:S(2)}, u32[]{:S(2)}) collective-permute-start(bf16[256,2048]{1,0:T(8,128)(2,1)S(1)} %maximum_maximum_fusion), channel_id=1, source_target_pairs={{0,1},{1,0},{2,3},{3,2},{4,5},{5,4},{6,7},{7,6},{8,9},{9,8},{10,11... | collective-permute-start | bytes 3145736 | tf_op jit(solution)/shard_map/ppermute | solution.py:29
  78.5 30.2 %collective-permute-start.12 = (bf16[256,2048]{1,0:T(8,128)(2,1)S(1)}, bf16[256,2048]{1,0:T(8,128)(2,1)S(1)}, u32[]{:S(2)}, u32[]{:S(2)}) collective-permute-start(bf16[256,2048]{1,0:T(8,128)(2,1)S(1)} %collective-permute-done.3), channel_id=1, source_target_pairs={{0,1},{1,0},{2,3},{3,2},{4,5},{5,4},{6,7},{7,6},{8,9},{9,8},{10,11... | collective-permute-start | bytes 3145736 | tf_op jit(solution)/shard_map/ppermute | solution.py:29
  78.6 31.5 %collective-permute-start.13 = (bf16[256,2048]{1,0:T(8,128)(2,1)S(1)}, bf16[256,2048]{1,0:T(8,128)(2,1)S(1)}, u32[]{:S(2)}, u32[]{:S(2)}) collective-permute-start(bf16[256,2048]{1,0:T(8,128)(2,1)S(1)} %collective-permute-done.4), channel_id=1, source_target_pairs={{0,1},{1,0},{2,3},{3,2},{4,5},{5,4},{6,7},{7,6},{8,9},{9,8},{10,11... | collective-permute-start | bytes 3145736 | tf_op jit(solution)/shard_map/ppermute | solution.py:29
  79.1 25.6 %collective-permute-start.9 = (bf16[256,1024]{1,0:T(8,128)(2,1)S(1)}, bf16[256,1024]{1,0:T(8,128)(2,1)S(1)}, u32[]{:S(2)}, u32[]{:S(2)}) collective-permute-start(bf16[256,1024]{1,0:T(8,128)(2,1)S(1)} %slice.403), channel_id=1, source_target_pairs={{0,2},{2,0},{1,3},{3,1},{4,6},{6,4},{5,7},{7,5},{8,10},{10,8},{9,1... | collective-permute-start | bytes 1572872 | tf_op jit(solution)/shard_map/ppermute | solution.py:29
  81.7 25.8 %collective-permute-start.10 = (bf16[256,1024]{1,0:T(8,128)(2,1)S(1)}, bf16[256,1024]{1,0:T(8,128)(2,1)S(1)}, u32[]{:S(2)}, u32[]{:S(2)}) collective-permute-start(bf16[256,1024]{1,0:T(8,128)(2,1)S(1)} %slice.404), channel_id=1, source_target_pairs={{0,4},{4,0},{1,5},{5,1},{2,6},{6,2},{3,7},{7,3},{8,12},{12,8},{9,1... | collective-permute-start | bytes 1572872 | tf_op jit(solution)/shard_map/ppermute | solution.py:29
  111.0 32.5 %all-to-all-start.1 = ((bf16[8,64,2048]{2,1,0:T(8,128)(2,1)}), bf16[8,64,2048]{2,1,0:T(8,128)(2,1)}, u32[]{:S(2)}, u32[]{:S(2)}) async-start(bf16[8,64,2048]{2,1,0:T(8,128)(2,1)} %pack_units.1), calls=%async_computation.1 | async-start | bytes 4194304 | tf_op jit(solution)/shard_map/all_to_all | solution.py:1044
  115.4 134.4 %all-gather.3.cloned.1.call-start = ((), (), s32[]{:S(2)}) async-start(), calls=%async_computation.7 | async-start | bytes 10485760 | tf_op jit(solution)/shard_map/all_gather | solution.py:1067
  143.5 183.7 %all-gather.5.cloned.1.call-start = ((), (), s32[]{:S(2)}) async-start(), calls=%async_computation.8 | async-start | bytes 5242880 | tf_op jit(solution)/shard_map/all_gather | solution.py:1104
  184.3 23.9 %collective-permute-start.18 = (bf16[256,2048]{1,0:T(8,128)(2,1)}, bf16[256,2048]{1,0:T(8,128)(2,1)}, u32[]{:S(2)}, u32[]{:S(2)}) collective-permute-start(bf16[256,2048]{1,0:T(8,128)(2,1)} %pad_maximum_fusion.2), channel_id=1, source_target_pairs={{0,8},{8,0},{16,24},{24,16},{1,9},{9,1},{17,25},{25,17},{2,10},{10... | collective-permute-start | bytes 3145736 | tf_op jit(solution)/shard_map/ppermute | solution.py:29
  187.3 23.5 %collective-permute-start.20 = (bf16[256,2048]{1,0:T(8,128)(2,1)}, bf16[256,2048]{1,0:T(8,128)(2,1)}, u32[]{:S(2)}, u32[]{:S(2)}) collective-permute-start(bf16[256,2048]{1,0:T(8,128)(2,1)} %pad_maximum_fusion.3), channel_id=1, source_target_pairs={{0,16},{8,24},{16,0},{24,8},{1,17},{9,25},{17,1},{25,9},{2,18},{10... | collective-permute-start | bytes 3145736 | tf_op jit(solution)/shard_map/ppermute | solution.py:29
  214.6 22.5 %collective-permute-start.23 = (bf16[256,2048]{1,0:T(8,128)(2,1)}, bf16[256,2048]{1,0:T(8,128)(2,1)S(1)}, u32[]{:S(2)}, u32[]{:S(2)}) collective-permute-start(bf16[256,2048]{1,0:T(8,128)(2,1)} %fusion.23.refs_0_), channel_id=1, source_target_pairs={{0,16},{8,24},{16,0},{24,8},{1,17},{9,25},{17,1},{25,9},{2,18},{10... | collective-permute-start | bytes 3145736 | tf_op jit(solution)/shard_map/ppermute | solution.py:29
  215.5 23.0 %collective-permute-start.22 = (bf16[256,2048]{1,0:T(8,128)(2,1)}, bf16[256,2048]{1,0:T(8,128)(2,1)S(1)}, u32[]{:S(2)}, u32[]{:S(2)}) collective-permute-start(bf16[256,2048]{1,0:T(8,128)(2,1)} %fusion.23.refs_0_), channel_id=1, source_target_pairs={{0,8},{8,0},{16,24},{24,16},{1,9},{9,1},{17,25},{25,17},{2,10},{10... | collective-permute-start | bytes 3145736 | tf_op jit(solution)/shard_map/ppermute | solution.py:29
  240.2 30.1 %collective-permute-start.21 = (bf16[256,2048]{1,0:T(8,128)(2,1)}, bf16[256,2048]{1,0:T(8,128)(2,1)}, u32[]{:S(2)}, u32[]{:S(2)}) collective-permute-start(bf16[256,2048]{1,0:T(8,128)(2,1)} %fusion.23.refs_0_), channel_id=1, source_target_pairs={{0,2},{2,0},{1,3},{3,1},{4,6},{6,4},{5,7},{7,5},{8,10},{10,8},{9,1... | collective-permute-start | bytes 3145736 | tf_op jit(solution)/shard_map/ppermute | solution.py:29
  270.3 342.6 %reduce-scatter.3.cloned.1.call-start = ((), (), s32[]{:S(2)}) async-start(), calls=%async_computation.9 | async-start | bytes 5242880 | tf_op jit(solution)/shard_map/reduce_scatter | solution.py:1133
  270.7 23.6 %collective-permute-start.26 = (bf16[256,2048]{1,0:T(8,128)(2,1)}, bf16[256,2048]{1,0:T(8,128)(2,1)S(1)}, u32[]{:S(2)}, u32[]{:S(2)}) collective-permute-start(bf16[256,2048]{1,0:T(8,128)(2,1)} %collective-permute-done.21.refs_0_), channel_id=1, source_target_pairs={{0,8},{8,0},{16,24},{24,16},{1,9},{9,1},{17,25},{25,17},{2,10},{10... | collective-permute-start | bytes 3145736 | tf_op jit(solution)/shard_map/ppermute | solution.py:29
  272.3 23.3 %collective-permute-start.27 = (bf16[256,2048]{1,0:T(8,128)(2,1)}, bf16[256,2048]{1,0:T(8,128)(2,1)S(1)}, u32[]{:S(2)}, u32[]{:S(2)}) collective-permute-start(bf16[256,2048]{1,0:T(8,128)(2,1)} %collective-permute-done.21.refs_0_), channel_id=1, source_target_pairs={{0,16},{8,24},{16,0},{24,8},{1,17},{9,25},{17,1},{25,9},{2,18},{10... | collective-permute-start | bytes 3145736 | tf_op jit(solution)/shard_map/ppermute | solution.py:29
  348.7 24.3 %collective-permute-start.34 = (bf16[256,2048]{1,0:T(8,128)(2,1)S(1)}, bf16[256,2048]{1,0:T(8,128)(2,1)S(1)}, u32[]{:S(2)}, u32[]{:S(2)}) collective-permute-start(bf16[256,2048]{1,0:T(8,128)(2,1)S(1)} %pad_maximum_fusion.7), channel_id=1, source_target_pairs={{0,8},{8,0},{16,24},{24,16},{1,9},{9,1},{17,25},{25,17},{2,10},{10... | collective-permute-start | bytes 3145736 | tf_op jit(solution)/shard_map/ppermute | solution.py:29
  350.5 24.1 %collective-permute-start.37 = (bf16[256,2048]{1,0:T(8,128)(2,1)S(1)}, bf16[256,2048]{1,0:T(8,128)(2,1)S(1)}, u32[]{:S(2)}, u32[]{:S(2)}) collective-permute-start(bf16[256,2048]{1,0:T(8,128)(2,1)S(1)} %pad_maximum_fusion.8), channel_id=1, source_target_pairs={{0,16},{8,24},{16,0},{24,8},{1,17},{9,25},{17,1},{25,9},{2,18},{10... | collective-permute-start | bytes 3145736 | tf_op jit(solution)/shard_map/ppermute | solution.py:29
  352.4 24.3 %collective-permute-start.31 = (bf16[256,2048]{1,0:T(8,128)(2,1)S(1)}, bf16[256,2048]{1,0:T(8,128)(2,1)S(1)}, u32[]{:S(2)}, u32[]{:S(2)}) collective-permute-start(bf16[256,2048]{1,0:T(8,128)(2,1)S(1)} %pad_maximum_fusion.6), channel_id=1, source_target_pairs={{0,2},{2,0},{1,3},{3,1},{4,6},{6,4},{5,7},{7,5},{8,10},{10,8},{9,1... | collective-permute-start | bytes 3145736 | tf_op jit(solution)/shard_map/ppermute | solution.py:29
  373.5 23.6 %collective-permute-start.35 = (bf16[256,2048]{1,0:T(8,128)(2,1)S(1)}, bf16[256,2048]{1,0:T(8,128)(2,1)S(1)}, u32[]{:S(2)}, u32[]{:S(2)}) collective-permute-start(bf16[256,2048]{1,0:T(8,128)(2,1)S(1)} %add_convert_fusion.5), channel_id=1, source_target_pairs={{0,16},{8,24},{16,0},{24,8},{1,17},{9,25},{17,1},{25,9},{2,18},{10... | collective-permute-start | bytes 3145736 | tf_op jit(solution)/shard_map/ppermute | solution.py:29
  375.0 23.7 %collective-permute-start.38 = (bf16[256,2048]{1,0:T(8,128)(2,1)S(1)}, bf16[256,2048]{1,0:T(8,128)(2,1)S(1)}, u32[]{:S(2)}, u32[]{:S(2)}) collective-permute-start(bf16[256,2048]{1,0:T(8,128)(2,1)S(1)} %add_convert_fusion.4), channel_id=1, source_target_pairs={{0,2},{2,0},{1,3},{3,1},{4,6},{6,4},{5,7},{7,5},{8,10},{10,8},{9,1... | collective-permute-start | bytes 3145736 | tf_op jit(solution)/shard_map/ppermute | solution.py:29
  377.1 22.3 %collective-permute-start.32 = (bf16[256,2048]{1,0:T(8,128)(2,1)S(1)}, bf16[256,2048]{1,0:T(8,128)(2,1)S(1)}, u32[]{:S(2)}, u32[]{:S(2)}) collective-permute-start(bf16[256,2048]{1,0:T(8,128)(2,1)S(1)} %add_convert_fusion.6), channel_id=1, source_target_pairs={{0,8},{8,0},{16,24},{24,16},{1,9},{9,1},{17,25},{25,17},{2,10},{10... | collective-permute-start | bytes 3145736 | tf_op jit(solution)/shard_map/ppermute | solution.py:29
  402.1 22.3 %collective-permute-start.40 = (bf16[256,2048]{1,0:T(8,128)(2,1)S(1)}, bf16[256,2048]{1,0:T(8,128)(2,1)}, u32[]{:S(2)}, u32[]{:S(2)}) collective-permute-start(bf16[256,2048]{1,0:T(8,128)(2,1)S(1)} %fusion.17.refs_0_), channel_id=1, source_target_pairs={{0,16},{8,24},{16,0},{24,8},{1,17},{9,25},{17,1},{25,9},{2,18},{10... | collective-permute-start | bytes 3145736 | tf_op jit(solution)/shard_map/ppermute | solution.py:29
  403.6 24.6 %collective-permute-start.39 = (bf16[256,2048]{1,0:T(8,128)(2,1)S(1)}, bf16[256,2048]{1,0:T(8,128)(2,1)}, u32[]{:S(2)}, u32[]{:S(2)}) collective-permute-start(bf16[256,2048]{1,0:T(8,128)(2,1)S(1)} %fusion.17.refs_0_), channel_id=1, source_target_pairs={{0,8},{8,0},{16,24},{24,16},{1,9},{9,1},{17,25},{25,17},{2,10},{10... | collective-permute-start | bytes 3145736 | tf_op jit(solution)/shard_map/ppermute | solution.py:29
  404.2 24.8 %collective-permute-start.41 = (bf16[256,2048]{1,0:T(8,128)(2,1)S(1)}, bf16[256,2048]{1,0:T(8,128)(2,1)S(1)}, u32[]{:S(2)}, u32[]{:S(2)}) collective-permute-start(bf16[256,2048]{1,0:T(8,128)(2,1)S(1)} %fusion.17.refs_0_), channel_id=1, source_target_pairs={{0,2},{2,0},{1,3},{3,1},{4,6},{6,4},{5,7},{7,5},{8,10},{10,8},{9,1... | collective-permute-start | bytes 3145736 | tf_op jit(solution)/shard_map/ppermute | solution.py:29
  424.4 30.0 %collective-permute-start.42 = (bf16[256,2048]{1,0:T(8,128)(2,1)}, bf16[256,2048]{1,0:T(8,128)(2,1)S(1)}, u32[]{:S(2)}, u32[]{:S(2)}) collective-permute-start(bf16[256,2048]{1,0:T(8,128)(2,1)} %collective-permute-done.40.refs_2_), channel_id=1, source_target_pairs={{0,8},{8,0},{16,24},{24,16},{1,9},{9,1},{17,25},{25,17},{2,10},{10... | collective-permute-start | bytes 3145736 | tf_op jit(solution)/shard_map/ppermute | solution.py:29
  428.2 24.1 %collective-permute-start.43 = (bf16[256,2048]{1,0:T(8,128)(2,1)}, bf16[256,2048]{1,0:T(8,128)(2,1)S(1)}, u32[]{:S(2)}, u32[]{:S(2)}) collective-permute-start(bf16[256,2048]{1,0:T(8,128)(2,1)} %collective-permute-done.39.refs_1_), channel_id=1, source_target_pairs={{0,2},{2,0},{1,3},{3,1},{4,6},{6,4},{5,7},{7,5},{8,10},{10,8},{9,1... | collective-permute-start | bytes 3145736 | tf_op jit(solution)/shard_map/ppermute | solution.py:29
  429.0 24.5 %collective-permute-start.44 = (bf16[256,2048]{1,0:T(8,128)(2,1)S(1)}, bf16[256,2048]{1,0:T(8,128)(2,1)S(1)}, u32[]{:S(2)}, u32[]{:S(2)}) collective-permute-start(bf16[256,2048]{1,0:T(8,128)(2,1)S(1)} %collective-permute-done.41.refs_3_), channel_id=1, source_target_pairs={{0,16},{8,24},{16,0},{24,8},{1,17},{9,25},{17,1},{25,9},{2,18},{10... | collective-permute-start | bytes 3145736 | tf_op jit(solution)/shard_map/ppermute | solution.py:29
  452.3 21.6 %collective-permute-start.46 = (bf16[256,768]{1,0:T(8,128)(2,1)S(1)}, bf16[256,768]{1,0:T(8,128)(2,1)S(1)}, u32[]{:S(2)}, u32[]{:S(2)}) collective-permute-start(bf16[256,768]{1,0:T(8,128)(2,1)S(1)} %slice.537), channel_id=1, source_target_pairs={{0,16},{8,24},{16,0},{24,8},{1,17},{9,25},{17,1},{25,9},{2,18},{10... | collective-permute-start | bytes 1179656 | tf_op jit(solution)/shard_map/ppermute | solution.py:29
  453.5 20.4 %collective-permute-start.45 = (bf16[256,640]{1,0:T(8,128)(2,1)S(1)}, bf16[256,640]{1,0:T(8,128)(2,1)S(1)}, u32[]{:S(2)}, u32[]{:S(2)}) collective-permute-start(bf16[256,640]{1,0:T(8,128)(2,1)S(1)} %slice.536), channel_id=1, source_target_pairs={{0,8},{8,0},{16,24},{24,16},{1,9},{9,1},{17,25},{25,17},{2,10},{10... | collective-permute-start | bytes 983048 | tf_op jit(solution)/shard_map/ppermute | solution.py:29
  501.3 206.6 %reduce-scatter.5.cloned.1.call-start = ((), (), s32[]{:S(2)}) async-start(), calls=%async_computation.10 | async-start | bytes 10485760 | tf_op jit(solution)/shard_map/reduce_scatter | solution.py:1133
  507.5 29.8 %collective-permute-start.52 = (bf16[256,2048]{1,0:T(8,128)(2,1)S(1)}, bf16[256,2048]{1,0:T(8,128)(2,1)S(1)}, u32[]{:S(2)}, u32[]{:S(2)}) collective-permute-start(bf16[256,2048]{1,0:T(8,128)(2,1)S(1)} %pad_maximum_fusion.11), channel_id=1, source_target_pairs={{0,2},{2,0},{1,3},{3,1},{4,6},{6,4},{5,7},{7,5},{8,10},{10,8},{9,1... | collective-permute-start | bytes 3145736 | tf_op jit(solution)/shard_map/ppermute | solution.py:29
  510.6 26.7 %collective-permute-start.51 = (bf16[256,2048]{1,0:T(8,128)(2,1)S(1)}, bf16[256,2048]{1,0:T(8,128)(2,1)S(1)}, u32[]{:S(2)}, u32[]{:S(2)}) collective-permute-start(bf16[256,2048]{1,0:T(8,128)(2,1)S(1)} %pad_maximum_fusion.10), channel_id=1, source_target_pairs={{0,8},{8,0},{16,24},{24,16},{1,9},{9,1},{17,25},{25,17},{2,10},{10... | collective-permute-start | bytes 3145736 | tf_op jit(solution)/shard_map/ppermute | solution.py:29
  537.7 31.5 %collective-permute-start.56 = (bf16[256,2048]{1,0:T(8,128)(2,1)S(1)}, bf16[256,2048]{1,0:T(8,128)(2,1)S(1)}, u32[]{:S(2)}, u32[]{:S(2)}) collective-permute-start(bf16[256,2048]{1,0:T(8,128)(2,1)S(1)} %add_convert_fusion), channel_id=1, source_target_pairs={{0,2},{2,0},{1,3},{3,1},{4,6},{6,4},{5,7},{7,5},{8,10},{10,8},{9,1... | collective-permute-start | bytes 3145736 | tf_op jit(solution)/shard_map/ppermute | solution.py:29
  540.7 28.5 %collective-permute-start.55 = (bf16[256,2048]{1,0:T(8,128)(2,1)S(1)}, bf16[256,2048]{1,0:T(8,128)(2,1)S(1)}, u32[]{:S(2)}, u32[]{:S(2)}) collective-permute-start(bf16[256,2048]{1,0:T(8,128)(2,1)S(1)} %add_convert_fusion.1), channel_id=1, source_target_pairs={{0,16},{8,24},{16,0},{24,8},{1,17},{9,25},{17,1},{25,9},{2,18},{10... | collective-permute-start | bytes 3145736 | tf_op jit(solution)/shard_map/ppermute | solution.py:29
  541.7 27.5 %collective-permute-start.54 = (bf16[256,2048]{1,0:T(8,128)(2,1)S(1)}, bf16[256,2048]{1,0:T(8,128)(2,1)S(1)}, u32[]{:S(2)}, u32[]{:S(2)}) collective-permute-start(bf16[256,2048]{1,0:T(8,128)(2,1)S(1)} %add_convert_fusion.2), channel_id=1, source_target_pairs={{0,8},{8,0},{16,24},{24,16},{1,9},{9,1},{17,25},{25,17},{2,10},{10... | collective-permute-start | bytes 3145736 | tf_op jit(solution)/shard_map/ppermute | solution.py:29
  579.8 22.7 %collective-permute-start.57 = (bf16[256,2048]{1,0:T(8,128)(2,1)S(1)}, bf16[256,2048]{1,0:T(8,128)(2,1)S(1)}, u32[]{:S(2)}, u32[]{:S(2)}) collective-permute-start(bf16[256,2048]{1,0:T(8,128)(2,1)S(1)} %get-tuple-element.295), channel_id=1, source_target_pairs={{0,8},{8,0},{16,24},{24,16},{1,9},{9,1},{17,25},{25,17},{2,10},{10... | collective-permute-start | bytes 3145736 | tf_op jit(solution)/shard_map/ppermute | solution.py:29
  685.7 20.1 %collective-permute-start.68 = (bf16[256,768]{1,0:T(8,128)(2,1)S(1)}, bf16[256,768]{1,0:T(8,128)(2,1)S(1)}, u32[]{:S(2)}, u32[]{:S(2)}) collective-permute-start(bf16[256,768]{1,0:T(8,128)(2,1)S(1)} %get-tuple-element.372), channel_id=1, source_target_pairs={{0,4},{4,0},{1,5},{5,1},{2,6},{6,2},{3,7},{7,3},{8,12},{12,8},{9,1... | collective-permute-start | bytes 1179656 | tf_op jit(solution)/shard_map/ppermute | solution.py:29
  707.9 62.8 %all-to-all-start.2 = ((bf16[8,64,2048]{2,1,0:T(8,128)(2,1)}), bf16[8,64,2048]{2,1,0:T(8,128)(2,1)S(1)}, u32[]{:S(2)}, u32[]{:S(2)}) async-start(bf16[8,64,2048]{2,1,0:T(8,128)(2,1)} %reduce-scatter.5.cloned.1.call-done), calls=%async_computation.4 | async-start | bytes 4194304 | tf_op jit(solution)/shard_map/all_to_all | solution.py:1194
  729.6 40.2 %collective-permute-start.69 = (bf16[256,1536]{1,0:T(8,128)(2,1)S(1)}, bf16[256,1536]{1,0:T(8,128)(2,1)S(1)}, u32[]{:S(2)}, u32[]{:S(2)}) collective-permute-start(bf16[256,1536]{1,0:T(8,128)(2,1)S(1)} %copy-done.104), channel_id=1, source_target_pairs={{0,2},{2,0},{1,3},{3,1},{4,6},{6,4},{5,7},{7,5},{8,10},{10,8},{9,1... | collective-permute-start | bytes 2359304 | tf_op jit(solution)/shard_map/ppermute | solution.py:29
  731.1 39.6 %collective-permute-start.70 = (bf16[256,1536]{1,0:T(8,128)(2,1)S(1)}, bf16[256,1536]{1,0:T(8,128)(2,1)}, u32[]{:S(2)}, u32[]{:S(2)}) collective-permute-start(bf16[256,1536]{1,0:T(8,128)(2,1)S(1)} %copy-done.103), channel_id=1, source_target_pairs={{0,4},{4,0},{1,5},{5,1},{2,6},{6,2},{3,7},{7,3},{8,12},{12,8},{9,1... | collective-permute-start | bytes 2359304 | tf_op jit(solution)/shard_map/ppermute | solution.py:29
  774.1 28.6 %all-to-all-start.3 = ((bf16[4,64,1536]{2,1,0:T(8,128)(2,1)}), bf16[4,64,1536]{2,1,0:T(8,128)(2,1)S(1)}, u32[]{:S(2)}, u32[]{:S(2)}) async-start(bf16[4,64,1536]{2,1,0:T(8,128)(2,1)} %bitcast.191), calls=%async_computation.5 | async-start | bytes 1572864 | tf_op jit(solution)/shard_map/all_to_all | solution.py:1201
  783.8 31.5 %collective-permute-start.77 = (bf16[256,2048]{1,0:T(8,128)(2,1)}, bf16[256,2048]{1,0:T(8,128)(2,1)}, u32[]{:S(2)}, u32[]{:S(2)}) collective-permute-start(bf16[256,2048]{1,0:T(8,128)(2,1)} %pad_maximum_fusion.15), channel_id=1, source_target_pairs={{0,8},{8,0},{16,24},{24,16},{1,9},{9,1},{17,25},{25,17},{2,10},{10... | collective-permute-start | bytes 3145736 | tf_op jit(solution)/shard_map/ppermute | solution.py:29
  787.1 28.2 %collective-permute-start.78 = (bf16[256,2048]{1,0:T(8,128)(2,1)}, bf16[256,2048]{1,0:T(8,128)(2,1)}, u32[]{:S(2)}, u32[]{:S(2)}) collective-permute-start(bf16[256,2048]{1,0:T(8,128)(2,1)} %pad_maximum_fusion.16), channel_id=1, source_target_pairs={{0,16},{8,24},{16,0},{24,8},{1,17},{9,25},{17,1},{25,9},{2,18},{10... | collective-permute-start | bytes 3145736 | tf_op jit(solution)/shard_map/ppermute | solution.py:29
  (170 other events, 1852.1 us)
Sparse Core Ops, SparseCore 0:
  143.6 104.1 all-gather.2
  270.4 56.7 all-gather.4
  501.4 65.9 reduce-scatter.2
  571.7 115.9 reduce-scatter.4

commit v4 on v3

--- a/solution.py
+++ b/solution.py
@@ -290,7 +290,7 @@
             pltpu.VMEM((n_w * rows, blocks * part), bf16),
             pltpu.SemaphoreType.DMA((n_x + 2 * number + 3,)),
         ],
-        compiler_params=pltpu.CompilerParams(vmem_limit_bytes=40 * 1024 * 1024),
+        compiler_params=pltpu.CompilerParams(vmem_limit_bytes=56 * 1024 * 1024),
         cost_estimate=pl.CostEstimate(
             flops=6 * length * width * part, bytes_accessed=20 * length * part, transcendentals=0
         ),
@@ -530,7 +530,7 @@
         ]
         + [jax.ShapeDtypeStruct((1, tokens, 1), f32)] * 2
         + [jax.ShapeDtypeStruct((1, width), f32)] * 2,
-        compiler_params=pltpu.CompilerParams(vmem_limit_bytes=40 * 1024 * 1024),
+        compiler_params=pltpu.CompilerParams(vmem_limit_bytes=56 * 1024 * 1024),
         cost_estimate=pl.CostEstimate(
             flops=5 * tokens * tokens * width,
             bytes_accessed=30 * tokens * width,
@@ -647,7 +647,7 @@
             copy.start()
         weights.wait()
         width = held_d.shape[1]
-        cols = math.gcd(width, 512)
+        cols = math.gcd(width, 1024)
         for n in range(0, width, cols):
             product = dot_t(held_gu[...], held_w[n : n + cols, :]).astype(bf16)
             for i, out in enumerate(partials):
@@ -695,7 +695,7 @@
 
 def feed(pieces, masks, total, w_gu, earlier):
     width, units = w_gu.shape[0], w_gu.shape[1] // 2
-    part = math.gcd(units, 256)
+    part = math.gcd(units, 512)
     steps = units // part
     number = len(pieces)
     rows = number * pieces[0].shape[0]
@@ -745,7 +745,7 @@
 
 def feed_back(pieces, masks, total, acts, w_gu, down, earlier):
     units, width = down.shape
-    part = math.gcd(units, 256)
+    part = math.gcd(units, 512)
     steps = units // part
     number = len(pieces)
     tok = pieces[0].shape[0]
@@ -915,6 +915,7 @@
         in_specs=[cols(0), cols(0), cols(0), cols(1)] + [rows(0), rows(1)] * 2 + [cols(0)],
         out_specs=pl.BlockSpec((block, 3 * part), lambda b: (b, 0)),
         out_shape=jax.ShapeDtypeStruct((length, 3 * part), bf16),
+        compiler_params=pltpu.CompilerParams(vmem_limit_bytes=56 * 1024 * 1024),
         name="finish",
     )(e_query, e_key, raw, raw, inverse, inverse, means, means, d_value)
 

time: 836 us -> 825 us (0.987)
  local copies, waits for them, and re-layouts: 78.8 us -> 60.6 us
  waiting for transfers between devices: 321 us -> 335 us
    unnamed x251 -> x249, local copies, waits for them, and re-layouts: 60.7 us -> 40.9 us
  transfers between devices with their start and end apart: 92 -> 92, of which waited for: 41 -> 45; matrix products, arithmetic and copies ran while one was open for 14% -> 14% of each run, Pallas kernels for 21% -> 21%
where the time goes in v4:
time: 825 us; the launch traced here: 817 us
  waiting for transfers between devices  335 us (41%)
  Pallas kernels  188 us (23%)
  starting transfers between devices  114 us (14%)
  local copies, waits for them, and re-layouts  60.6 us (7%)
  matrix products  53.6 us (6%)
  other arithmetic  49.4 us (6%)
  between operations  16.5 us (2%)
    ppermute x83, waiting for transfers between devices, swap(): lax.ppermute(block, axis, [(i, i ^ mask) for i in range(lax.axis_size(axi...  312 us
    ppermute x83, starting transfers between devices, swap(): lax.ppermute(block, axis, [(i, i ^ mask) for i in range(lax.axis_size(axi...  94.8 us
    pallas_call x7, Pallas kernels, feed_call(): pl.pallas_call(body, grid=(steps,), in_specs=[somewhere] * number + in_sp...  86.1 us
    unnamed x249, local copies, waits for them, and re-layouts  40.9 us
    dot_general x3, matrix products, t_dot(): lax.dot_general(left, right, (((0,), (0,)), ((), ())), preferred_element_...  26.2 us
    dot_general x8, matrix products, dot_t(): lax.dot_general(left, right, (((1,), (1,)), ((), ())), preferred_element_...  23.6 us
    pallas_call x2, Pallas kernels, owner_grad(): pl.pallas_call(kernel, grid=(n_seq,), in_specs=[pl.BlockSpec((tokens, col...  23 us
    pallas_call x1, Pallas kernels, attend_back(): pl.pallas_call(functools.partial(backward_kernel, scale * math.log2(math....  20.2 us
  transfers between devices with their start and end apart: 92, of which 45 were waited for; matrix products, arithmetic and copies ran while one was open for 14% of the time, Pallas kernels for 21%

profile of v4, /device:TPU:0, one launch (start us, length us, event | category | flops | bytes accessed | tf_op | source)
XLA Modules:
  0.0 816.5 jit_solution(6784130380312437277)
XLA Ops:
  25.9 4.1 all-to-all-done
  35.7 20.2 %collective-permute-done.6.refs_2_ = bf16[272,2048]{1,0:T(8,128)(2,1)S(1)} collective-permute-done((bf16[272,2048]{1,0:T(8,128)(2,1)S(1)}, bf16[272,2048]{1,0:T(8,128)(2,1)S(1)}, u32[]{:S(2)}, u32[]{:S(2)}) %collective-permute-start.6) | collective-permute-done | bytes 1114144 | tf_op jit(solution)/shard_map/ppermute | solution.py:29
  60.4 8.5 %collective-permute-done.7 = bf16[272,1024]{1,0:T(8,128)(2,1)S(1)} collective-permute-done((bf16[272,1024]{1,0:T(8,128)(2,1)S(1)}, bf16[272,1024]{1,0:T(8,128)(2,1)S(1)}, u32[]{:S(2)}, u32[]{:S(2)}) %collective-permute-start.7) | collective-permute-done | bytes 557088 | tf_op jit(solution)/shard_map/ppermute | solution.py:29
  70.5 8.0 collective-permute-done.3
  84.5 20.2 %collective-permute-done.9 = bf16[256,1024]{1,0:T(8,128)(2,1)S(1)} collective-permute-done((bf16[256,1024]{1,0:T(8,128)(2,1)S(1)}, bf16[256,1024]{1,0:T(8,128)(2,1)S(1)}, u32[]{:S(2)}, u32[]{:S(2)}) %collective-permute-start.9) | collective-permute-done | bytes 524320 | tf_op jit(solution)/shard_map/ppermute | solution.py:29
  109.1 4.3 all-to-all-start.1
  117.3 14.5 %project.1 = (f32[1024,1536]{1,0:T(8,128)}, f32[2,1024,1]{2,1,0:T(8,128)}, bf16[1024,2048]{1,0:T(8,128)(2,1)}, bf16[2048,1536]{1,0:T(8,128)(2,1)}, bf16[512,2048]{1,0:T(8,128)(2,1)}) custom-call(s32[32]{0:T(128)} %stack.206.table, s32[8]{0:T(128)} %stack.207.out_table, bf16[272,2048]{1,0:T(8,128)(2,1)} %copy-done.64, bf16[272,2048]{1,0:T(8,128)(2,1)} %copy-done.91, ...), custom_call_target="tpu_custom_call" | custom-call | flops 6442450944 | bytes 10485760 | tf_op jit(solution)/shard_map/project/pallas_call | solution.py:269
  131.8 6.2 all-to-all-done.1
  154.1 10.1 %attend.1 = (f32[1024,512]{1,0:T(8,128)S(1)}, bf16[1024,512]{1,0:T(8,128)(2,1)S(1)}, f32[4,4,1,256]{3,2,1,0:T(1,128)S(1)}) custom-call(s32[1]{0:T(128)} %bitcast.1.place, f32[1024,1536]{1,0:T(8,128)S(1)} %copy-done, f32[1024,1536]{1,0:T(8,128)S(1)} %copy-done, f32[1024,1536]{1,0:T(8,128)S(1)} %copy-done, f32[2,1024,1]{2,1,0:T(8,128)S(1)} %rsqrt.28.q_inv.k_inv, ...), custom_call_target="tpu_custom_call" | custom-call | flops 1073741824 | bytes 9437184 | tf_op jit(solution)/shard_map/attend/pallas_call | solution.py:475
  169.3 6.1 collective-permute-done.17
  182.3 17.0 %collective-permute-done.18 = bf16[256,2048]{1,0:T(8,128)(2,1)} collective-permute-done((bf16[256,2048]{1,0:T(8,128)(2,1)S(1)}, bf16[256,2048]{1,0:T(8,128)(2,1)}, u32[]{:S(2)}, u32[]{:S(2)}) %collective-permute-start.18) | collective-permute-done | bytes 1048608 | tf_op jit(solution)/shard_map/ppermute | solution.py:29
  205.6 19.8 %collective-permute-done.23.refs_0_ = bf16[256,2048]{1,0:T(8,128)(2,1)S(1)} collective-permute-done((bf16[256,2048]{1,0:T(8,128)(2,1)S(1)}, bf16[256,2048]{1,0:T(8,128)(2,1)S(1)}, u32[]{:S(2)}, u32[]{:S(2)}) %collective-permute-start.23) | collective-permute-done | bytes 1048608 | tf_op jit(solution)/shard_map/ppermute | solution.py:29
  230.1 5.8 collective-permute-start.21
  238.4 4.8 all-gather.3.cloned.1.call-done.ref
  250.8 10.3 %feed.4 = (bf16[2048,2048]{1,0:T(8,128)(2,1)}, bf16[2048,1024]{1,0:T(8,128)(2,1)}, bf16[256,1024]{1,0:T(8,128)(2,1)S(1)}, bf16[256,1024]{1,0:T(8,128)(2,1)S(1)},...) custom-call(bf16[256,2048]{1,0:T(8,128)(2,1)S(1)} %fusion.23.refs_0_, bf16[256,2048]{1,0:T(8,128)(2,1)} %copy-done.98, ...), custom_call_target="tpu_custom_call" | custom-call | flops 6442450944 | bytes 23068672 | tf_op jit(solution)/shard_map/feed/pallas_call | solution.py:672
  267.9 10.3 %feed.5 = (bf16[2048,2048]{1,0:T(8,128)(2,1)}, bf16[2048,1024]{1,0:T(8,128)(2,1)}, bf16[256,1024]{1,0:T(8,128)(2,1)S(1)}, bf16[256,1024]{1,0:T(8,128)(2,1)S(1)},...) custom-call(bf16[256,2048]{1,0:T(8,128)(2,1)S(1)} %collective-permute-, ...), custom_call_target="tpu_custom_call", output_to_operand_aliasing={{0}: (4, {}), {1}: (5, {})} | custom-call | flops 6442450944 | bytes 23068672 | tf_op jit(solution)/shard_map/feed/pallas_call | solution.py:672
  278.2 12.3 %collective-permute-done.26.refs_1_ = bf16[256,2048]{1,0:T(8,128)(2,1)S(1)} collective-permute-done((bf16[256,2048]{1,0:T(8,128)(2,1)}, bf16[256,2048]{1,0:T(8,128)(2,1)S(1)}, u32[]{:S(2)}, u32[]{:S(2)}) %collective-permute-start.26) | collective-permute-done | bytes 1048608 | tf_op jit(solution)/shard_map/ppermute | solution.py:29
  293.9 13.2 %feed.6 = (bf16[2048,2048]{1,0:T(8,128)(2,1)}, bf16[2048,1024]{1,0:T(8,128)(2,1)}, bf16[256,1024]{1,0:T(8,128)(2,1)S(1)}, bf16[256,1024]{1,0:T(8,128)(2,1)S(1)},...) custom-call(bf16[256,2048]{1,0:T(8,128)(2,1)} %collective-permute-do, ...), custom_call_target="tpu_custom_call", output_to_operand_aliasing={{0}: (5, {}), {1}: (6, {})} | custom-call | flops 9663676416 | bytes 28311552 | tf_op jit(solution)/shard_map/feed/pallas_call | solution.py:672
  310.0 6.1 feed.7
  316.2 7.7 all-gather.5.cloned.1.call-done.weight.refs_12_.refs_9_.refs_3_
  328.3 5.7 feed_down.3
  337.3 5.8 feed_down.2
  348.5 21.2 %collective-permute-done.34 = bf16[256,2048]{1,0:T(8,128)(2,1)S(1)} collective-permute-done((bf16[256,2048]{1,0:T(8,128)(2,1)S(1)}, bf16[256,2048]{1,0:T(8,128)(2,1)S(1)}, u32[]{:S(2)}, u32[]{:S(2)}) %collective-permute-start.34) | collective-permute-done | bytes 1048608 | tf_op jit(solution)/shard_map/ppermute | solution.py:29
  373.7 19.9 %collective-permute-done.35 = bf16[256,2048]{1,0:T(8,128)(2,1)S(1)} collective-permute-done((bf16[256,2048]{1,0:T(8,128)(2,1)S(1)}, bf16[256,2048]{1,0:T(8,128)(2,1)S(1)}, u32[]{:S(2)}, u32[]{:S(2)}) %collective-permute-start.35) | collective-permute-done | bytes 1048608 | tf_op jit(solution)/shard_map/ppermute | solution.py:29
  402.4 18.5 %collective-permute-done.40.refs_2_ = bf16[256,2048]{1,0:T(8,128)(2,1)S(1)} collective-permute-done((bf16[256,2048]{1,0:T(8,128)(2,1)S(1)}, bf16[256,2048]{1,0:T(8,128)(2,1)S(1)}, u32[]{:S(2)}, u32[]{:S(2)}) %collective-permute-start.40) | collective-permute-done | bytes 1048608 | tf_op jit(solution)/shard_map/ppermute | solution.py:29
  426.3 20.7 %feed_back.3 = (bf16[2048,2048]{1,0:T(8,128)(2,1)}, bf16[2048,1024]{1,0:T(8,128)(2,1)}, bf16[2048,1024]{1,0:T(8,128)(2,1)}, bf16[256,2048]{1,0:T(8,128)(2,1)}, b...) custom-call(bf16[256,2048]{1,0:T(8,128)(2,1)} %copy-done.79, ...), custom_call_target="tpu_custom_call" | custom-call | flops 12884901888 | bytes 33554432 | tf_op jit(solution)/shard_map/feed_back/pallas_call | solution.py:672
  450.9 16.7 %feed_back.4 = (bf16[2048,2048]{1,0:T(8,128)(2,1)}, bf16[2048,1024]{1,0:T(8,128)(2,1)}, bf16[2048,1024]{1,0:T(8,128)(2,1)}, bf16[256,2048]{1,0:T(8,128)(2,1)}, b...) custom-call(bf16[256,2048]{1,0:T(8,128)(2,1)} %copy-done.104, ...), custom_call_target="tpu_custom_call", output_to_operand_aliasing={{0}: (11, {}), {1}: (12, {}), {2}: (13, {})} | custom-call | flops 9663676416 | bytes 28311552 | tf_op jit(solution)/shard_map/feed_back/pallas_call | solution.py:672
  467.8 8.6 %feed_back.5 = (bf16[2048,2048]{1,0:T(8,128)(2,1)}, bf16[2048,1024]{1,0:T(8,128)(2,1)}, bf16[2048,1024]{1,0:T(8,128)(2,1)}, bf16[256,2048]{1,0:T(8,128)(2,1)S(1)}) custom-call(bf16[256,2048]{1,0:T(8,128)(2,1)S(1)} %pad_maximum_fusion.9.refs_0_, ...), custom_call_target="tpu_custom_call", output_to_operand_aliasing={{0}: (5, {}), {1}: (6, {}), {2}: (7, {})} | custom-call | flops 3221225472 | bytes 17825792 | tf_op jit(solution)/shard_map/feed_back/pallas_call | solution.py:672
  479.3 12.7 %convolution_convert_fusion.1 = bf16[1024,2048]{1,0:T(8,128)(2,1)} fusion(bf16[2048,1024]{1,0:T(8,128)(2,1)S(1)} %copy-done.4, bf16[2048,2048]{1,0:T(8,128)(2,1)} %get-tuple-element.252), kind=kOutput, calls=%fused_computation.9 | convolution fusion | flops 8592031744 | bytes 16777216 | tf_op jit(solution)/shard_map/dot_general | solution.py:932
  500.5 11.7 %owner_grad.2.refs_0_ = bf16[2,2,4,2,64,2048]{5,4,3,2,1,0:T(8,128)(2,1)S(1)} custom-call(bf16[2048,2048]{1,0:T(8,128)(2,1)} %get-tuple-element.256.h, bf16[2048,1024]{1,0:T(8,128)(2,1)S(1)} %copy-done.11), custom_call_target="tpu_custom_call" | custom-call | flops 8589934592 | bytes 16777216 | tf_op jit(solution)/shard_map/owner_grad/pallas_call | solution.py:780
  515.1 8.3 %collective-permute-done.52 = bf16[256,2048]{1,0:T(8,128)(2,1)S(1)} collective-permute-done((bf16[256,2048]{1,0:T(8,128)(2,1)S(1)}, bf16[256,2048]{1,0:T(8,128)(2,1)S(1)}, u32[]{:S(2)}, u32[]{:S(2)}) %collective-permute-start.52) | collective-permute-done | bytes 1048608 | tf_op jit(solution)/shard_map/ppermute | solution.py:29
  529.1 11.3 %owner_grad.3 = bf16[2,2,4,2,64,2048]{5,4,3,2,1,0:T(8,128)(2,1)S(1)} custom-call(bf16[2048,2048]{1,0:T(8,128)(2,1)} %get-tuple-element.256.h, bf16[2048,1024]{1,0:T(8,128)(2,1)S(1)} %copy-done.12, bf16[2,2,4,2,64,2048]{5,4,3,2,1,0:T(8,128)(2,1)S(1)} %owner_grad.2.refs_0_), custom_call_target="tpu_custom_call", output_to_operand_aliasing={{}: (2, {})} | custom-call | flops 8589934592 | bytes 16777216 | tf_op jit(solution)/shard_map/owner_grad/pallas_call | solution.py:780
  543.7 14.7 %collective-permute-done.56 = bf16[256,2048]{1,0:T(8,128)(2,1)S(1)} collective-permute-done((bf16[256,2048]{1,0:T(8,128)(2,1)S(1)}, bf16[256,2048]{1,0:T(8,128)(2,1)S(1)}, u32[]{:S(2)}, u32[]{:S(2)}) %collective-permute-start.56) | collective-permute-done | bytes 1048608 | tf_op jit(solution)/shard_map/ppermute | solution.py:29
  569.6 20.3 %collective-permute-done.58 = bf16[256,2048]{1,0:T(8,128)(2,1)S(1)} collective-permute-done((bf16[256,2048]{1,0:T(8,128)(2,1)S(1)}, bf16[256,2048]{1,0:T(8,128)(2,1)S(1)}, u32[]{:S(2)}, u32[]{:S(2)}) %collective-permute-start.58) | collective-permute-done | bytes 1048608 | tf_op jit(solution)/shard_map/ppermute | solution.py:29
  592.9 6.2 collective-permute-done.59
  607.5 20.2 %attend_back.1 = (f32[1024,512]{1,0:T(8,128)}, f32[1024,512]{1,0:T(8,128)}, bf16[1024,512]{1,0:T(8,128)(2,1)}, f32[1,1024,1]{2,1,0:T(8,128)}, f32[1,1024,1]{2,1,...) custom-call(s32[1]{0:T(128)} %bitcast.1.place, f32[1024,1536]{1,0:T(8,128)} %get-tuple-element.180.q_raw.k_raw.v_raw, ...), custom_call_target="tpu_custom_call" | custom-call | flops 2684354560 | bytes 15728640 | tf_op jit(solution)/shard_map/attend_back/pallas_call | solution.py:509
  639.6 6.6 finish.1
  646.2 8.9 %convolution_convert_fusion = bf16[2048,1536]{1,0:T(8,128)(2,1)S(1)} fusion(bf16[1024,2048]{1,0:T(8,128)(2,1)S(1)} %copy-done.120, bf16[1024,1536]{1,0:T(8,128)(2,1)} %finish.1), kind=kOutput, calls=%fused_computation | convolution fusion | flops 6445596672 | bytes 13631488 | tf_op jit(solution)/shard_map/dot_general | solution.py:932
  658.7 6.0 convolution_convert_fusion.9
  671.5 17.4 %collective-permute-done.67 = bf16[256,768]{1,0:T(8,128)(2,1)S(1)} collective-permute-done((bf16[256,768]{1,0:T(8,128)(2,1)S(1)}, bf16[256,768]{1,0:T(8,128)(2,1)S(1)}, u32[]{:S(2)}, u32[]{:S(2)}) %collective-permute-start.67) | collective-permute-done | bytes 393248 | tf_op jit(solution)/shard_map/ppermute | solution.py:29
  688.9 4.5 collective-permute-done.68
  695.5 4.1 all-to-all-start.2
  702.0 4.5 fusion.8
  708.6 5.4 convolution_convert_fusion.7
  723.7 8.8 %collective-permute-done.71 = bf16[256,1024]{1,0:T(8,128)(2,1)S(1)} collective-permute-done((bf16[256,1024]{1,0:T(8,128)(2,1)S(1)}, bf16[256,1024]{1,0:T(8,128)(2,1)S(1)}, u32[]{:S(2)}, u32[]{:S(2)}) %collective-permute-start.71) | collective-permute-done | bytes 524320 | tf_op jit(solution)/shard_map/ppermute | solution.py:29
  732.5 27.4 %collective-permute-done.69 = bf16[256,1536]{1,0:T(8,128)(2,1)S(1)} collective-permute-done((bf16[256,1536]{1,0:T(8,128)(2,1)S(1)}, bf16[256,1536]{1,0:T(8,128)(2,1)S(1)}, u32[]{:S(2)}, u32[]{:S(2)}) %collective-permute-start.69) | collective-permute-done | bytes 786464 | tf_op jit(solution)/shard_map/ppermute | solution.py:29
  783.3 5.8 convolution_convert_fusion.8
  789.2 4.2 unpack_units.1
  (599 shorter events, 264.1 us)
Async XLA Ops:
  30.4 25.6 %collective-permute-start.6 = (bf16[272,2048]{1,0:T(8,128)(2,1)S(1)}, bf16[272,2048]{1,0:T(8,128)(2,1)S(1)}, u32[]{:S(2)}, u32[]{:S(2)}) collective-permute-start(bf16[272,2048]{1,0:T(8,128)(2,1)S(1)} %fusion.26.refs_0_), channel_id=1, source_target_pairs={{0,16},{8,24},{16,0},{24,8},{1,17},{9,25},{17,1},{25,9},{2,18},{10... | collective-permute-start | bytes 3342344 | tf_op jit(solution)/shard_map/ppermute | solution.py:29
  31.9 25.3 %collective-permute-start.5 = (bf16[272,2048]{1,0:T(8,128)(2,1)S(1)}, bf16[272,2048]{1,0:T(8,128)(2,1)S(1)}, u32[]{:S(2)}, u32[]{:S(2)}) collective-permute-start(bf16[272,2048]{1,0:T(8,128)(2,1)S(1)} %fusion.26.refs_0_), channel_id=1, source_target_pairs={{0,8},{8,0},{16,24},{24,16},{1,9},{9,1},{17,25},{25,17},{2,10},{10... | collective-permute-start | bytes 3342344 | tf_op jit(solution)/shard_map/ppermute | solution.py:29
  32.6 45.9 %collective-permute-start.3 = (bf16[256,2048]{1,0:T(8,128)(2,1)S(1)}, bf16[256,2048]{1,0:T(8,128)(2,1)S(1)}, u32[]{:S(2)}, u32[]{:S(2)}) collective-permute-start(bf16[256,2048]{1,0:T(8,128)(2,1)S(1)} %maximum_maximum_fusion), channel_id=1, source_target_pairs={{0,2},{2,0},{1,3},{3,1},{4,6},{6,4},{5,7},{7,5},{8,10},{10,8},{9,1... | collective-permute-start | bytes 3145736 | tf_op jit(solution)/shard_map/ppermute | solution.py:29
  33.1 45.4 %collective-permute-start.4 = (bf16[256,2048]{1,0:T(8,128)(2,1)S(1)}, bf16[256,2048]{1,0:T(8,128)(2,1)S(1)}, u32[]{:S(2)}, u32[]{:S(2)}) collective-permute-start(bf16[256,2048]{1,0:T(8,128)(2,1)S(1)} %maximum_maximum_fusion), channel_id=1, source_target_pairs={{0,4},{4,0},{1,5},{5,1},{2,6},{6,2},{3,7},{7,3},{8,12},{12,8},{9,1... | collective-permute-start | bytes 3145736 | tf_op jit(solution)/shard_map/ppermute | solution.py:29
  60.3 47.4 %collective-permute-start.11 = (bf16[256,2048]{1,0:T(8,128)(2,1)S(1)}, bf16[256,2048]{1,0:T(8,128)(2,1)S(1)}, u32[]{:S(2)}, u32[]{:S(2)}) collective-permute-start(bf16[256,2048]{1,0:T(8,128)(2,1)S(1)} %maximum_maximum_fusion), channel_id=1, source_target_pairs={{0,1},{1,0},{2,3},{3,2},{4,5},{5,4},{6,7},{7,6},{8,9},{9,8},{10,11... | collective-permute-start | bytes 3145736 | tf_op jit(solution)/shard_map/ppermute | solution.py:29
  78.5 29.2 %collective-permute-start.12 = (bf16[256,2048]{1,0:T(8,128)(2,1)S(1)}, bf16[256,2048]{1,0:T(8,128)(2,1)S(1)}, u32[]{:S(2)}, u32[]{:S(2)}) collective-permute-start(bf16[256,2048]{1,0:T(8,128)(2,1)S(1)} %collective-permute-done.3), channel_id=1, source_target_pairs={{0,1},{1,0},{2,3},{3,2},{4,5},{5,4},{6,7},{7,6},{8,9},{9,8},{10,11... | collective-permute-start | bytes 3145736 | tf_op jit(solution)/shard_map/ppermute | solution.py:29
  78.6 30.5 %collective-permute-start.13 = (bf16[256,2048]{1,0:T(8,128)(2,1)S(1)}, bf16[256,2048]{1,0:T(8,128)(2,1)}, u32[]{:S(2)}, u32[]{:S(2)}) collective-permute-start(bf16[256,2048]{1,0:T(8,128)(2,1)S(1)} %collective-permute-done.4), channel_id=1, source_target_pairs={{0,1},{1,0},{2,3},{3,2},{4,5},{5,4},{6,7},{7,6},{8,9},{9,8},{10,11... | collective-permute-start | bytes 3145736 | tf_op jit(solution)/shard_map/ppermute | solution.py:29
  79.1 25.6 %collective-permute-start.9 = (bf16[256,1024]{1,0:T(8,128)(2,1)S(1)}, bf16[256,1024]{1,0:T(8,128)(2,1)S(1)}, u32[]{:S(2)}, u32[]{:S(2)}) collective-permute-start(bf16[256,1024]{1,0:T(8,128)(2,1)S(1)} %slice.403), channel_id=1, source_target_pairs={{0,2},{2,0},{1,3},{3,1},{4,6},{6,4},{5,7},{7,5},{8,10},{10,8},{9,1... | collective-permute-start | bytes 1572872 | tf_op jit(solution)/shard_map/ppermute | solution.py:29
  81.8 25.8 %collective-permute-start.10 = (bf16[256,1024]{1,0:T(8,128)(2,1)S(1)}, bf16[256,1024]{1,0:T(8,128)(2,1)S(1)}, u32[]{:S(2)}, u32[]{:S(2)}) collective-permute-start(bf16[256,1024]{1,0:T(8,128)(2,1)S(1)} %slice.404), channel_id=1, source_target_pairs={{0,4},{4,0},{1,5},{5,1},{2,6},{6,2},{3,7},{7,3},{8,12},{12,8},{9,1... | collective-permute-start | bytes 1572872 | tf_op jit(solution)/shard_map/ppermute | solution.py:29
  109.1 28.9 %all-to-all-start.1 = ((bf16[8,64,2048]{2,1,0:T(8,128)(2,1)}), bf16[8,64,2048]{2,1,0:T(8,128)(2,1)}, u32[]{:S(2)}, u32[]{:S(2)}) async-start(bf16[8,64,2048]{2,1,0:T(8,128)(2,1)} %pack_units.1), calls=%async_computation.1 | async-start | bytes 4194304 | tf_op jit(solution)/shard_map/all_to_all | solution.py:1045
  113.5 129.7 %all-gather.3.cloned.1.call-start = ((), (), s32[]{:S(2)}) async-start(), calls=%async_computation.7 | async-start | bytes 10485760 | tf_op jit(solution)/shard_map/all_gather | solution.py:1068
  138.1 185.8 %all-gather.5.cloned.1.call-start = ((), (), s32[]{:S(2)}) async-start(), calls=%async_computation.8 | async-start | bytes 5242880 | tf_op jit(solution)/shard_map/all_gather | solution.py:1105
  175.7 23.7 %collective-permute-start.18 = (bf16[256,2048]{1,0:T(8,128)(2,1)S(1)}, bf16[256,2048]{1,0:T(8,128)(2,1)}, u32[]{:S(2)}, u32[]{:S(2)}) collective-permute-start(bf16[256,2048]{1,0:T(8,128)(2,1)S(1)} %pad_maximum_fusion.2), channel_id=1, source_target_pairs={{0,8},{8,0},{16,24},{24,16},{1,9},{9,1},{17,25},{25,17},{2,10},{10... | collective-permute-start | bytes 3145736 | tf_op jit(solution)/shard_map/ppermute | solution.py:29
  203.5 21.9 %collective-permute-start.23 = (bf16[256,2048]{1,0:T(8,128)(2,1)S(1)}, bf16[256,2048]{1,0:T(8,128)(2,1)S(1)}, u32[]{:S(2)}, u32[]{:S(2)}) collective-permute-start(bf16[256,2048]{1,0:T(8,128)(2,1)S(1)} %fusion.23.refs_0_), channel_id=1, source_target_pairs={{0,16},{8,24},{16,0},{24,8},{1,17},{9,25},{17,1},{25,9},{2,18},{10... | collective-permute-start | bytes 3145736 | tf_op jit(solution)/shard_map/ppermute | solution.py:29
  205.3 22.4 %collective-permute-start.22 = (bf16[256,2048]{1,0:T(8,128)(2,1)S(1)}, bf16[256,2048]{1,0:T(8,128)(2,1)S(1)}, u32[]{:S(2)}, u32[]{:S(2)}) collective-permute-start(bf16[256,2048]{1,0:T(8,128)(2,1)S(1)} %fusion.23.refs_0_), channel_id=1, source_target_pairs={{0,8},{8,0},{16,24},{24,16},{1,9},{9,1},{17,25},{25,17},{2,10},{10... | collective-permute-start | bytes 3145736 | tf_op jit(solution)/shard_map/ppermute | solution.py:29
  230.1 34.3 %collective-permute-start.21 = (bf16[256,2048]{1,0:T(8,128)(2,1)S(1)}, bf16[256,2048]{1,0:T(8,128)(2,1)}, u32[]{:S(2)}, u32[]{:S(2)}) collective-permute-start(bf16[256,2048]{1,0:T(8,128)(2,1)S(1)} %fusion.23.refs_0_), channel_id=1, source_target_pairs={{0,2},{2,0},{1,3},{3,1},{4,6},{6,4},{5,7},{7,5},{8,10},{10,8},{9,1... | collective-permute-start | bytes 3145736 | tf_op jit(solution)/shard_map/ppermute | solution.py:29
  264.4 336.9 %reduce-scatter.3.cloned.1.call-start = ((), (), s32[]{:S(2)}) async-start(), calls=%async_computation.9 | async-start | bytes 5242880 | tf_op jit(solution)/shard_map/reduce_scatter | solution.py:1134
  264.8 25.6 %collective-permute-start.26 = (bf16[256,2048]{1,0:T(8,128)(2,1)}, bf16[256,2048]{1,0:T(8,128)(2,1)S(1)}, u32[]{:S(2)}, u32[]{:S(2)}) collective-permute-start(bf16[256,2048]{1,0:T(8,128)(2,1)} %collective-permute-done.21.refs_0_), channel_id=1, source_target_pairs={{0,8},{8,0},{16,24},{24,16},{1,9},{9,1},{17,25},{25,17},{2,10},{10... | collective-permute-start | bytes 3145736 | tf_op jit(solution)/shard_map/ppermute | solution.py:29
  266.4 25.3 %collective-permute-start.27 = (bf16[256,2048]{1,0:T(8,128)(2,1)}, bf16[256,2048]{1,0:T(8,128)(2,1)S(1)}, u32[]{:S(2)}, u32[]{:S(2)}) collective-permute-start(bf16[256,2048]{1,0:T(8,128)(2,1)} %collective-permute-done.21.refs_0_), channel_id=1, source_target_pairs={{0,16},{8,24},{16,0},{24,8},{1,17},{9,25},{17,1},{25,9},{2,18},{10... | collective-permute-start | bytes 3145736 | tf_op jit(solution)/shard_map/ppermute | solution.py:29
  345.4 24.2 %collective-permute-start.34 = (bf16[256,2048]{1,0:T(8,128)(2,1)S(1)}, bf16[256,2048]{1,0:T(8,128)(2,1)S(1)}, u32[]{:S(2)}, u32[]{:S(2)}) collective-permute-start(bf16[256,2048]{1,0:T(8,128)(2,1)S(1)} %pad_maximum_fusion.7), channel_id=1, source_target_pairs={{0,8},{8,0},{16,24},{24,16},{1,9},{9,1},{17,25},{25,17},{2,10},{10... | collective-permute-start | bytes 3145736 | tf_op jit(solution)/shard_map/ppermute | solution.py:29
  347.2 24.1 %collective-permute-start.37 = (bf16[256,2048]{1,0:T(8,128)(2,1)S(1)}, bf16[256,2048]{1,0:T(8,128)(2,1)S(1)}, u32[]{:S(2)}, u32[]{:S(2)}) collective-permute-start(bf16[256,2048]{1,0:T(8,128)(2,1)S(1)} %pad_maximum_fusion.8), channel_id=1, source_target_pairs={{0,16},{8,24},{16,0},{24,8},{1,17},{9,25},{17,1},{25,9},{2,18},{10... | collective-permute-start | bytes 3145736 | tf_op jit(solution)/shard_map/ppermute | solution.py:29
  348.1 24.1 %collective-permute-start.31 = (bf16[256,2048]{1,0:T(8,128)(2,1)S(1)}, bf16[256,2048]{1,0:T(8,128)(2,1)S(1)}, u32[]{:S(2)}, u32[]{:S(2)}) collective-permute-start(bf16[256,2048]{1,0:T(8,128)(2,1)S(1)} %pad_maximum_fusion.6), channel_id=1, source_target_pairs={{0,2},{2,0},{1,3},{3,1},{4,6},{6,4},{5,7},{7,5},{8,10},{10,8},{9,1... | collective-permute-start | bytes 3145736 | tf_op jit(solution)/shard_map/ppermute | solution.py:29
  370.1 23.5 %collective-permute-start.35 = (bf16[256,2048]{1,0:T(8,128)(2,1)S(1)}, bf16[256,2048]{1,0:T(8,128)(2,1)S(1)}, u32[]{:S(2)}, u32[]{:S(2)}) collective-permute-start(bf16[256,2048]{1,0:T(8,128)(2,1)S(1)} %add_convert_fusion.5), channel_id=1, source_target_pairs={{0,16},{8,24},{16,0},{24,8},{1,17},{9,25},{17,1},{25,9},{2,18},{10... | collective-permute-start | bytes 3145736 | tf_op jit(solution)/shard_map/ppermute | solution.py:29
  371.7 22.9 %collective-permute-start.38 = (bf16[256,2048]{1,0:T(8,128)(2,1)S(1)}, bf16[256,2048]{1,0:T(8,128)(2,1)S(1)}, u32[]{:S(2)}, u32[]{:S(2)}) collective-permute-start(bf16[256,2048]{1,0:T(8,128)(2,1)S(1)} %add_convert_fusion.4), channel_id=1, source_target_pairs={{0,2},{2,0},{1,3},{3,1},{4,6},{6,4},{5,7},{7,5},{8,10},{10,8},{9,1... | collective-permute-start | bytes 3145736 | tf_op jit(solution)/shard_map/ppermute | solution.py:29
  372.6 23.1 %collective-permute-start.32 = (bf16[256,2048]{1,0:T(8,128)(2,1)S(1)}, bf16[256,2048]{1,0:T(8,128)(2,1)S(1)}, u32[]{:S(2)}, u32[]{:S(2)}) collective-permute-start(bf16[256,2048]{1,0:T(8,128)(2,1)S(1)} %add_convert_fusion.6), channel_id=1, source_target_pairs={{0,8},{8,0},{16,24},{24,16},{1,9},{9,1},{17,25},{25,17},{2,10},{10... | collective-permute-start | bytes 3145736 | tf_op jit(solution)/shard_map/ppermute | solution.py:29
  398.8 22.2 %collective-permute-start.40 = (bf16[256,2048]{1,0:T(8,128)(2,1)S(1)}, bf16[256,2048]{1,0:T(8,128)(2,1)S(1)}, u32[]{:S(2)}, u32[]{:S(2)}) collective-permute-start(bf16[256,2048]{1,0:T(8,128)(2,1)S(1)} %fusion.17.refs_0_), channel_id=1, source_target_pairs={{0,16},{8,24},{16,0},{24,8},{1,17},{9,25},{17,1},{25,9},{2,18},{10... | collective-permute-start | bytes 3145736 | tf_op jit(solution)/shard_map/ppermute | solution.py:29
  399.9 23.6 %collective-permute-start.39 = (bf16[256,2048]{1,0:T(8,128)(2,1)S(1)}, bf16[256,2048]{1,0:T(8,128)(2,1)S(1)}, u32[]{:S(2)}, u32[]{:S(2)}) collective-permute-start(bf16[256,2048]{1,0:T(8,128)(2,1)S(1)} %fusion.17.refs_0_), channel_id=1, source_target_pairs={{0,8},{8,0},{16,24},{24,16},{1,9},{9,1},{17,25},{25,17},{2,10},{10... | collective-permute-start | bytes 3145736 | tf_op jit(solution)/shard_map/ppermute | solution.py:29
  401.3 24.0 %collective-permute-start.41 = (bf16[256,2048]{1,0:T(8,128)(2,1)S(1)}, bf16[256,2048]{1,0:T(8,128)(2,1)S(1)}, u32[]{:S(2)}, u32[]{:S(2)}) collective-permute-start(bf16[256,2048]{1,0:T(8,128)(2,1)S(1)} %fusion.17.refs_0_), channel_id=1, source_target_pairs={{0,2},{2,0},{1,3},{3,1},{4,6},{6,4},{5,7},{7,5},{8,10},{10,8},{9,1... | collective-permute-start | bytes 3145736 | tf_op jit(solution)/shard_map/ppermute | solution.py:29
  420.9 28.8 %collective-permute-start.42 = (bf16[256,2048]{1,0:T(8,128)(2,1)S(1)}, bf16[256,2048]{1,0:T(8,128)(2,1)S(1)}, u32[]{:S(2)}, u32[]{:S(2)}) collective-permute-start(bf16[256,2048]{1,0:T(8,128)(2,1)S(1)} %collective-permute-done.40.refs_2_), channel_id=1, source_target_pairs={{0,8},{8,0},{16,24},{24,16},{1,9},{9,1},{17,25},{25,17},{2,10},{10... | collective-permute-start | bytes 3145736 | tf_op jit(solution)/shard_map/ppermute | solution.py:29
  423.4 23.6 %collective-permute-start.43 = (bf16[256,2048]{1,0:T(8,128)(2,1)S(1)}, bf16[256,2048]{1,0:T(8,128)(2,1)S(1)}, u32[]{:S(2)}, u32[]{:S(2)}) collective-permute-start(bf16[256,2048]{1,0:T(8,128)(2,1)S(1)} %collective-permute-done.39.refs_1_), channel_id=1, source_target_pairs={{0,2},{2,0},{1,3},{3,1},{4,6},{6,4},{5,7},{7,5},{8,10},{10,8},{9,1... | collective-permute-start | bytes 3145736 | tf_op jit(solution)/shard_map/ppermute | solution.py:29
  425.3 23.0 %collective-permute-start.44 = (bf16[256,2048]{1,0:T(8,128)(2,1)S(1)}, bf16[256,2048]{1,0:T(8,128)(2,1)S(1)}, u32[]{:S(2)}, u32[]{:S(2)}) collective-permute-start(bf16[256,2048]{1,0:T(8,128)(2,1)S(1)} %collective-permute-done.41.refs_3_), channel_id=1, source_target_pairs={{0,16},{8,24},{16,0},{24,8},{1,17},{9,25},{17,1},{25,9},{2,18},{10... | collective-permute-start | bytes 3145736 | tf_op jit(solution)/shard_map/ppermute | solution.py:29
  447.1 20.5 %collective-permute-start.46 = (bf16[256,768]{1,0:T(8,128)(2,1)S(1)}, bf16[256,768]{1,0:T(8,128)(2,1)S(1)}, u32[]{:S(2)}, u32[]{:S(2)}) collective-permute-start(bf16[256,768]{1,0:T(8,128)(2,1)S(1)} %slice.537), channel_id=1, source_target_pairs={{0,16},{8,24},{16,0},{24,8},{1,17},{9,25},{17,1},{25,9},{2,18},{10... | collective-permute-start | bytes 1179656 | tf_op jit(solution)/shard_map/ppermute | solution.py:29
  492.1 203.4 %reduce-scatter.5.cloned.1.call-start = ((), (), s32[]{:S(2)}) async-start(), calls=%async_computation.10 | async-start | bytes 10485760 | tf_op jit(solution)/shard_map/reduce_scatter | solution.py:1134
  496.6 26.8 %collective-permute-start.52 = (bf16[256,2048]{1,0:T(8,128)(2,1)S(1)}, bf16[256,2048]{1,0:T(8,128)(2,1)S(1)}, u32[]{:S(2)}, u32[]{:S(2)}) collective-permute-start(bf16[256,2048]{1,0:T(8,128)(2,1)S(1)} %pad_maximum_fusion.11), channel_id=1, source_target_pairs={{0,2},{2,0},{1,3},{3,1},{4,6},{6,4},{5,7},{7,5},{8,10},{10,8},{9,1... | collective-permute-start | bytes 3145736 | tf_op jit(solution)/shard_map/ppermute | solution.py:29
  499.1 24.3 %collective-permute-start.51 = (bf16[256,2048]{1,0:T(8,128)(2,1)S(1)}, bf16[256,2048]{1,0:T(8,128)(2,1)S(1)}, u32[]{:S(2)}, u32[]{:S(2)}) collective-permute-start(bf16[256,2048]{1,0:T(8,128)(2,1)S(1)} %pad_maximum_fusion.10), channel_id=1, source_target_pairs={{0,8},{8,0},{16,24},{24,16},{1,9},{9,1},{17,25},{25,17},{2,10},{10... | collective-permute-start | bytes 3145736 | tf_op jit(solution)/shard_map/ppermute | solution.py:29
  523.8 34.6 %collective-permute-start.56 = (bf16[256,2048]{1,0:T(8,128)(2,1)S(1)}, bf16[256,2048]{1,0:T(8,128)(2,1)S(1)}, u32[]{:S(2)}, u32[]{:S(2)}) collective-permute-start(bf16[256,2048]{1,0:T(8,128)(2,1)S(1)} %add_convert_fusion), channel_id=1, source_target_pairs={{0,2},{2,0},{1,3},{3,1},{4,6},{6,4},{5,7},{7,5},{8,10},{10,8},{9,1... | collective-permute-start | bytes 3145736 | tf_op jit(solution)/shard_map/ppermute | solution.py:29
  526.1 32.3 %collective-permute-start.55 = (bf16[256,2048]{1,0:T(8,128)(2,1)S(1)}, bf16[256,2048]{1,0:T(8,128)(2,1)S(1)}, u32[]{:S(2)}, u32[]{:S(2)}) collective-permute-start(bf16[256,2048]{1,0:T(8,128)(2,1)S(1)} %add_convert_fusion.1), channel_id=1, source_target_pairs={{0,16},{8,24},{16,0},{24,8},{1,17},{9,25},{17,1},{25,9},{2,18},{10... | collective-permute-start | bytes 3145736 | tf_op jit(solution)/shard_map/ppermute | solution.py:29
  527.5 30.9 %collective-permute-start.54 = (bf16[256,2048]{1,0:T(8,128)(2,1)S(1)}, bf16[256,2048]{1,0:T(8,128)(2,1)S(1)}, u32[]{:S(2)}, u32[]{:S(2)}) collective-permute-start(bf16[256,2048]{1,0:T(8,128)(2,1)S(1)} %add_convert_fusion.2), channel_id=1, source_target_pairs={{0,8},{8,0},{16,24},{24,16},{1,9},{9,1},{17,25},{25,17},{2,10},{10... | collective-permute-start | bytes 3145736 | tf_op jit(solution)/shard_map/ppermute | solution.py:29
  568.2 21.6 %collective-permute-start.58 = (bf16[256,2048]{1,0:T(8,128)(2,1)S(1)}, bf16[256,2048]{1,0:T(8,128)(2,1)S(1)}, u32[]{:S(2)}, u32[]{:S(2)}) collective-permute-start(bf16[256,2048]{1,0:T(8,128)(2,1)S(1)} %get-tuple-element.295), channel_id=1, source_target_pairs={{0,16},{8,24},{16,0},{24,8},{1,17},{9,25},{17,1},{25,9},{2,18},{10... | collective-permute-start | bytes 3145736 | tf_op jit(solution)/shard_map/ppermute | solution.py:29
  569.6 22.3 %collective-permute-start.57 = (bf16[256,2048]{1,0:T(8,128)(2,1)S(1)}, bf16[256,2048]{1,0:T(8,128)(2,1)S(1)}, u32[]{:S(2)}, u32[]{:S(2)}) collective-permute-start(bf16[256,2048]{1,0:T(8,128)(2,1)S(1)} %get-tuple-element.295), channel_id=1, source_target_pairs={{0,8},{8,0},{16,24},{24,16},{1,9},{9,1},{17,25},{25,17},{2,10},{10... | collective-permute-start | bytes 3145736 | tf_op jit(solution)/shard_map/ppermute | solution.py:29
  668.5 20.4 %collective-permute-start.67 = (bf16[256,768]{1,0:T(8,128)(2,1)S(1)}, bf16[256,768]{1,0:T(8,128)(2,1)S(1)}, u32[]{:S(2)}, u32[]{:S(2)}) collective-permute-start(bf16[256,768]{1,0:T(8,128)(2,1)S(1)} %get-tuple-element.373), channel_id=1, source_target_pairs={{0,2},{2,0},{1,3},{3,1},{4,6},{6,4},{5,7},{7,5},{8,10},{10,8},{9,1... | collective-permute-start | bytes 1179656 | tf_op jit(solution)/shard_map/ppermute | solution.py:29
  671.4 22.0 %collective-permute-start.68 = (bf16[256,768]{1,0:T(8,128)(2,1)S(1)}, bf16[256,768]{1,0:T(8,128)(2,1)S(1)}, u32[]{:S(2)}, u32[]{:S(2)}) collective-permute-start(bf16[256,768]{1,0:T(8,128)(2,1)S(1)} %get-tuple-element.372), channel_id=1, source_target_pairs={{0,4},{4,0},{1,5},{5,1},{2,6},{6,2},{3,7},{7,3},{8,12},{12,8},{9,1... | collective-permute-start | bytes 1179656 | tf_op jit(solution)/shard_map/ppermute | solution.py:29
  695.5 65.3 %all-to-all-start.2 = ((bf16[8,64,2048]{2,1,0:T(8,128)(2,1)}), bf16[8,64,2048]{2,1,0:T(8,128)(2,1)S(1)}, u32[]{:S(2)}, u32[]{:S(2)}) async-start(bf16[8,64,2048]{2,1,0:T(8,128)(2,1)} %reduce-scatter.5.cloned.1.call-done), calls=%async_computation.4 | async-start | bytes 4194304 | tf_op jit(solution)/shard_map/all_to_all | solution.py:1195
  717.7 42.2 %collective-permute-start.69 = (bf16[256,1536]{1,0:T(8,128)(2,1)S(1)}, bf16[256,1536]{1,0:T(8,128)(2,1)S(1)}, u32[]{:S(2)}, u32[]{:S(2)}) collective-permute-start(bf16[256,1536]{1,0:T(8,128)(2,1)S(1)} %copy-done.85), channel_id=1, source_target_pairs={{0,2},{2,0},{1,3},{3,1},{4,6},{6,4},{5,7},{7,5},{8,10},{10,8},{9,1... | collective-permute-start | bytes 2359304 | tf_op jit(solution)/shard_map/ppermute | solution.py:29
  719.2 41.6 %collective-permute-start.70 = (bf16[256,1536]{1,0:T(8,128)(2,1)S(1)}, bf16[256,1536]{1,0:T(8,128)(2,1)}, u32[]{:S(2)}, u32[]{:S(2)}) collective-permute-start(bf16[256,1536]{1,0:T(8,128)(2,1)S(1)} %copy-done.84), channel_id=1, source_target_pairs={{0,4},{4,0},{1,5},{5,1},{2,6},{6,2},{3,7},{7,3},{8,12},{12,8},{9,1... | collective-permute-start | bytes 2359304 | tf_op jit(solution)/shard_map/ppermute | solution.py:29
  764.1 29.4 %all-to-all-start.3 = ((bf16[4,64,1536]{2,1,0:T(8,128)(2,1)}), bf16[4,64,1536]{2,1,0:T(8,128)(2,1)S(1)}, u32[]{:S(2)}, u32[]{:S(2)}) async-start(bf16[4,64,1536]{2,1,0:T(8,128)(2,1)} %bitcast.184), calls=%async_computation.5 | async-start | bytes 1572864 | tf_op jit(solution)/shard_map/all_to_all | solution.py:1202
  774.9 31.2 %collective-permute-start.77 = (bf16[256,2048]{1,0:T(8,128)(2,1)}, bf16[256,2048]{1,0:T(8,128)(2,1)}, u32[]{:S(2)}, u32[]{:S(2)}) collective-permute-start(bf16[256,2048]{1,0:T(8,128)(2,1)} %pad_maximum_fusion.15), channel_id=1, source_target_pairs={{0,8},{8,0},{16,24},{24,16},{1,9},{9,1},{17,25},{25,17},{2,10},{10... | collective-permute-start | bytes 3145736 | tf_op jit(solution)/shard_map/ppermute | solution.py:29
  778.3 27.8 %collective-permute-start.78 = (bf16[256,2048]{1,0:T(8,128)(2,1)}, bf16[256,2048]{1,0:T(8,128)(2,1)}, u32[]{:S(2)}, u32[]{:S(2)}) collective-permute-start(bf16[256,2048]{1,0:T(8,128)(2,1)} %pad_maximum_fusion.16), channel_id=1, source_target_pairs={{0,16},{8,24},{16,0},{24,8},{1,17},{9,25},{17,1},{25,9},{2,18},{10... | collective-permute-start | bytes 3145736 | tf_op jit(solution)/shard_map/ppermute | solution.py:29
  (169 other events, 1672.8 us)
Sparse Core Ops, SparseCore 0:
  138.2 104.9 all-gather.2
  264.5 59.3 all-gather.4
  492.2 66.5 reduce-scatter.2
  561.4 118.3 reduce-scatter.4

commit v5 on v4

--- a/solution.py
+++ b/solution.py
@@ -300,24 +300,37 @@
 
 def regroup(blocks, order):
     number, rows, width = blocks.shape
-
-    def kernel(ref, out, sems):
-        copies = [
-            pltpu.make_async_copy(ref.at[at], out.at[pl.ds(i * rows, rows)], sems.at[i])
+    group = math.gcd(number, 8)
+
+    def kernel(ref, out, held, sems):
+        arrive = [
+            pltpu.make_async_copy(ref.at[at], held.at[pl.ds(i * rows, rows)], sems.at[i])
             for i, at in enumerate(order)
         ]
-        for copy in copies:
+        leave = []
+        for i in range(0, number, group):
+            here = pl.ds(i * rows, group * rows)
+            sem = sems.at[number + i // group]
+            leave.append(pltpu.make_async_copy(held.at[here], out.at[here], sem))
+        for copy in arrive:
             copy.start()
-        for copy in copies:
+        for i, copy in enumerate(leave):
+            for piece in arrive[i * group : (i + 1) * group]:
+                piece.wait()
+            copy.start()
+        for copy in leave:
             copy.wait()
 
     return pl.pallas_call(
         kernel,
-        in_specs=[pl.BlockSpec(memory_space=pltpu.HBM)],
-        out_specs=pl.BlockSpec(memory_space=pltpu.VMEM),
+        in_specs=[pl.BlockSpec(memory_space=pl.ANY)],
+        out_specs=pl.BlockSpec(memory_space=pl.ANY),
         out_shape=jax.ShapeDtypeStruct((number * rows, width), blocks.dtype),
-        scratch_shapes=[pltpu.SemaphoreType.DMA((number,))],
-        compiler_params=pltpu.CompilerParams(vmem_limit_bytes=24 * 1024 * 1024),
+        scratch_shapes=[
+            pltpu.VMEM((number * rows, width), blocks.dtype),
+            pltpu.SemaphoreType.DMA((number + number // group,)),
+        ],
+        compiler_params=pltpu.CompilerParams(vmem_limit_bytes=56 * 1024 * 1024),
         name="regroup",
     )(blocks)
 

time: 825 us -> 825 us (level)
    unnamed x249 -> x245, local copies, waits for them, and re-layouts: 40.9 us -> 34.4 us
  transfers between devices with their start and end apart: 92 -> 92, of which waited for: 45 -> 45; matrix products, arithmetic and copies ran while one was open for 14% -> 14% of each run, Pallas kernels for 21% -> 22%
where the time goes in v5:
time: 825 us; the launch traced here: 816 us
  waiting for transfers between devices  334 us (40%)
  Pallas kernels  194 us (24%)
  starting transfers between devices  115 us (14%)
  local copies, waits for them, and re-layouts  54.2 us (7%)
  matrix products  53.6 us (6%)
  other arithmetic  49.1 us (6%)
  between operations  16.5 us (2%)
    ppermute x83, waiting for transfers between devices, swap(): lax.ppermute(block, axis, [(i, i ^ mask) for i in range(lax.axis_size(axi...  311 us
    ppermute x83, starting transfers between devices, swap(): lax.ppermute(block, axis, [(i, i ^ mask) for i in range(lax.axis_size(axi...  95.9 us
    pallas_call x7, Pallas kernels, feed_call(): pl.pallas_call(body, grid=(steps,), in_specs=[somewhere] * number + in_sp...  86.2 us
    unnamed x245, local copies, waits for them, and re-layouts  34.4 us
    dot_general x3, matrix products, t_dot(): lax.dot_general(left, right, (((0,), (0,)), ((), ())), preferred_element_...  26.2 us
    dot_general x8, matrix products, dot_t(): lax.dot_general(left, right, (((1,), (1,)), ((), ())), preferred_element_...  23.6 us
    pallas_call x2, Pallas kernels, owner_grad(): pl.pallas_call(kernel, grid=(n_seq,), in_specs=[pl.BlockSpec((tokens, col...  23 us
    pallas_call x1, Pallas kernels, attend_back(): pl.pallas_call(functools.partial(backward_kernel, scale * math.log2(math....  20.1 us
  transfers between devices with their start and end apart: 92, of which 45 were waited for; matrix products, arithmetic and copies ran while one was open for 14% of the time, Pallas kernels for 22%

profile of v5, /device:TPU:0, one launch (start us, length us, event | category | flops | bytes accessed | tf_op | source)
XLA Modules:
  0.0 816.4 jit_solution(9531241025030046617)
XLA Ops:
  25.9 4.1 all-to-all-done
  35.7 20.2 %collective-permute-done.6.refs_2_ = bf16[272,2048]{1,0:T(8,128)(2,1)S(1)} collective-permute-done((bf16[272,2048]{1,0:T(8,128)(2,1)S(1)}, bf16[272,2048]{1,0:T(8,128)(2,1)S(1)}, u32[]{:S(2)}, u32[]{:S(2)}) %collective-permute-start.6) | collective-permute-done | bytes 1114144 | tf_op jit(solution)/shard_map/ppermute | solution.py:29
  60.4 8.5 %collective-permute-done.7 = bf16[272,1024]{1,0:T(8,128)(2,1)S(1)} collective-permute-done((bf16[272,1024]{1,0:T(8,128)(2,1)S(1)}, bf16[272,1024]{1,0:T(8,128)(2,1)S(1)}, u32[]{:S(2)}, u32[]{:S(2)}) %collective-permute-start.7) | collective-permute-done | bytes 557088 | tf_op jit(solution)/shard_map/ppermute | solution.py:29
  70.5 8.0 collective-permute-done.3
  84.5 20.2 %collective-permute-done.9 = bf16[256,1024]{1,0:T(8,128)(2,1)S(1)} collective-permute-done((bf16[256,1024]{1,0:T(8,128)(2,1)S(1)}, bf16[256,1024]{1,0:T(8,128)(2,1)S(1)}, u32[]{:S(2)}, u32[]{:S(2)}) %collective-permute-start.9) | collective-permute-done | bytes 524320 | tf_op jit(solution)/shard_map/ppermute | solution.py:29
  109.0 4.4 all-to-all-start.1
  117.2 14.6 %project.1 = (f32[1024,1536]{1,0:T(8,128)}, f32[2,1024,1]{2,1,0:T(8,128)}, bf16[1024,2048]{1,0:T(8,128)(2,1)}, bf16[2048,1536]{1,0:T(8,128)(2,1)}, bf16[512,2048]{1,0:T(8,128)(2,1)}) custom-call(s32[32]{0:T(128)} %stack.206.table, s32[8]{0:T(128)} %stack.207.out_table, bf16[272,2048]{1,0:T(8,128)(2,1)} %copy-done.62, bf16[272,2048]{1,0:T(8,128)(2,1)} %copy-done.89, ...), custom_call_target="tpu_custom_call" | custom-call | flops 6442450944 | bytes 10485760 | tf_op jit(solution)/shard_map/project/pallas_call | solution.py:269
  131.8 6.2 all-to-all-done.1
  154.0 10.1 %attend.1 = (f32[1024,512]{1,0:T(8,128)S(1)}, bf16[1024,512]{1,0:T(8,128)(2,1)S(1)}, f32[4,4,1,256]{3,2,1,0:T(1,128)S(1)}) custom-call(s32[1]{0:T(128)} %bitcast.1.place, f32[1024,1536]{1,0:T(8,128)S(1)} %copy-done, f32[1024,1536]{1,0:T(8,128)S(1)} %copy-done, f32[1024,1536]{1,0:T(8,128)S(1)} %copy-done, f32[2,1024,1]{2,1,0:T(8,128)S(1)} %rsqrt.28.q_inv.k_inv, ...), custom_call_target="tpu_custom_call" | custom-call | flops 1073741824 | bytes 9437184 | tf_op jit(solution)/shard_map/attend/pallas_call | solution.py:488
  169.3 6.1 collective-permute-done.17
  182.4 16.9 %collective-permute-done.18 = bf16[256,2048]{1,0:T(8,128)(2,1)} collective-permute-done((bf16[256,2048]{1,0:T(8,128)(2,1)S(1)}, bf16[256,2048]{1,0:T(8,128)(2,1)}, u32[]{:S(2)}, u32[]{:S(2)}) %collective-permute-start.18) | collective-permute-done | bytes 1048608 | tf_op jit(solution)/shard_map/ppermute | solution.py:29
  205.6 19.8 %collective-permute-done.23.refs_0_ = bf16[256,2048]{1,0:T(8,128)(2,1)S(1)} collective-permute-done((bf16[256,2048]{1,0:T(8,128)(2,1)S(1)}, bf16[256,2048]{1,0:T(8,128)(2,1)S(1)}, u32[]{:S(2)}, u32[]{:S(2)}) %collective-permute-start.23) | collective-permute-done | bytes 1048608 | tf_op jit(solution)/shard_map/ppermute | solution.py:29
  230.0 5.9 collective-permute-start.21
  238.5 4.6 all-gather.3.cloned.1.call-done.ref
  243.1 7.3 regroup.1.refs_2_.refs_3_.refs_4_.refs_1_.refs_13_.refs_10_
  250.4 10.3 %feed.4 = (bf16[2048,2048]{1,0:T(8,128)(2,1)}, bf16[2048,1024]{1,0:T(8,128)(2,1)}, bf16[256,1024]{1,0:T(8,128)(2,1)S(1)}, bf16[256,1024]{1,0:T(8,128)(2,1)S(1)},...) custom-call(bf16[256,2048]{1,0:T(8,128)(2,1)S(1)} %fusion.23.refs_0_, bf16[256,2048]{1,0:T(8,128)(2,1)} %copy-done.96, ...), custom_call_target="tpu_custom_call" | custom-call | flops 6442450944 | bytes 23068672 | tf_op jit(solution)/shard_map/feed/pallas_call | solution.py:685
  267.4 10.3 %feed.5 = (bf16[2048,2048]{1,0:T(8,128)(2,1)}, bf16[2048,1024]{1,0:T(8,128)(2,1)}, bf16[256,1024]{1,0:T(8,128)(2,1)S(1)}, bf16[256,1024]{1,0:T(8,128)(2,1)S(1)},...) custom-call(bf16[256,2048]{1,0:T(8,128)(2,1)S(1)} %collective-permute-, ...), custom_call_target="tpu_custom_call", output_to_operand_aliasing={{0}: (4, {}), {1}: (5, {})} | custom-call | flops 6442450944 | bytes 23068672 | tf_op jit(solution)/shard_map/feed/pallas_call | solution.py:685
  277.8 12.3 %collective-permute-done.26.refs_1_ = bf16[256,2048]{1,0:T(8,128)(2,1)S(1)} collective-permute-done((bf16[256,2048]{1,0:T(8,128)(2,1)}, bf16[256,2048]{1,0:T(8,128)(2,1)S(1)}, u32[]{:S(2)}, u32[]{:S(2)}) %collective-permute-start.26) | collective-permute-done | bytes 1048608 | tf_op jit(solution)/shard_map/ppermute | solution.py:29
  293.5 13.2 %feed.6 = (bf16[2048,2048]{1,0:T(8,128)(2,1)}, bf16[2048,1024]{1,0:T(8,128)(2,1)}, bf16[256,1024]{1,0:T(8,128)(2,1)S(1)}, bf16[256,1024]{1,0:T(8,128)(2,1)S(1)},...) custom-call(bf16[256,2048]{1,0:T(8,128)(2,1)} %collective-permute-do, ...), custom_call_target="tpu_custom_call", output_to_operand_aliasing={{0}: (5, {}), {1}: (6, {})} | custom-call | flops 9663676416 | bytes 28311552 | tf_op jit(solution)/shard_map/feed/pallas_call | solution.py:685
  309.7 6.1 feed.7
  315.8 7.7 all-gather.5.cloned.1.call-done.weight.refs_12_.refs_9_.refs_3_
  327.9 5.7 feed_down.3
  336.9 5.8 feed_down.2
  348.1 21.2 %collective-permute-done.34 = bf16[256,2048]{1,0:T(8,128)(2,1)S(1)} collective-permute-done((bf16[256,2048]{1,0:T(8,128)(2,1)S(1)}, bf16[256,2048]{1,0:T(8,128)(2,1)S(1)}, u32[]{:S(2)}, u32[]{:S(2)}) %collective-permute-start.34) | collective-permute-done | bytes 1048608 | tf_op jit(solution)/shard_map/ppermute | solution.py:29
  373.4 19.9 %collective-permute-done.35 = bf16[256,2048]{1,0:T(8,128)(2,1)S(1)} collective-permute-done((bf16[256,2048]{1,0:T(8,128)(2,1)S(1)}, bf16[256,2048]{1,0:T(8,128)(2,1)S(1)}, u32[]{:S(2)}, u32[]{:S(2)}) %collective-permute-start.35) | collective-permute-done | bytes 1048608 | tf_op jit(solution)/shard_map/ppermute | solution.py:29
  402.1 18.5 %collective-permute-done.40.refs_2_ = bf16[256,2048]{1,0:T(8,128)(2,1)S(1)} collective-permute-done((bf16[256,2048]{1,0:T(8,128)(2,1)S(1)}, bf16[256,2048]{1,0:T(8,128)(2,1)S(1)}, u32[]{:S(2)}, u32[]{:S(2)}) %collective-permute-start.40) | collective-permute-done | bytes 1048608 | tf_op jit(solution)/shard_map/ppermute | solution.py:29
  426.0 20.8 %feed_back.3 = (bf16[2048,2048]{1,0:T(8,128)(2,1)}, bf16[2048,1024]{1,0:T(8,128)(2,1)}, bf16[2048,1024]{1,0:T(8,128)(2,1)}, bf16[256,2048]{1,0:T(8,128)(2,1)}, b...) custom-call(bf16[256,2048]{1,0:T(8,128)(2,1)} %copy-done.77, ...), custom_call_target="tpu_custom_call" | custom-call | flops 12884901888 | bytes 33554432 | tf_op jit(solution)/shard_map/feed_back/pallas_call | solution.py:685
  450.6 16.8 %feed_back.4 = (bf16[2048,2048]{1,0:T(8,128)(2,1)}, bf16[2048,1024]{1,0:T(8,128)(2,1)}, bf16[2048,1024]{1,0:T(8,128)(2,1)}, bf16[256,2048]{1,0:T(8,128)(2,1)}, b...) custom-call(bf16[256,2048]{1,0:T(8,128)(2,1)} %copy-done.102, ...), custom_call_target="tpu_custom_call", output_to_operand_aliasing={{0}: (11, {}), {1}: (12, {}), {2}: (13, {})} | custom-call | flops 9663676416 | bytes 28311552 | tf_op jit(solution)/shard_map/feed_back/pallas_call | solution.py:685
  467.6 8.6 %feed_back.5 = (bf16[2048,2048]{1,0:T(8,128)(2,1)}, bf16[2048,1024]{1,0:T(8,128)(2,1)}, bf16[2048,1024]{1,0:T(8,128)(2,1)}, bf16[256,2048]{1,0:T(8,128)(2,1)S(1)}) custom-call(bf16[256,2048]{1,0:T(8,128)(2,1)S(1)} %pad_maximum_fusion.9.refs_0_, ...), custom_call_target="tpu_custom_call", output_to_operand_aliasing={{0}: (5, {}), {1}: (6, {}), {2}: (7, {})} | custom-call | flops 3221225472 | bytes 17825792 | tf_op jit(solution)/shard_map/feed_back/pallas_call | solution.py:685
  479.1 12.8 %convolution_convert_fusion.1 = bf16[1024,2048]{1,0:T(8,128)(2,1)} fusion(bf16[2048,1024]{1,0:T(8,128)(2,1)S(1)} %copy-done.3, bf16[2048,2048]{1,0:T(8,128)(2,1)} %get-tuple-element.252), kind=kOutput, calls=%fused_computation.9 | convolution fusion | flops 8592031744 | bytes 16777216 | tf_op jit(solution)/shard_map/dot_general | solution.py:945
  500.3 11.7 %owner_grad.2.refs_0_ = bf16[2,2,4,2,64,2048]{5,4,3,2,1,0:T(8,128)(2,1)S(1)} custom-call(bf16[2048,2048]{1,0:T(8,128)(2,1)} %get-tuple-element.256.h, bf16[2048,1024]{1,0:T(8,128)(2,1)S(1)} %copy-done.9), custom_call_target="tpu_custom_call" | custom-call | flops 8589934592 | bytes 16777216 | tf_op jit(solution)/shard_map/owner_grad/pallas_call | solution.py:793
  514.8 8.4 %collective-permute-done.52 = bf16[256,2048]{1,0:T(8,128)(2,1)S(1)} collective-permute-done((bf16[256,2048]{1,0:T(8,128)(2,1)S(1)}, bf16[256,2048]{1,0:T(8,128)(2,1)S(1)}, u32[]{:S(2)}, u32[]{:S(2)}) %collective-permute-start.52) | collective-permute-done | bytes 1048608 | tf_op jit(solution)/shard_map/ppermute | solution.py:29
  528.6 11.3 %owner_grad.3 = bf16[2,2,4,2,64,2048]{5,4,3,2,1,0:T(8,128)(2,1)S(1)} custom-call(bf16[2048,2048]{1,0:T(8,128)(2,1)} %get-tuple-element.256.h, bf16[2048,1024]{1,0:T(8,128)(2,1)S(1)} %copy-done.10, bf16[2,2,4,2,64,2048]{5,4,3,2,1,0:T(8,128)(2,1)S(1)} %owner_grad.2.refs_0_), custom_call_target="tpu_custom_call", output_to_operand_aliasing={{}: (2, {})} | custom-call | flops 8589934592 | bytes 16777216 | tf_op jit(solution)/shard_map/owner_grad/pallas_call | solution.py:793
  543.2 15.1 %collective-permute-done.56 = bf16[256,2048]{1,0:T(8,128)(2,1)S(1)} collective-permute-done((bf16[256,2048]{1,0:T(8,128)(2,1)S(1)}, bf16[256,2048]{1,0:T(8,128)(2,1)S(1)}, u32[]{:S(2)}, u32[]{:S(2)}) %collective-permute-start.56) | collective-permute-done | bytes 1048608 | tf_op jit(solution)/shard_map/ppermute | solution.py:29
  569.4 20.9 %collective-permute-done.58 = bf16[256,2048]{1,0:T(8,128)(2,1)S(1)} collective-permute-done((bf16[256,2048]{1,0:T(8,128)(2,1)S(1)}, bf16[256,2048]{1,0:T(8,128)(2,1)S(1)}, u32[]{:S(2)}, u32[]{:S(2)}) %collective-permute-start.58) | collective-permute-done | bytes 1048608 | tf_op jit(solution)/shard_map/ppermute | solution.py:29
  592.7 6.9 collective-permute-done.59
  606.9 20.1 %attend_back.1 = (f32[1024,512]{1,0:T(8,128)}, f32[1024,512]{1,0:T(8,128)}, bf16[1024,512]{1,0:T(8,128)(2,1)}, f32[1,1024,1]{2,1,0:T(8,128)}, f32[1,1024,1]{2,1,...) custom-call(s32[1]{0:T(128)} %bitcast.1.place, f32[1024,1536]{1,0:T(8,128)} %get-tuple-element.180.q_raw.k_raw.v_raw, ...), custom_call_target="tpu_custom_call" | custom-call | flops 2684354560 | bytes 15728640 | tf_op jit(solution)/shard_map/attend_back/pallas_call | solution.py:522
  639.1 6.6 finish.1
  645.7 8.9 %convolution_convert_fusion = bf16[2048,1536]{1,0:T(8,128)(2,1)S(1)} fusion(bf16[1024,2048]{1,0:T(8,128)(2,1)S(1)} %copy-done.118, bf16[1024,1536]{1,0:T(8,128)(2,1)} %finish.1), kind=kOutput, calls=%fused_computation | convolution fusion | flops 6445596672 | bytes 13631488 | tf_op jit(solution)/shard_map/dot_general | solution.py:945
  658.2 6.0 convolution_convert_fusion.9
  670.9 17.2 %collective-permute-done.67 = bf16[256,768]{1,0:T(8,128)(2,1)S(1)} collective-permute-done((bf16[256,768]{1,0:T(8,128)(2,1)S(1)}, bf16[256,768]{1,0:T(8,128)(2,1)S(1)}, u32[]{:S(2)}, u32[]{:S(2)}) %collective-permute-start.67) | collective-permute-done | bytes 393248 | tf_op jit(solution)/shard_map/ppermute | solution.py:29
  688.1 5.2 collective-permute-done.68
  701.9 4.5 fusion.8
  708.5 5.4 convolution_convert_fusion.7
  723.6 8.8 %collective-permute-done.71 = bf16[256,1024]{1,0:T(8,128)(2,1)S(1)} collective-permute-done((bf16[256,1024]{1,0:T(8,128)(2,1)S(1)}, bf16[256,1024]{1,0:T(8,128)(2,1)S(1)}, u32[]{:S(2)}, u32[]{:S(2)}) %collective-permute-start.71) | collective-permute-done | bytes 524320 | tf_op jit(solution)/shard_map/ppermute | solution.py:29
  732.4 27.4 %collective-permute-done.69 = bf16[256,1536]{1,0:T(8,128)(2,1)S(1)} collective-permute-done((bf16[256,1536]{1,0:T(8,128)(2,1)S(1)}, bf16[256,1536]{1,0:T(8,128)(2,1)S(1)}, u32[]{:S(2)}, u32[]{:S(2)}) %collective-permute-start.69) | collective-permute-done | bytes 786464 | tf_op jit(solution)/shard_map/ppermute | solution.py:29
  783.2 5.8 convolution_convert_fusion.8
  789.0 4.2 unpack_units.1
  (595 shorter events, 258.7 us)
Async XLA Ops:
  30.4 25.6 %collective-permute-start.6 = (bf16[272,2048]{1,0:T(8,128)(2,1)S(1)}, bf16[272,2048]{1,0:T(8,128)(2,1)S(1)}, u32[]{:S(2)}, u32[]{:S(2)}) collective-permute-start(bf16[272,2048]{1,0:T(8,128)(2,1)S(1)} %fusion.26.refs_0_), channel_id=1, source_target_pairs={{0,16},{8,24},{16,0},{24,8},{1,17},{9,25},{17,1},{25,9},{2,18},{10... | collective-permute-start | bytes 3342344 | tf_op jit(solution)/shard_map/ppermute | solution.py:29
  31.9 25.3 %collective-permute-start.5 = (bf16[272,2048]{1,0:T(8,128)(2,1)S(1)}, bf16[272,2048]{1,0:T(8,128)(2,1)S(1)}, u32[]{:S(2)}, u32[]{:S(2)}) collective-permute-start(bf16[272,2048]{1,0:T(8,128)(2,1)S(1)} %fusion.26.refs_0_), channel_id=1, source_target_pairs={{0,8},{8,0},{16,24},{24,16},{1,9},{9,1},{17,25},{25,17},{2,10},{10... | collective-permute-start | bytes 3342344 | tf_op jit(solution)/shard_map/ppermute | solution.py:29
  32.6 45.9 %collective-permute-start.3 = (bf16[256,2048]{1,0:T(8,128)(2,1)S(1)}, bf16[256,2048]{1,0:T(8,128)(2,1)S(1)}, u32[]{:S(2)}, u32[]{:S(2)}) collective-permute-start(bf16[256,2048]{1,0:T(8,128)(2,1)S(1)} %maximum_maximum_fusion), channel_id=1, source_target_pairs={{0,2},{2,0},{1,3},{3,1},{4,6},{6,4},{5,7},{7,5},{8,10},{10,8},{9,1... | collective-permute-start | bytes 3145736 | tf_op jit(solution)/shard_map/ppermute | solution.py:29
  33.1 45.4 %collective-permute-start.4 = (bf16[256,2048]{1,0:T(8,128)(2,1)S(1)}, bf16[256,2048]{1,0:T(8,128)(2,1)S(1)}, u32[]{:S(2)}, u32[]{:S(2)}) collective-permute-start(bf16[256,2048]{1,0:T(8,128)(2,1)S(1)} %maximum_maximum_fusion), channel_id=1, source_target_pairs={{0,4},{4,0},{1,5},{5,1},{2,6},{6,2},{3,7},{7,3},{8,12},{12,8},{9,1... | collective-permute-start | bytes 3145736 | tf_op jit(solution)/shard_map/ppermute | solution.py:29
  60.3 47.4 %collective-permute-start.11 = (bf16[256,2048]{1,0:T(8,128)(2,1)S(1)}, bf16[256,2048]{1,0:T(8,128)(2,1)S(1)}, u32[]{:S(2)}, u32[]{:S(2)}) collective-permute-start(bf16[256,2048]{1,0:T(8,128)(2,1)S(1)} %maximum_maximum_fusion), channel_id=1, source_target_pairs={{0,1},{1,0},{2,3},{3,2},{4,5},{5,4},{6,7},{7,6},{8,9},{9,8},{10,11... | collective-permute-start | bytes 3145736 | tf_op jit(solution)/shard_map/ppermute | solution.py:29
  78.5 29.2 %collective-permute-start.12 = (bf16[256,2048]{1,0:T(8,128)(2,1)S(1)}, bf16[256,2048]{1,0:T(8,128)(2,1)S(1)}, u32[]{:S(2)}, u32[]{:S(2)}) collective-permute-start(bf16[256,2048]{1,0:T(8,128)(2,1)S(1)} %collective-permute-done.3), channel_id=1, source_target_pairs={{0,1},{1,0},{2,3},{3,2},{4,5},{5,4},{6,7},{7,6},{8,9},{9,8},{10,11... | collective-permute-start | bytes 3145736 | tf_op jit(solution)/shard_map/ppermute | solution.py:29
  78.6 30.4 %collective-permute-start.13 = (bf16[256,2048]{1,0:T(8,128)(2,1)S(1)}, bf16[256,2048]{1,0:T(8,128)(2,1)}, u32[]{:S(2)}, u32[]{:S(2)}) collective-permute-start(bf16[256,2048]{1,0:T(8,128)(2,1)S(1)} %collective-permute-done.4), channel_id=1, source_target_pairs={{0,1},{1,0},{2,3},{3,2},{4,5},{5,4},{6,7},{7,6},{8,9},{9,8},{10,11... | collective-permute-start | bytes 3145736 | tf_op jit(solution)/shard_map/ppermute | solution.py:29
  79.1 25.6 %collective-permute-start.9 = (bf16[256,1024]{1,0:T(8,128)(2,1)S(1)}, bf16[256,1024]{1,0:T(8,128)(2,1)S(1)}, u32[]{:S(2)}, u32[]{:S(2)}) collective-permute-start(bf16[256,1024]{1,0:T(8,128)(2,1)S(1)} %slice.403), channel_id=1, source_target_pairs={{0,2},{2,0},{1,3},{3,1},{4,6},{6,4},{5,7},{7,5},{8,10},{10,8},{9,1... | collective-permute-start | bytes 1572872 | tf_op jit(solution)/shard_map/ppermute | solution.py:29
  81.8 25.8 %collective-permute-start.10 = (bf16[256,1024]{1,0:T(8,128)(2,1)S(1)}, bf16[256,1024]{1,0:T(8,128)(2,1)S(1)}, u32[]{:S(2)}, u32[]{:S(2)}) collective-permute-start(bf16[256,1024]{1,0:T(8,128)(2,1)S(1)} %slice.404), channel_id=1, source_target_pairs={{0,4},{4,0},{1,5},{5,1},{2,6},{6,2},{3,7},{7,3},{8,12},{12,8},{9,1... | collective-permute-start | bytes 1572872 | tf_op jit(solution)/shard_map/ppermute | solution.py:29
  109.0 28.9 %all-to-all-start.1 = ((bf16[8,64,2048]{2,1,0:T(8,128)(2,1)}), bf16[8,64,2048]{2,1,0:T(8,128)(2,1)}, u32[]{:S(2)}, u32[]{:S(2)}) async-start(bf16[8,64,2048]{2,1,0:T(8,128)(2,1)} %pack_units.1), calls=%async_computation.1 | async-start | bytes 4194304 | tf_op jit(solution)/shard_map/all_to_all | solution.py:1058
  113.4 129.7 %all-gather.3.cloned.1.call-start = ((), (), s32[]{:S(2)}) async-start(), calls=%async_computation.7 | async-start | bytes 10485760 | tf_op jit(solution)/shard_map/all_gather | solution.py:1081
  138.0 185.6 %all-gather.5.cloned.1.call-start = ((), (), s32[]{:S(2)}) async-start(), calls=%async_computation.8 | async-start | bytes 5242880 | tf_op jit(solution)/shard_map/all_gather | solution.py:1118
  175.7 23.7 %collective-permute-start.18 = (bf16[256,2048]{1,0:T(8,128)(2,1)S(1)}, bf16[256,2048]{1,0:T(8,128)(2,1)}, u32[]{:S(2)}, u32[]{:S(2)}) collective-permute-start(bf16[256,2048]{1,0:T(8,128)(2,1)S(1)} %pad_maximum_fusion.2), channel_id=1, source_target_pairs={{0,8},{8,0},{16,24},{24,16},{1,9},{9,1},{17,25},{25,17},{2,10},{10... | collective-permute-start | bytes 3145736 | tf_op jit(solution)/shard_map/ppermute | solution.py:29
  203.5 21.8 %collective-permute-start.23 = (bf16[256,2048]{1,0:T(8,128)(2,1)S(1)}, bf16[256,2048]{1,0:T(8,128)(2,1)S(1)}, u32[]{:S(2)}, u32[]{:S(2)}) collective-permute-start(bf16[256,2048]{1,0:T(8,128)(2,1)S(1)} %fusion.23.refs_0_), channel_id=1, source_target_pairs={{0,16},{8,24},{16,0},{24,8},{1,17},{9,25},{17,1},{25,9},{2,18},{10... | collective-permute-start | bytes 3145736 | tf_op jit(solution)/shard_map/ppermute | solution.py:29
  205.3 22.4 %collective-permute-start.22 = (bf16[256,2048]{1,0:T(8,128)(2,1)S(1)}, bf16[256,2048]{1,0:T(8,128)(2,1)S(1)}, u32[]{:S(2)}, u32[]{:S(2)}) collective-permute-start(bf16[256,2048]{1,0:T(8,128)(2,1)S(1)} %fusion.23.refs_0_), channel_id=1, source_target_pairs={{0,8},{8,0},{16,24},{24,16},{1,9},{9,1},{17,25},{25,17},{2,10},{10... | collective-permute-start | bytes 3145736 | tf_op jit(solution)/shard_map/ppermute | solution.py:29
  230.0 34.0 %collective-permute-start.21 = (bf16[256,2048]{1,0:T(8,128)(2,1)S(1)}, bf16[256,2048]{1,0:T(8,128)(2,1)}, u32[]{:S(2)}, u32[]{:S(2)}) collective-permute-start(bf16[256,2048]{1,0:T(8,128)(2,1)S(1)} %fusion.23.refs_0_), channel_id=1, source_target_pairs={{0,2},{2,0},{1,3},{3,1},{4,6},{6,4},{5,7},{7,5},{8,10},{10,8},{9,1... | collective-permute-start | bytes 3145736 | tf_op jit(solution)/shard_map/ppermute | solution.py:29
  264.0 336.8 %reduce-scatter.3.cloned.1.call-start = ((), (), s32[]{:S(2)}) async-start(), calls=%async_computation.9 | async-start | bytes 5242880 | tf_op jit(solution)/shard_map/reduce_scatter | solution.py:1147
  264.4 25.6 %collective-permute-start.26 = (bf16[256,2048]{1,0:T(8,128)(2,1)}, bf16[256,2048]{1,0:T(8,128)(2,1)S(1)}, u32[]{:S(2)}, u32[]{:S(2)}) collective-permute-start(bf16[256,2048]{1,0:T(8,128)(2,1)} %collective-permute-done.21.refs_0_), channel_id=1, source_target_pairs={{0,8},{8,0},{16,24},{24,16},{1,9},{9,1},{17,25},{25,17},{2,10},{10... | collective-permute-start | bytes 3145736 | tf_op jit(solution)/shard_map/ppermute | solution.py:29
  266.0 25.3 %collective-permute-start.27 = (bf16[256,2048]{1,0:T(8,128)(2,1)}, bf16[256,2048]{1,0:T(8,128)(2,1)S(1)}, u32[]{:S(2)}, u32[]{:S(2)}) collective-permute-start(bf16[256,2048]{1,0:T(8,128)(2,1)} %collective-permute-done.21.refs_0_), channel_id=1, source_target_pairs={{0,16},{8,24},{16,0},{24,8},{1,17},{9,25},{17,1},{25,9},{2,18},{10... | collective-permute-start | bytes 3145736 | tf_op jit(solution)/shard_map/ppermute | solution.py:29
  345.1 24.2 %collective-permute-start.34 = (bf16[256,2048]{1,0:T(8,128)(2,1)S(1)}, bf16[256,2048]{1,0:T(8,128)(2,1)S(1)}, u32[]{:S(2)}, u32[]{:S(2)}) collective-permute-start(bf16[256,2048]{1,0:T(8,128)(2,1)S(1)} %pad_maximum_fusion.7), channel_id=1, source_target_pairs={{0,8},{8,0},{16,24},{24,16},{1,9},{9,1},{17,25},{25,17},{2,10},{10... | collective-permute-start | bytes 3145736 | tf_op jit(solution)/shard_map/ppermute | solution.py:29
  346.8 24.1 %collective-permute-start.37 = (bf16[256,2048]{1,0:T(8,128)(2,1)S(1)}, bf16[256,2048]{1,0:T(8,128)(2,1)S(1)}, u32[]{:S(2)}, u32[]{:S(2)}) collective-permute-start(bf16[256,2048]{1,0:T(8,128)(2,1)S(1)} %pad_maximum_fusion.8), channel_id=1, source_target_pairs={{0,16},{8,24},{16,0},{24,8},{1,17},{9,25},{17,1},{25,9},{2,18},{10... | collective-permute-start | bytes 3145736 | tf_op jit(solution)/shard_map/ppermute | solution.py:29
  347.8 24.1 %collective-permute-start.31 = (bf16[256,2048]{1,0:T(8,128)(2,1)S(1)}, bf16[256,2048]{1,0:T(8,128)(2,1)S(1)}, u32[]{:S(2)}, u32[]{:S(2)}) collective-permute-start(bf16[256,2048]{1,0:T(8,128)(2,1)S(1)} %pad_maximum_fusion.6), channel_id=1, source_target_pairs={{0,2},{2,0},{1,3},{3,1},{4,6},{6,4},{5,7},{7,5},{8,10},{10,8},{9,1... | collective-permute-start | bytes 3145736 | tf_op jit(solution)/shard_map/ppermute | solution.py:29
  369.7 23.5 %collective-permute-start.35 = (bf16[256,2048]{1,0:T(8,128)(2,1)S(1)}, bf16[256,2048]{1,0:T(8,128)(2,1)S(1)}, u32[]{:S(2)}, u32[]{:S(2)}) collective-permute-start(bf16[256,2048]{1,0:T(8,128)(2,1)S(1)} %add_convert_fusion.5), channel_id=1, source_target_pairs={{0,16},{8,24},{16,0},{24,8},{1,17},{9,25},{17,1},{25,9},{2,18},{10... | collective-permute-start | bytes 3145736 | tf_op jit(solution)/shard_map/ppermute | solution.py:29
  371.4 22.9 %collective-permute-start.38 = (bf16[256,2048]{1,0:T(8,128)(2,1)S(1)}, bf16[256,2048]{1,0:T(8,128)(2,1)S(1)}, u32[]{:S(2)}, u32[]{:S(2)}) collective-permute-start(bf16[256,2048]{1,0:T(8,128)(2,1)S(1)} %add_convert_fusion.4), channel_id=1, source_target_pairs={{0,2},{2,0},{1,3},{3,1},{4,6},{6,4},{5,7},{7,5},{8,10},{10,8},{9,1... | collective-permute-start | bytes 3145736 | tf_op jit(solution)/shard_map/ppermute | solution.py:29
  372.3 23.1 %collective-permute-start.32 = (bf16[256,2048]{1,0:T(8,128)(2,1)S(1)}, bf16[256,2048]{1,0:T(8,128)(2,1)S(1)}, u32[]{:S(2)}, u32[]{:S(2)}) collective-permute-start(bf16[256,2048]{1,0:T(8,128)(2,1)S(1)} %add_convert_fusion.6), channel_id=1, source_target_pairs={{0,8},{8,0},{16,24},{24,16},{1,9},{9,1},{17,25},{25,17},{2,10},{10... | collective-permute-start | bytes 3145736 | tf_op jit(solution)/shard_map/ppermute | solution.py:29
  398.4 22.2 %collective-permute-start.40 = (bf16[256,2048]{1,0:T(8,128)(2,1)S(1)}, bf16[256,2048]{1,0:T(8,128)(2,1)S(1)}, u32[]{:S(2)}, u32[]{:S(2)}) collective-permute-start(bf16[256,2048]{1,0:T(8,128)(2,1)S(1)} %fusion.17.refs_0_), channel_id=1, source_target_pairs={{0,16},{8,24},{16,0},{24,8},{1,17},{9,25},{17,1},{25,9},{2,18},{10... | collective-permute-start | bytes 3145736 | tf_op jit(solution)/shard_map/ppermute | solution.py:29
  399.5 23.6 %collective-permute-start.39 = (bf16[256,2048]{1,0:T(8,128)(2,1)S(1)}, bf16[256,2048]{1,0:T(8,128)(2,1)S(1)}, u32[]{:S(2)}, u32[]{:S(2)}) collective-permute-start(bf16[256,2048]{1,0:T(8,128)(2,1)S(1)} %fusion.17.refs_0_), channel_id=1, source_target_pairs={{0,8},{8,0},{16,24},{24,16},{1,9},{9,1},{17,25},{25,17},{2,10},{10... | collective-permute-start | bytes 3145736 | tf_op jit(solution)/shard_map/ppermute | solution.py:29
  401.0 23.9 %collective-permute-start.41 = (bf16[256,2048]{1,0:T(8,128)(2,1)S(1)}, bf16[256,2048]{1,0:T(8,128)(2,1)S(1)}, u32[]{:S(2)}, u32[]{:S(2)}) collective-permute-start(bf16[256,2048]{1,0:T(8,128)(2,1)S(1)} %fusion.17.refs_0_), channel_id=1, source_target_pairs={{0,2},{2,0},{1,3},{3,1},{4,6},{6,4},{5,7},{7,5},{8,10},{10,8},{9,1... | collective-permute-start | bytes 3145736 | tf_op jit(solution)/shard_map/ppermute | solution.py:29
  420.6 28.9 %collective-permute-start.42 = (bf16[256,2048]{1,0:T(8,128)(2,1)S(1)}, bf16[256,2048]{1,0:T(8,128)(2,1)S(1)}, u32[]{:S(2)}, u32[]{:S(2)}) collective-permute-start(bf16[256,2048]{1,0:T(8,128)(2,1)S(1)} %collective-permute-done.40.refs_2_), channel_id=1, source_target_pairs={{0,8},{8,0},{16,24},{24,16},{1,9},{9,1},{17,25},{25,17},{2,10},{10... | collective-permute-start | bytes 3145736 | tf_op jit(solution)/shard_map/ppermute | solution.py:29
  423.1 23.7 %collective-permute-start.43 = (bf16[256,2048]{1,0:T(8,128)(2,1)S(1)}, bf16[256,2048]{1,0:T(8,128)(2,1)S(1)}, u32[]{:S(2)}, u32[]{:S(2)}) collective-permute-start(bf16[256,2048]{1,0:T(8,128)(2,1)S(1)} %collective-permute-done.39.refs_1_), channel_id=1, source_target_pairs={{0,2},{2,0},{1,3},{3,1},{4,6},{6,4},{5,7},{7,5},{8,10},{10,8},{9,1... | collective-permute-start | bytes 3145736 | tf_op jit(solution)/shard_map/ppermute | solution.py:29
  424.9 23.1 %collective-permute-start.44 = (bf16[256,2048]{1,0:T(8,128)(2,1)S(1)}, bf16[256,2048]{1,0:T(8,128)(2,1)S(1)}, u32[]{:S(2)}, u32[]{:S(2)}) collective-permute-start(bf16[256,2048]{1,0:T(8,128)(2,1)S(1)} %collective-permute-done.41.refs_3_), channel_id=1, source_target_pairs={{0,16},{8,24},{16,0},{24,8},{1,17},{9,25},{17,1},{25,9},{2,18},{10... | collective-permute-start | bytes 3145736 | tf_op jit(solution)/shard_map/ppermute | solution.py:29
  446.9 20.5 %collective-permute-start.46 = (bf16[256,768]{1,0:T(8,128)(2,1)S(1)}, bf16[256,768]{1,0:T(8,128)(2,1)S(1)}, u32[]{:S(2)}, u32[]{:S(2)}) collective-permute-start(bf16[256,768]{1,0:T(8,128)(2,1)S(1)} %slice.537), channel_id=1, source_target_pairs={{0,16},{8,24},{16,0},{24,8},{1,17},{9,25},{17,1},{25,9},{2,18},{10... | collective-permute-start | bytes 1179656 | tf_op jit(solution)/shard_map/ppermute | solution.py:29
  492.0 203.4 %reduce-scatter.5.cloned.1.call-start = ((), (), s32[]{:S(2)}) async-start(), calls=%async_computation.10 | async-start | bytes 10485760 | tf_op jit(solution)/shard_map/reduce_scatter | solution.py:1147
  496.4 26.7 %collective-permute-start.52 = (bf16[256,2048]{1,0:T(8,128)(2,1)S(1)}, bf16[256,2048]{1,0:T(8,128)(2,1)S(1)}, u32[]{:S(2)}, u32[]{:S(2)}) collective-permute-start(bf16[256,2048]{1,0:T(8,128)(2,1)S(1)} %pad_maximum_fusion.11), channel_id=1, source_target_pairs={{0,2},{2,0},{1,3},{3,1},{4,6},{6,4},{5,7},{7,5},{8,10},{10,8},{9,1... | collective-permute-start | bytes 3145736 | tf_op jit(solution)/shard_map/ppermute | solution.py:29
  498.9 24.3 %collective-permute-start.51 = (bf16[256,2048]{1,0:T(8,128)(2,1)S(1)}, bf16[256,2048]{1,0:T(8,128)(2,1)S(1)}, u32[]{:S(2)}, u32[]{:S(2)}) collective-permute-start(bf16[256,2048]{1,0:T(8,128)(2,1)S(1)} %pad_maximum_fusion.10), channel_id=1, source_target_pairs={{0,8},{8,0},{16,24},{24,16},{1,9},{9,1},{17,25},{25,17},{2,10},{10... | collective-permute-start | bytes 3145736 | tf_op jit(solution)/shard_map/ppermute | solution.py:29
  523.5 34.7 %collective-permute-start.56 = (bf16[256,2048]{1,0:T(8,128)(2,1)S(1)}, bf16[256,2048]{1,0:T(8,128)(2,1)S(1)}, u32[]{:S(2)}, u32[]{:S(2)}) collective-permute-start(bf16[256,2048]{1,0:T(8,128)(2,1)S(1)} %add_convert_fusion), channel_id=1, source_target_pairs={{0,2},{2,0},{1,3},{3,1},{4,6},{6,4},{5,7},{7,5},{8,10},{10,8},{9,1... | collective-permute-start | bytes 3145736 | tf_op jit(solution)/shard_map/ppermute | solution.py:29
  525.9 32.4 %collective-permute-start.55 = (bf16[256,2048]{1,0:T(8,128)(2,1)S(1)}, bf16[256,2048]{1,0:T(8,128)(2,1)S(1)}, u32[]{:S(2)}, u32[]{:S(2)}) collective-permute-start(bf16[256,2048]{1,0:T(8,128)(2,1)S(1)} %add_convert_fusion.1), channel_id=1, source_target_pairs={{0,16},{8,24},{16,0},{24,8},{1,17},{9,25},{17,1},{25,9},{2,18},{10... | collective-permute-start | bytes 3145736 | tf_op jit(solution)/shard_map/ppermute | solution.py:29
  527.4 30.9 %collective-permute-start.54 = (bf16[256,2048]{1,0:T(8,128)(2,1)S(1)}, bf16[256,2048]{1,0:T(8,128)(2,1)S(1)}, u32[]{:S(2)}, u32[]{:S(2)}) collective-permute-start(bf16[256,2048]{1,0:T(8,128)(2,1)S(1)} %add_convert_fusion.2), channel_id=1, source_target_pairs={{0,8},{8,0},{16,24},{24,16},{1,9},{9,1},{17,25},{25,17},{2,10},{10... | collective-permute-start | bytes 3145736 | tf_op jit(solution)/shard_map/ppermute | solution.py:29
  568.1 22.2 %collective-permute-start.58 = (bf16[256,2048]{1,0:T(8,128)(2,1)S(1)}, bf16[256,2048]{1,0:T(8,128)(2,1)S(1)}, u32[]{:S(2)}, u32[]{:S(2)}) collective-permute-start(bf16[256,2048]{1,0:T(8,128)(2,1)S(1)} %get-tuple-element.295), channel_id=1, source_target_pairs={{0,16},{8,24},{16,0},{24,8},{1,17},{9,25},{17,1},{25,9},{2,18},{10... | collective-permute-start | bytes 3145736 | tf_op jit(solution)/shard_map/ppermute | solution.py:29
  569.4 22.0 %collective-permute-start.57 = (bf16[256,2048]{1,0:T(8,128)(2,1)S(1)}, bf16[256,2048]{1,0:T(8,128)(2,1)S(1)}, u32[]{:S(2)}, u32[]{:S(2)}) collective-permute-start(bf16[256,2048]{1,0:T(8,128)(2,1)S(1)} %get-tuple-element.295), channel_id=1, source_target_pairs={{0,8},{8,0},{16,24},{24,16},{1,9},{9,1},{17,25},{25,17},{2,10},{10... | collective-permute-start | bytes 3145736 | tf_op jit(solution)/shard_map/ppermute | solution.py:29
  667.9 20.2 %collective-permute-start.67 = (bf16[256,768]{1,0:T(8,128)(2,1)S(1)}, bf16[256,768]{1,0:T(8,128)(2,1)S(1)}, u32[]{:S(2)}, u32[]{:S(2)}) collective-permute-start(bf16[256,768]{1,0:T(8,128)(2,1)S(1)} %get-tuple-element.373), channel_id=1, source_target_pairs={{0,2},{2,0},{1,3},{3,1},{4,6},{6,4},{5,7},{7,5},{8,10},{10,8},{9,1... | collective-permute-start | bytes 1179656 | tf_op jit(solution)/shard_map/ppermute | solution.py:29
  670.9 22.4 %collective-permute-start.68 = (bf16[256,768]{1,0:T(8,128)(2,1)S(1)}, bf16[256,768]{1,0:T(8,128)(2,1)S(1)}, u32[]{:S(2)}, u32[]{:S(2)}) collective-permute-start(bf16[256,768]{1,0:T(8,128)(2,1)S(1)} %get-tuple-element.372), channel_id=1, source_target_pairs={{0,4},{4,0},{1,5},{5,1},{2,6},{6,2},{3,7},{7,3},{8,12},{12,8},{9,1... | collective-permute-start | bytes 1179656 | tf_op jit(solution)/shard_map/ppermute | solution.py:29
  695.4 65.3 %all-to-all-start.2 = ((bf16[8,64,2048]{2,1,0:T(8,128)(2,1)}), bf16[8,64,2048]{2,1,0:T(8,128)(2,1)S(1)}, u32[]{:S(2)}, u32[]{:S(2)}) async-start(bf16[8,64,2048]{2,1,0:T(8,128)(2,1)} %reduce-scatter.5.cloned.1.call-done), calls=%async_computation.4 | async-start | bytes 4194304 | tf_op jit(solution)/shard_map/all_to_all | solution.py:1208
  717.6 42.2 %collective-permute-start.69 = (bf16[256,1536]{1,0:T(8,128)(2,1)S(1)}, bf16[256,1536]{1,0:T(8,128)(2,1)S(1)}, u32[]{:S(2)}, u32[]{:S(2)}) collective-permute-start(bf16[256,1536]{1,0:T(8,128)(2,1)S(1)} %copy-done.83), channel_id=1, source_target_pairs={{0,2},{2,0},{1,3},{3,1},{4,6},{6,4},{5,7},{7,5},{8,10},{10,8},{9,1... | collective-permute-start | bytes 2359304 | tf_op jit(solution)/shard_map/ppermute | solution.py:29
  719.1 41.7 %collective-permute-start.70 = (bf16[256,1536]{1,0:T(8,128)(2,1)S(1)}, bf16[256,1536]{1,0:T(8,128)(2,1)}, u32[]{:S(2)}, u32[]{:S(2)}) collective-permute-start(bf16[256,1536]{1,0:T(8,128)(2,1)S(1)} %copy-done.82), channel_id=1, source_target_pairs={{0,4},{4,0},{1,5},{5,1},{2,6},{6,2},{3,7},{7,3},{8,12},{12,8},{9,1... | collective-permute-start | bytes 2359304 | tf_op jit(solution)/shard_map/ppermute | solution.py:29
  764.1 29.3 %all-to-all-start.3 = ((bf16[4,64,1536]{2,1,0:T(8,128)(2,1)}), bf16[4,64,1536]{2,1,0:T(8,128)(2,1)S(1)}, u32[]{:S(2)}, u32[]{:S(2)}) async-start(bf16[4,64,1536]{2,1,0:T(8,128)(2,1)} %bitcast.184), calls=%async_computation.5 | async-start | bytes 1572864 | tf_op jit(solution)/shard_map/all_to_all | solution.py:1215
  774.8 31.1 %collective-permute-start.77 = (bf16[256,2048]{1,0:T(8,128)(2,1)}, bf16[256,2048]{1,0:T(8,128)(2,1)}, u32[]{:S(2)}, u32[]{:S(2)}) collective-permute-start(bf16[256,2048]{1,0:T(8,128)(2,1)} %pad_maximum_fusion.15), channel_id=1, source_target_pairs={{0,8},{8,0},{16,24},{24,16},{1,9},{9,1},{17,25},{25,17},{2,10},{10... | collective-permute-start | bytes 3145736 | tf_op jit(solution)/shard_map/ppermute | solution.py:29
  778.2 27.8 %collective-permute-start.78 = (bf16[256,2048]{1,0:T(8,128)(2,1)}, bf16[256,2048]{1,0:T(8,128)(2,1)}, u32[]{:S(2)}, u32[]{:S(2)}) collective-permute-start(bf16[256,2048]{1,0:T(8,128)(2,1)} %pad_maximum_fusion.16), channel_id=1, source_target_pairs={{0,16},{8,24},{16,0},{24,8},{1,17},{9,25},{17,1},{25,9},{2,18},{10... | collective-permute-start | bytes 3145736 | tf_op jit(solution)/shard_map/ppermute | solution.py:29
  (167 other events, 1669.6 us)
Sparse Core Ops, SparseCore 0:
  138.1 104.9 all-gather.2
  264.1 59.4 all-gather.4
  492.1 66.5 reduce-scatter.2
  561.3 118.7 reduce-scatter.4
